TPU v7x, 256 devices: a whole 4x4x8 slice. The times are simulated.
256 devices in a mesh: dp: 256 (over z, x, y, core).
Axes of the slice: x: 4, y: 4, z: 8, core: 2. Of those that a mesh axis runs over, the one named last changes fastest.
Arguments:
- audio: bfloat16 [65536, 1024], P('dp'), may hold values from -64 to 64, as said below
- text: bfloat16 [65536, 1024], P('dp'), may hold values from -64 to 64, as said below
- log_scale: float32 [1], replicated, may hold values from 3.7 to 4.4
- bias: float32 [1], replicated, may hold values from -4 to -2
- plan: int32 [256, 3], P('dp'), may hold values from 0 to 255, as said below
Outputs:
- row_loss: float32 [65536], P('dp')
- grad_audio: float32 [65536, 1024], P('dp')
- grad_text: float32 [65536, 1024], P('dp')
- stats: float32 [3], replicated
Inputs may be any that keep to these rules, and one draw needn't show every extreme that they name: `plan`: the partner of player g in round r is (g + s_r) mod 256, where s_r lies in 1 .. 255, is the same for every player, and differs between rounds. Rows of audio have differing norms; every row is nonzero. Rows of text have differing norms; every row is nonzero.
All inputs are finite; a program needn't handle non-finite values.
Results may differ from a plain program's by a relative error of at most 0.0022.
Values may be sent and summed in bfloat16 or wider, within the bound.
A program may use at most 320 MiB of HBM per device.

v0:
```python
from functools import partial

import jax
import jax.numpy as jnp
from jax import lax
from jax.sharding import PartitionSpec as P

EPSILON = 1e-06


def as_sent(shard):
    return jax.tree.map(lambda a: a.astype(jnp.bfloat16) if a.dtype == jnp.float32 else a, shard)


def passed_along(shard, axis, by):
    peers = lax.axis_size(axis)
    return lax.ppermute(shard, axis, [(i, (i + by) % peers) for i in range(peers)])


def unit_rows(raw_rows):
    widened = raw_rows.astype(jnp.float32)
    reciprocal = lax.rsqrt(jnp.sum(widened * widened, axis=-1, keepdims=True) + EPSILON)
    return (widened * reciprocal, reciprocal)


def block_logits(left_rows, right_rows, logit_scale, logit_bias, positive):
    cosine = jnp.dot(left_rows, right_rows.T, preferred_element_type=jnp.float32)
    logits = logit_scale * cosine + logit_bias
    diagonal = positive * jnp.eye(left_rows.shape[0], dtype=jnp.float32)
    labels = 2.0 * diagonal - 1.0
    losses = -jax.nn.log_sigmoid(labels * logits)
    slopes = jax.nn.sigmoid(logits) - diagonal
    weights = (logit_scale * slopes).astype(jnp.bfloat16)
    block_sums = jnp.stack(
        [jnp.sum(losses), jnp.sum(slopes), jnp.sum(slopes * (logits - logit_bias))]
    )
    return (jnp.sum(losses, axis=1), weights, block_sums)


def send_text(value, distance):
    return jax.tree.map(
        lambda part, own: part.astype(own.dtype),
        passed_along(as_sent(value), "dp", distance),
        value,
    )


def send_grad(value, distance):
    return jax.tree.map(
        lambda part, own: part.astype(own.dtype),
        passed_along(as_sent(value), "dp", distance),
        value,
    )


def keep_value(value):
    return value


def moved_value(sender, distance, value):
    return sender(value, distance)


def route_blocks(value, offset, player_count, sender):
    branches = [keep_value] + [
        partial(moved_value, sender, player_count - step) for step in range(1, player_count)
    ]
    return lax.switch(offset, branches, value)


def local(audio, text, log_scale, bias, plan):
    audio_wide, audio_recip = unit_rows(audio)
    text_wide, text_recip = unit_rows(text)
    audio_unit = audio_wide.astype(jnp.bfloat16)
    text_unit = text_wide.astype(jnp.bfloat16)
    logit_scale = jnp.exp(log_scale[0])
    logit_bias = bias[0]
    row_count = audio.shape[0]
    row_sums, weights, totals = block_logits(audio_unit, text_unit, logit_scale, logit_bias, 1.0)
    audio_grad = jnp.dot(weights, text_unit, preferred_element_type=jnp.float32)
    text_grad = jnp.dot(weights.T, audio_unit, preferred_element_type=jnp.float32)
    player_count = lax.axis_size("dp")
    player = lax.axis_index("dp")
    round_count = plan.shape[1]
    for round_index in range(round_count):
        offset = jnp.remainder(plan[0, round_index] - player, player_count)
        back_offset = jnp.remainder(player_count - offset, player_count)
        far_text = route_blocks(text_unit, offset, player_count, send_text)
        part_sums, weights, block_sums = block_logits(
            audio_unit, far_text, logit_scale, logit_bias, 0.0
        )
        audio_grad = audio_grad + jnp.dot(weights, far_text, preferred_element_type=jnp.float32)
        partial_grad = jnp.dot(weights.T, audio_unit, preferred_element_type=jnp.float32).astype(
            jnp.bfloat16
        )
        returned = route_blocks(partial_grad, back_offset, player_count, send_grad)
        text_grad = text_grad + returned.astype(jnp.float32)
        row_sums = row_sums + part_sums
        totals = totals + block_sums
    totals = lax.psum(totals, "dp")
    stats = totals / float((round_count + 1) * row_count * row_count * player_count)
    grad_audio = audio_recip * (
        audio_grad - audio_wide * jnp.sum(audio_wide * audio_grad, axis=-1, keepdims=True)
    )
    grad_text = text_recip * (
        text_grad - text_wide * jnp.sum(text_wide * text_grad, axis=-1, keepdims=True)
    )
    return (row_sums, grad_audio, grad_text, stats)


def solution(mesh):
    return jax.shard_map(
        local,
        mesh=mesh,
        in_specs=(P("dp", None), P("dp", None), P(), P(), P("dp", None)),
        out_specs=(P("dp"), P("dp", None), P("dp", None), P()),
        check_vma=False,
    )
```

profile of v0, /device:TPU:1, one launch (start us, length us, event | category | flops | bytes accessed | tf_op | source)
XLA Modules:
  0.0 610.1 jit_solution(3616369879239270185)
XLA Ops:
  1.3 1.4 fusion.43
  3.4 0.0 copy-start.1
  3.4 1.3 fusion.19
  4.7 0.0 copy-done
  4.7 0.2 fusion.15
  4.9 0.2 fusion.4
  5.0 0.4 copy-done.7
  5.5 101.9 %conditional.8 = (bf16[256,1024]{1,0:T(8,128)(2,1)}) conditional(s32[]{:T(128)} %clamp.20, bf16[256,1024]{1,0:T(8,128)(2,1)S(1)} %fusion.4, bf16[256,1024]{1,0:T(8,128)(2,1)S(1)} %fusion.4, bf16[256,1024]{1,0:T(8,128)(2,1)S(1)} %fusion.4, bf16[256,1024]{1,0:T(8,128)(2,1)S(1)} %fusion.4, ...), branch_computations={%region_517.518_spmd, %region_518.519_spmd, %region_519.520_spmd, ... | conditional | bytes 2097200 | solution.py:68
  28.3 13.9 %collective-permute-start.675 = (bf16[256,1024]{1,0:T(8,128)(2,1)S(1)}, bf16[256,1024]{1,0:T(8,128)(2,1)}, u32[]{:S(2)}, u32[]{:S(2)}) collective-permute-start(bf16[256,1024]{1,0:T(8,128)(2,1)S(1)} %param.678), channel_id=1, source_target_pairs={{0,90},{1,91},{2,92},{3,93},{4,94},{5,95},{6,96},{7,97},{8,98},{9,... | collective-permute-start | bytes 1572872 | tf_op jit(solution)/shard_map/cond/branch_166_fun/ppermute | solution.py:17
  42.2 42.0 %collective-permute-done.675 = bf16[256,1024]{1,0:T(8,128)(2,1)} collective-permute-done((bf16[256,1024]{1,0:T(8,128)(2,1)S(1)}, bf16[256,1024]{1,0:T(8,128)(2,1)}, u32[]{:S(2)}, u32[]{:S(2)}) %collective-permute-start.675) | collective-permute-done | bytes 524320 | tf_op jit(solution)/shard_map/cond/branch_166_fun/ppermute | solution.py:17
  108.1 2.3 fusion.24
  111.0 62.7 %conditional.7 = (bf16[256,1024]{1,0:T(8,128)(2,1)}) conditional(s32[]{:T(128)} %clamp.19, bf16[256,1024]{1,0:T(8,128)(2,1)S(1)} %fusion.4, bf16[256,1024]{1,0:T(8,128)(2,1)S(1)} %fusion.4, bf16[256,1024]{1,0:T(8,128)(2,1)S(1)} %fusion.4, bf16[256,1024]{1,0:T(8,128)(2,1)S(1)} %fusion.4, ...), branch_computations={%region_260.261_spmd, %region_261.262_spmd, %region_262.263_spmd, ... | conditional | bytes 2097200 | solution.py:68
  146.7 0.1 collective-permute-start.481
  146.8 16.8 %collective-permute-done.481 = bf16[256,1024]{1,0:T(8,128)(2,1)} collective-permute-done((bf16[256,1024]{1,0:T(8,128)(2,1)S(1)}, bf16[256,1024]{1,0:T(8,128)(2,1)}, u32[]{:S(2)}, u32[]{:S(2)}) %collective-permute-start.481) | collective-permute-done | bytes 524320 | tf_op jit(solution)/shard_map/cond/branch_227_fun/ppermute | solution.py:17
  173.8 2.4 fusion.22
  176.1 1.3 fusion.26
  178.1 70.0 %conditional.6 = (bf16[256,1024]{1,0:T(8,128)(2,1)}) conditional(s32[]{:T(128)} %clamp.18, bf16[256,1024]{1,0:T(8,128)(2,1)S(1)} %fusion.4, bf16[256,1024]{1,0:T(8,128)(2,1)S(1)} %fusion.4, bf16[256,1024]{1,0:T(8,128)(2,1)S(1)} %fusion.4, bf16[256,1024]{1,0:T(8,128)(2,1)S(1)} %fusion.4, ...), branch_computations={%region_3.4_spmd, %region_4.5_spmd, %region_5.6_spmd, %region_6.7_... | conditional | bytes 2097200 | solution.py:68
  191.6 6.6 %collective-permute-start.59 = (bf16[256,1024]{1,0:T(8,128)(2,1)S(1)}, bf16[256,1024]{1,0:T(8,128)(2,1)}, u32[]{:S(2)}, u32[]{:S(2)}) collective-permute-start(bf16[256,1024]{1,0:T(8,128)(2,1)S(1)} %param.60), channel_id=1, source_target_pairs={{0,196},{1,197},{2,198},{3,199},{4,200},{5,201},{6,202},{7,203},{8... | collective-permute-start | bytes 1572872 | tf_op jit(solution)/shard_map/cond/branch_60_fun/ppermute | solution.py:17
  198.2 21.6 %collective-permute-done.59 = bf16[256,1024]{1,0:T(8,128)(2,1)} collective-permute-done((bf16[256,1024]{1,0:T(8,128)(2,1)S(1)}, bf16[256,1024]{1,0:T(8,128)(2,1)}, u32[]{:S(2)}, u32[]{:S(2)}) %collective-permute-start.59) | collective-permute-done | bytes 524320 | tf_op jit(solution)/shard_map/cond/branch_60_fun/ppermute | solution.py:17
  248.1 2.3 fusion.20
  250.4 0.6 add_add_fusion
  251.0 0.3 fusion.28
  251.3 1.4 convolution_add_fusion.3
  252.7 1.4 convolution_add_fusion.2
  254.1 1.5 fusion.12
  255.6 1.2 fusion.14
  256.8 0.4 convolution_convert_fusion
  257.3 87.2 %conditional.11 = (bf16[256,1024]{1,0:T(8,128)(2,1)S(1)}) conditional(s32[]{:T(128)} %clamp.23, bf16[256,1024]{1,0:T(8,128)(2,1)S(1)} %convolution_convert_fusion, bf16[256,1024]{1,0:T(8,128)(2,1)S(1)} %convolution_convert_fusion, bf16[256,1024]{1,0:T(8,128)(2,1)S(1)} %convolution_convert_fusion, ...), branch_computations={%region_1287.1288_spmd, %region_1288.1289_spmd, %region_1289.1290_... | conditional | bytes 3145776 | solution.py:68
  271.6 15.6 %collective-permute-start.1364 = (bf16[256,1024]{1,0:T(8,128)(2,1)S(1)}, bf16[256,1024]{1,0:T(8,128)(2,1)S(1)}, u32[]{:S(2)}, u32[]{:S(2)}) collective-permute-start(bf16[256,1024]{1,0:T(8,128)(2,1)S(1)} %param.1370), channel_id=1, source_target_pairs={{0,166},{1,167},{2,168},{3,169},{4,170},{5,171},{6,172},{7,173},{8... | collective-permute-start | bytes 1572872 | tf_op jit(solution)/shard_map/cond/branch_90_fun/ppermute | solution.py:17
  287.2 29.1 %collective-permute-done.1364 = bf16[256,1024]{1,0:T(8,128)(2,1)S(1)} collective-permute-done((bf16[256,1024]{1,0:T(8,128)(2,1)S(1)}, bf16[256,1024]{1,0:T(8,128)(2,1)S(1)}, u32[]{:S(2)}, u32[]{:S(2)}) %collective-permute-start.1364) | collective-permute-done | bytes 524320 | tf_op jit(solution)/shard_map/cond/branch_90_fun/ppermute | solution.py:17
  344.5 0.0 copy-start.9
  344.5 0.8 copy-done.9
  345.3 0.4 convolution_convert_fusion.1
  345.7 81.5 %conditional.10 = (bf16[256,1024]{1,0:T(8,128)(2,1)S(1)}) conditional(s32[]{:T(128)} %clamp.22, bf16[256,1024]{1,0:T(8,128)(2,1)S(1)} %convolution_convert_fusion.1, bf16[256,1024]{1,0:T(8,128)(2,1)S(1)} %convolution_convert_fusion.1, bf16[256,1024]{1,0:T(8,128)(2,1)S(1)} %convolution_convert_fusion.1, ...), branch_computations={%region_1031.1032_spmd, %region_1032.1033_spmd, %region_1033.1034_... | conditional | bytes 3145776 | solution.py:68
  348.5 19.1 %collective-permute-start.1048 = (bf16[256,1024]{1,0:T(8,128)(2,1)S(1)}, bf16[256,1024]{1,0:T(8,128)(2,1)S(1)}, u32[]{:S(2)}, u32[]{:S(2)}) collective-permute-start(bf16[256,1024]{1,0:T(8,128)(2,1)S(1)} %param.1053), channel_id=1, source_target_pairs={{0,227},{1,228},{2,229},{3,230},{4,231},{5,232},{6,233},{7,234},{8... | collective-permute-start | bytes 1572872 | tf_op jit(solution)/shard_map/cond/branch_29_fun/ppermute | solution.py:17
  367.6 17.3 %collective-permute-done.1048 = bf16[256,1024]{1,0:T(8,128)(2,1)S(1)} collective-permute-done((bf16[256,1024]{1,0:T(8,128)(2,1)S(1)}, bf16[256,1024]{1,0:T(8,128)(2,1)S(1)}, u32[]{:S(2)}, u32[]{:S(2)}) %collective-permute-start.1048) | collective-permute-done | bytes 524320 | tf_op jit(solution)/shard_map/cond/branch_29_fun/ppermute | solution.py:17
  427.2 0.4 convolution_convert_fusion.2
  427.6 0.0 copy-start.2
  427.7 0.0 copy-start.10
  427.7 79.0 %conditional.9 = (bf16[256,1024]{1,0:T(8,128)(2,1)S(1)}) conditional(s32[]{:T(128)} %clamp.21, bf16[256,1024]{1,0:T(8,128)(2,1)S(1)} %convolution_convert_fusion.2, bf16[256,1024]{1,0:T(8,128)(2,1)S(1)} %convolution_convert_fusion.2, bf16[256,1024]{1,0:T(8,128)(2,1)S(1)} %convolution_convert_fusion.2, ...), branch_computations={%region_775.776_spmd, %region_776.777_spmd, %region_777.778_spmd, ... | conditional | bytes 3145776 | solution.py:68
  455.1 8.3 %collective-permute-start.960 = (bf16[256,1024]{1,0:T(8,128)(2,1)S(1)}, bf16[256,1024]{1,0:T(8,128)(2,1)S(1)}, u32[]{:S(2)}, u32[]{:S(2)}) collective-permute-start(bf16[256,1024]{1,0:T(8,128)(2,1)S(1)} %param.964), channel_id=1, source_target_pairs={{0,60},{1,61},{2,62},{3,63},{4,64},{5,65},{6,66},{7,67},{8,68},{9,... | collective-permute-start | bytes 1572872 | tf_op jit(solution)/shard_map/cond/branch_196_fun/ppermute | solution.py:17
  463.4 23.2 %collective-permute-done.960 = bf16[256,1024]{1,0:T(8,128)(2,1)S(1)} collective-permute-done((bf16[256,1024]{1,0:T(8,128)(2,1)S(1)}, bf16[256,1024]{1,0:T(8,128)(2,1)S(1)}, u32[]{:S(2)}, u32[]{:S(2)}) %collective-permute-start.960) | collective-permute-done | bytes 524320 | tf_op jit(solution)/shard_map/cond/branch_196_fun/ppermute | solution.py:17
  506.8 0.6 copy-done.8
  507.4 0.7 fusion.16
  508.1 1.2 fusion.18
  509.3 7.4 %fusion.30 = f32[3]{0:T(128)S(1)} fusion(f32[1]{0:T(128)} %bitcast.7, f32[1]{0:T(128)} %bitcast.6, f32[1]{0:T(128)} %bitcast.5, f32[1]{0:T(128)} %bitcast.10, f32[1]{0:T(128)} %bitcast.9, f32[1]{0:T(128)} %bitcast.8, f32[1]{0:T(128)} %bitcast.13, f32[1]{0:T(128)} %bitcast.12, f32[1]{0:T(128)} %bitcast.11, f32[1]{0:T(128)} %bitcast.16, f32[1]{0:T(128)} %bitcast.15, ...), kind=kLoop, calls=%fused_computation.66 | loop fusion | flops 33 | bytes 60 | tf_op jit(solution)/shard_map/add | solution.py:99
  516.7 92.7 %psum.7 = f32[3]{0:T(128)S(1)} all-reduce(f32[3]{0:T(128)S(1)} %fusion.30), channel_id=1, replica_groups=mesh['dp'=256] {'dp'}, use_global_device_ids=true, to_apply=%region_1556.1557 | all-reduce | flops 3 | bytes 24 | tf_op jit(solution)/shard_map/psum | solution.py:100
  609.4 0.5 broadcast_multiply_fusion
  (18 shorter events, 0.1 us)
Async XLA Ops:
  0.6 4.0 copy-start
  3.4 1.5 copy-start.1
  4.9 0.6 copy-start.7
  28.3 55.8 %collective-permute-start.675 = (bf16[256,1024]{1,0:T(8,128)(2,1)S(1)}, bf16[256,1024]{1,0:T(8,128)(2,1)}, u32[]{:S(2)}, u32[]{:S(2)}) collective-permute-start(bf16[256,1024]{1,0:T(8,128)(2,1)S(1)} %param.678), channel_id=1, source_target_pairs={{0,90},{1,91},{2,92},{3,93},{4,94},{5,95},{6,96},{7,97},{8,98},{9,... | collective-permute-start | bytes 1572872 | tf_op jit(solution)/shard_map/cond/branch_166_fun/ppermute | solution.py:17
  146.7 16.9 %collective-permute-start.481 = (bf16[256,1024]{1,0:T(8,128)(2,1)S(1)}, bf16[256,1024]{1,0:T(8,128)(2,1)}, u32[]{:S(2)}, u32[]{:S(2)}) collective-permute-start(bf16[256,1024]{1,0:T(8,128)(2,1)S(1)} %param.483), channel_id=1, source_target_pairs={{0,29},{1,30},{2,31},{3,32},{4,33},{5,34},{6,35},{7,36},{8,37},{9,... | collective-permute-start | bytes 1572872 | tf_op jit(solution)/shard_map/cond/branch_227_fun/ppermute | solution.py:17
  177.4 73.5 %copy-start.5 = (f32[256,256]{0,1:T(8,128)}, f32[256,256]{0,1:T(8,128)S(1)}, u32[]{:S(2)}) copy-start(f32[256,256]{0,1:T(8,128)S(1)} %get-tuple-element.3121) | copy-start | bytes 786436
  191.6 28.2 %collective-permute-start.59 = (bf16[256,1024]{1,0:T(8,128)(2,1)S(1)}, bf16[256,1024]{1,0:T(8,128)(2,1)}, u32[]{:S(2)}, u32[]{:S(2)}) collective-permute-start(bf16[256,1024]{1,0:T(8,128)(2,1)S(1)} %param.60), channel_id=1, source_target_pairs={{0,196},{1,197},{2,198},{3,199},{4,200},{5,201},{6,202},{7,203},{8... | collective-permute-start | bytes 1572872 | tf_op jit(solution)/shard_map/cond/branch_60_fun/ppermute | solution.py:17
  250.4 1.0 copy-start.3
  271.6 44.7 %collective-permute-start.1364 = (bf16[256,1024]{1,0:T(8,128)(2,1)S(1)}, bf16[256,1024]{1,0:T(8,128)(2,1)S(1)}, u32[]{:S(2)}, u32[]{:S(2)}) collective-permute-start(bf16[256,1024]{1,0:T(8,128)(2,1)S(1)} %param.1370), channel_id=1, source_target_pairs={{0,166},{1,167},{2,168},{3,169},{4,170},{5,171},{6,172},{7,173},{8... | collective-permute-start | bytes 1572872 | tf_op jit(solution)/shard_map/cond/branch_90_fun/ppermute | solution.py:17
  344.5 0.8 copy-start.9
  345.7 81.5 %copy-start.4 = (f32[256,256]{0,1:T(8,128)S(1)}, f32[256,256]{0,1:T(8,128)}, u32[]{:S(2)}) copy-start(f32[256,256]{0,1:T(8,128)} %copy-done.3) | copy-start | bytes 786436
  348.5 36.4 %collective-permute-start.1048 = (bf16[256,1024]{1,0:T(8,128)(2,1)S(1)}, bf16[256,1024]{1,0:T(8,128)(2,1)S(1)}, u32[]{:S(2)}, u32[]{:S(2)}) collective-permute-start(bf16[256,1024]{1,0:T(8,128)(2,1)S(1)} %param.1053), channel_id=1, source_target_pairs={{0,227},{1,228},{2,229},{3,230},{4,231},{5,232},{6,233},{7,234},{8... | collective-permute-start | bytes 1572872 | tf_op jit(solution)/shard_map/cond/branch_29_fun/ppermute | solution.py:17
  427.6 79.1 %copy-start.2 = (bf16[256,1024]{1,0:T(8,128)(2,1)S(1)}, bf16[256,1024]{1,0:T(8,128)(2,1)}, u32[]{:S(2)}) copy-start(bf16[256,1024]{1,0:T(8,128)(2,1)} %param.1542) | copy-start | bytes 1572868
  427.7 79.1 %copy-start.6 = (f32[256,256]{0,1:T(8,128)S(1)}, f32[256,256]{0,1:T(8,128)}, u32[]{:S(2)}) copy-start(f32[256,256]{0,1:T(8,128)} %copy-done.5) | copy-start | bytes 786436
  427.7 79.1 %copy-start.10 = (bf16[256,1024]{1,0:T(8,128)(2,1)S(1)}, bf16[256,1024]{1,0:T(8,128)(2,1)}, u32[]{:S(2)}) copy-start(bf16[256,1024]{1,0:T(8,128)(2,1)} %copy-done.9) | copy-start | bytes 1572868
  455.1 31.5 %collective-permute-start.960 = (bf16[256,1024]{1,0:T(8,128)(2,1)S(1)}, bf16[256,1024]{1,0:T(8,128)(2,1)S(1)}, u32[]{:S(2)}, u32[]{:S(2)}) collective-permute-start(bf16[256,1024]{1,0:T(8,128)(2,1)S(1)} %param.964), channel_id=1, source_target_pairs={{0,60},{1,61},{2,62},{3,63},{4,64},{5,65},{6,66},{7,67},{8,68},{9,... | collective-permute-start | bytes 1572872 | tf_op jit(solution)/shard_map/cond/branch_196_fun/ppermute | solution.py:17
  506.7 0.7 copy-start.8
where the time goes:
time: 620 us; the launch traced here: 610 us
  loops' own time  269 us (43%)
  waiting for transfers between devices  150 us (24%)
  blocking collectives  92.7 us (15%)
  starting transfers between devices  63.6 us (10%)
  matrix products  14.8 us (2%)
  other arithmetic  12.5 us (2%)
    another operation x6, loops' own time, route_blocks(): return lax.switch(offset, branches, value)  269 us
    ppermute x6, waiting for transfers between devices, passed_along(): lax.ppermute(shard, axis, [(i, (i + by) % peers) for i in range(peers)])  150 us
    psum x1, blocking collectives, local(): totals = lax.psum(totals, 'dp')  92.7 us
    ppermute x6, starting transfers between devices, passed_along(): lax.ppermute(shard, axis, [(i, (i + by) % peers) for i in range(peers)])  63.6 us
  transfers between devices with their start and end apart: 6, of which 6 were waited for; matrix products, arithmetic and copies ran while one was open for 0% of the time, Pallas kernels for 0%

commit v1 on v0

v1 whole, which is shorter than its diff:
```python
from functools import partial

import jax
import jax.numpy as jnp
import numpy as np
from jax import lax
from jax.experimental import pallas as pl
from jax.experimental.pallas import tpu as pltpu
from jax.sharding import PartitionSpec as P

EPSILON = 1e-06
ROUNDS = 3
HALF = 128
BRANCHES = (8, 4, 4)
STAGES = ((1, 8), (8, 4), (32, 8))
MESH = pl.DeviceIdType.MESH


def shift_costs():
    return np.array(COST, np.int32)


COST = [112, 165, 217, 270, 217, 165, 151, 165, 178, 191, 217, 270, 230, 243, 256, 270, 256, 243, 230, 270, 217, 191, 178, 165, 151, 165, 217, 270, 217, 165, 161, 165, 168, 171, 217, 270, 217, 184, 187, 191, 194, 197, 217, 270, 230, 243, 256, 270, 256, 243, 230, 270, 233, 237, 240, 243, 247, 250, 253, 270, 260, 263, 266, 270, 273, 276, 279, 283, 286, 289, 292, 296, 299, 302, 306, 309, 312, 315, 319, 322, 325, 329, 332, 335, 338, 342, 345, 348, 352, 355, 358, 361, 365, 368, 371, 375, 378, 381, 384, 388, 391, 394, 397, 401, 404, 407, 411, 414, 417, 420, 424, 427, 430, 434, 437, 440, 443, 447, 450, 453, 457, 460, 463, 466, 470, 473, 476, 480]


def schedule_kernel(plan_ref, cost_ref, out_ref):
    me = lax.axis_index("dp")
    offsets = [(plan_ref[0, r] - me) & 255 for r in range(ROUNDS)]

    def cost(distance):
        return cost_ref[jnp.maximum(jnp.minimum(distance, 256 - distance) - 1, 0)]

    far = jnp.int32(1 << 28)
    best = [cost(s) for s in offsets]
    parent = [jnp.int32(0)] * ROUNDS
    step_of = list(offsets)
    done = [jnp.int32(0)] * ROUNDS
    for step in range(ROUNDS):
        keys = [jnp.where(done[j] == 1, far, best[j]) for j in range(ROUNDS)]
        first = (keys[0] <= keys[1]) & (keys[0] <= keys[2])
        pick = jnp.where(first, 0, jnp.where(keys[1] <= keys[2], 1, 2))

        def chosen(values):
            return jnp.where(pick == 0, values[0], jnp.where(pick == 1, values[1], values[2]))

        distance = chosen(step_of)
        at = chosen(offsets)
        wrapped = jnp.where(distance <= HALF, 0, 1)
        out_ref[4 * step] = chosen(parent)
        out_ref[4 * step + 1] = jnp.maximum(jnp.minimum(distance, 256 - distance) - 1, 0)
        out_ref[4 * step + 2] = wrapped
        out_ref[4 * step + 3] = 0
        for j in range(ROUNDS):
            done[j] = jnp.where(pick == j, 1, done[j])
            onward = (offsets[j] - at) & 255
            price = cost(onward)
            nearer = price < best[j]
            best[j] = jnp.where(nearer, price, best[j])
            parent[j] = jnp.where(nearer, step + 1, parent[j])
            step_of[j] = jnp.where(nearer, onward, step_of[j])


def make_schedule(plan):
    return pl.pallas_call(
        schedule_kernel,
        out_shape=jax.ShapeDtypeStruct((4 * ROUNDS,), jnp.int32),
        in_specs=[pl.BlockSpec(memory_space=pltpu.SMEM)] * 2,
        out_specs=pl.BlockSpec(memory_space=pltpu.SMEM),
    )(plan, jnp.asarray(shift_costs()))


def both_ways(distance, blocks):
    ahead, back = blocks
    peers = lax.axis_size("dp")
    return (
        lax.ppermute(ahead, "dp", [(i, (i + distance) % peers) for i in range(peers)]),
        lax.ppermute(back, "dp", [(i, (i - distance) % peers) for i in range(peers)]),
    )


def exchange(distances, digits, widths, blocks):
    if not widths:
        return both_ways(distances[0], blocks)
    count = len(distances) // widths[0]
    branches = [
        partial(exchange, distances[i * count : (i + 1) * count], digits[1:], widths[1:])
        for i in range(widths[0])
    ]
    return lax.switch(digits[0], branches, blocks)


def unit_rows(raw):
    wide = raw.astype(jnp.float32)
    recip = lax.rsqrt(jnp.sum(wide * wide, axis=-1, keepdims=True) + EPSILON)
    wide = wide * recip
    return wide, recip, wide.astype(jnp.bfloat16)


def dot_t(a, b):
    return lax.dot_general(a, b, (((1,), (1,)), ((), ())), preferred_element_type=jnp.float32)


def project(wide, recip, grad):
    along = jnp.sum(wide * grad, axis=-1, keepdims=True)
    return recip * (grad - wide * along)


def loss_kernel(scale_ref, bias_ref, held_ref, row_ref, ga_ref, gt_ref, tot_ref):
    scale = jnp.exp(jnp.full((1, 1), scale_ref[0], jnp.float32))
    bias = bias_ref[0]
    n = held_ref.shape[2]
    rows = lax.broadcasted_iota(jnp.int32, (n, n), 0)
    cols = lax.broadcasted_iota(jnp.int32, (n, n), 1)
    eye = (rows == cols).astype(jnp.float32)

    audio_wide, audio_recip, audio_unit = unit_rows(held_ref[0, 0])
    text_wide, text_recip, text_unit = unit_rows(held_ref[0, 1])
    losses_sum = jnp.zeros((n, n), jnp.float32)
    slopes_sum = jnp.zeros((n, n), jnp.float32)
    scaled_sum = jnp.zeros((n, n), jnp.float32)
    audio_grad = jnp.zeros(audio_wide.shape, jnp.float32)
    text_grad = jnp.zeros(text_wide.shape, jnp.float32)
    for slot in range(ROUNDS + 1):
        far_text = text_unit if slot == 0 else unit_rows(held_ref[slot, 1])[2]
        far_audio = audio_unit if slot == 0 else unit_rows(held_ref[slot, 0])[2]
        scaled = scale * dot_t(audio_unit, far_text)
        logits = scaled + bias
        small = jnp.exp(-jnp.abs(logits))
        slopes = jnp.where(logits >= 0.0, 1.0, small) / (1.0 + small)
        if slot == 0:
            flipped = jnp.where(rows == cols, -logits, logits)
            slopes = slopes - eye
        else:
            flipped = logits
        losses_sum = losses_sum + (jnp.maximum(flipped, 0.0) + jnp.log1p(small))
        slopes_sum = slopes_sum + slopes
        scaled_sum = scaled_sum + slopes * scaled
        weights = (scale * slopes).astype(jnp.bfloat16)
        audio_grad = audio_grad + jnp.dot(weights, far_text, preferred_element_type=jnp.float32)

        logits = scale * dot_t(text_unit, far_audio) + bias
        small = jnp.exp(-jnp.abs(logits))
        slopes = jnp.where(logits >= 0.0, 1.0, small) / (1.0 + small)
        if slot == 0:
            slopes = slopes - eye
        weights = (scale * slopes).astype(jnp.bfloat16)
        text_grad = text_grad + jnp.dot(weights, far_audio, preferred_element_type=jnp.float32)

    ga_ref[...] = project(audio_wide, audio_recip, audio_grad)
    gt_ref[...] = project(text_wide, text_recip, text_grad)
    folded = losses_sum[:, : n // 2] + losses_sum[:, n // 2 :]
    row_ref[...] = jnp.sum(folded.T, axis=0, keepdims=True)
    parts = []
    for total in (losses_sum, slopes_sum, scaled_sum):
        down = jnp.sum(total, axis=0, keepdims=True)
        parts.append(down[:, : n // 2] + down[:, n // 2 :])
    tot_ref[...] = jnp.concatenate(parts + [jnp.zeros((5, n // 2), jnp.float32)], axis=0)


def loss_and_grads(log_scale, bias, held):
    n, d = held.shape[2:]
    vmem = pl.BlockSpec(memory_space=pltpu.VMEM)
    smem = pl.BlockSpec(memory_space=pltpu.SMEM)
    return pl.pallas_call(
        loss_kernel,
        out_shape=(
            jax.ShapeDtypeStruct((1, n), jnp.float32),
            jax.ShapeDtypeStruct((n, d), jnp.float32),
            jax.ShapeDtypeStruct((n, d), jnp.float32),
            jax.ShapeDtypeStruct((8, n // 2), jnp.float32),
        ),
        in_specs=[smem, smem, vmem],
        out_specs=(vmem, vmem, vmem, vmem),
        compiler_params=pltpu.CompilerParams(vmem_limit_bytes=48 * 1024 * 1024),
    )(log_scale, bias, held)


def stats_kernel(denominator, part_ref, out_ref, *scratch):
    me = lax.axis_index("dp")
    buffers, sends, recvs = scratch[0:3], scratch[3:6], scratch[6:9]
    groups = []
    for stride, peers in STAGES:
        digit = lax.rem(lax.div(me, stride), peers)
        others = []
        for k in range(1, peers):
            other = lax.rem(digit + k, peers)
            others.append((other, me + (other - digit) * stride))
        groups.append((digit, others))
    barrier = pltpu.get_barrier_semaphore()
    count = 0
    for _, others in groups:
        for _, device in others:
            pl.semaphore_signal(barrier, inc=1, device_id=(device,), device_id_type=MESH)
            count += 1
    pl.semaphore_wait(barrier, count)
    value = part_ref[...]
    for stage, (digit, others) in enumerate(groups):
        buffer, send, recv = buffers[stage], sends[stage], recvs[stage]
        buffer[digit] = value
        for other, device in others:
            pltpu.make_async_remote_copy(
                src_ref=buffer.at[digit],
                dst_ref=buffer.at[digit],
                send_sem=send.at[other],
                recv_sem=recv.at[digit],
                device_id=(device,),
                device_id_type=MESH,
            ).start()
        for other, device in others:
            arrived = pltpu.make_async_remote_copy(
                src_ref=buffer.at[digit],
                dst_ref=buffer.at[other],
                send_sem=send.at[other],
                recv_sem=recv.at[other],
                device_id=(device,),
                device_id_type=MESH,
            )
            arrived.wait_recv()
            arrived.wait_send()
        value = buffer[0]
        for j in range(1, STAGES[stage][1]):
            value = value + buffer[j]
    total = jnp.sum(value, axis=1, keepdims=True) / denominator
    out_ref[...] = jnp.broadcast_to(total, out_ref.shape)


def all_stats(parts, denominator):
    vmem = pl.BlockSpec(memory_space=pltpu.VMEM)
    scratch = [pltpu.VMEM((peers,) + parts.shape, jnp.float32) for _, peers in STAGES]
    scratch += [pltpu.SemaphoreType.DMA((peers,)) for _, peers in STAGES] * 2
    return pl.pallas_call(
        partial(stats_kernel, denominator),
        out_shape=jax.ShapeDtypeStruct(parts.shape, jnp.float32),
        in_specs=[vmem],
        out_specs=vmem,
        scratch_shapes=scratch,
        compiler_params=pltpu.CompilerParams(collective_id=0, has_side_effects=True),
    )(parts)[:3, 0]


def local(audio, text, log_scale, bias, plan):
    n, d = audio.shape
    player_count = lax.axis_size("dp")
    steps = make_schedule(plan)
    held = jnp.zeros((ROUNDS + 1, 2, n, d), audio.dtype)
    held = held.at[0, 0].set(audio).at[0, 1].set(text)

    def fetch(step, held):
        parent, branch, wrapped = [steps[4 * step + i] for i in range(3)]
        blocks = (held[parent, wrapped], held[parent, 1 - wrapped])
        digits = []
        for width in reversed(BRANCHES):
            digits.insert(0, lax.rem(branch, width))
            branch = lax.div(branch, width)
        ahead, back = exchange(list(range(1, HALF + 1)), digits, BRANCHES, blocks)
        held = held.at[step + 1, wrapped].set(ahead)
        return held.at[step + 1, 1 - wrapped].set(back)

    held = lax.fori_loop(0, ROUNDS, fetch, held)
    row_loss, grad_audio, grad_text, parts = loss_and_grads(log_scale, bias, held)
    stats = all_stats(parts, float((ROUNDS + 1) * n * n * player_count))
    return (row_loss.reshape(n), grad_audio, grad_text, stats)


def solution(mesh):
    return jax.shard_map(
        local,
        mesh=mesh,
        in_specs=(P("dp", None), P("dp", None), P(), P(), P("dp", None)),
        out_specs=(P("dp"), P("dp", None), P("dp", None), P()),
        check_vma=False,
    )
```

time: 620 us -> 340 us (0.55); the launches traced: 610 us -> 338 us
  loops' own time: 269 us -> 153 us
  blocking collectives: 92.7 us -> 0 us
  waiting for transfers between devices: 150 us -> 58.4 us
  Pallas kernels: 0 us -> 43.5 us
  starting transfers between devices: 63.6 us -> 47.6 us
  matrix products: 14.8 us -> 0 us
  local copies, waits for them, and re-layouts: 3.33 us -> 13.9 us
  other arithmetic: 12.5 us -> 19.3 us
    another operation x6 -> x10, loops' own time: 269 us -> 153 us  [the longest x9 118 us: exchange(): return lax.switch(digits[0], branches, blocks)]
    psum x1 -> x0, blocking collectives: 92.7 us -> none  [local(): totals = lax.psum(totals, 'dp')]
    ppermute x6, waiting for transfers between devices: 150 us -> 58.4 us  [the longest x3 36.7 us: both_ways(): lax.ppermute(ahead, 'dp', [(i, (i + distance) % peers) for i in range(pee...]
    pallas_call x0 -> x3, Pallas kernels: none -> 43.5 us  [the longest x1 34.5 us: all_stats(): pl.pallas_call(partial(stats_kernel, denominator), out_shape=jax.ShapeDty...]
    scatter x0 -> x6, other arithmetic: none -> 17.2 us  [the longest x3 8.59 us: fetch(): held = held.at[step + 1, wrapped].set(ahead)]
    ppermute x6, starting transfers between devices: 63.6 us -> 47.6 us  [the longest x3 34.4 us: both_ways(): lax.ppermute(back, 'dp', [(i, (i - distance) % peers) for i in range(peer...]
    dot_general x12 -> x0, matrix products: 14.8 us -> none  [the longest x4 8.26 us: block_logits(): jnp.dot(left_rows, right_rows.T, preferred_element_type=jnp.float32)]
    add x2 -> x0, other arithmetic: 7.97 us -> none  [the longest x1 7.37 us: local(): totals = totals + block_sums]
  transfers between devices with their start and end apart: 6 -> 6, of which waited for: 6 -> 4; matrix products, arithmetic and copies ran while one was open for 0% -> 0% of each run, Pallas kernels for 0% -> 0%
where the time goes in v1:
time: 340 us; the launch traced here: 338 us
  loops' own time  153 us (45%)
  waiting for transfers between devices  58.4 us (17%)
  starting transfers between devices  47.6 us (14%)
  Pallas kernels  43.5 us (13%)
  other arithmetic  19.3 us (6%)
  local copies, waits for them, and re-layouts  13.9 us (4%)
    another operation x9, loops' own time, exchange(): return lax.switch(digits[0], branches, blocks)  118 us
    ppermute x3, waiting for transfers between devices, both_ways(): lax.ppermute(ahead, 'dp', [(i, (i + distance) % peers) for i in range(pee...  36.7 us
    another operation x1, loops' own time, local(): held = lax.fori_loop(0, ROUNDS, fetch, held)  34.5 us
    pallas_call x1, Pallas kernels, all_stats(): pl.pallas_call(partial(stats_kernel, denominator), out_shape=jax.ShapeDty...  34.5 us
    ppermute x3, starting transfers between devices, both_ways(): lax.ppermute(back, 'dp', [(i, (i - distance) % peers) for i in range(peer...  34.4 us
    ppermute x3, waiting for transfers between devices, both_ways(): lax.ppermute(back, 'dp', [(i, (i - distance) % peers) for i in range(peer...  21.7 us
    ppermute x3, starting transfers between devices, both_ways(): lax.ppermute(ahead, 'dp', [(i, (i + distance) % peers) for i in range(pee...  13.3 us
    scatter x3, other arithmetic, fetch(): held = held.at[step + 1, wrapped].set(ahead)  8.59 us
  transfers between devices with their start and end apart: 6, of which 4 were waited for; matrix products, arithmetic and copies ran while one was open for 0% of the time, Pallas kernels for 0%

profile of v1, /device:TPU:1, one launch (start us, length us, event | category | flops | bytes accessed | tf_op | source)
XLA Modules:
  0.0 337.5 jit_solution(7514349229095007463)
XLA Ops:
  0.6 0.0 copy-start.2
  0.6 0.0 copy-start.1
  0.7 0.6 fusion.1
  1.2 3.6 %scatter.14 = bf16[4,2,256,1024]{3,2,1,0:T(8,128)(2,1)} pad(bf16[1,1,256,1024]{3,2,1,0:T(8,128)(2,1)} %bitcast.312, bf16[]{:T(256)} %constant.446.clone.1), padding=0_3x0_1x0_0x0_0 | pad | bytes 4718594 | tf_op jit(solution)/shard_map/scatter | solution.py:246
  4.8 0.0 copy-done.1
  4.8 2.2 bitcast_dynamic-update-slice_fusion
  7.0 1.3 shard_map.93
  8.4 283.6 %while.19 = (s32[]{:T(128)}, bf16[4,2,256,1024]{3,2,1,0:T(8,128)(2,1)}, s32[12]{0:T(128)S(1)}, s32[]{:T(128)}, s32[]{:T(128)}, /*index=5*/s32[]{:T(128)}, s32[]{...) while((s32[]{:T(128)}, ...), condition=%wide.region_171.172_spmd, body=%wide.region_0.171_spmd.sunk | while | flops 524396 | bytes 9441284 | solution.py:259
  8.6 0.6 fusion.3
  16.4 66.1 %conditional.42 = ((bf16[1,1,256,1024]{3,2,1,0:T(8,128)(2,1)}, bf16[1,1,256,1024]{3,2,1,0:T(8,128)(2,1)})) conditional(s32[]{:T(128)} %clamp.131, (s32[]{:T(128)}, pred[]{:T(512)}, s32[]{:T(128)}, pred[]{:T(512)}, bf16[4,2,256,1024]{3,2,1,0:T(8,128)(2,1)}, /*index=5*/s32[]{:T(128)}, s32[]{:T(128)}, ...), branch_computations={%region_2.22_spmd, %region_23.43_spmd, %region_44.64_spmd, %region... | conditional | flops 6 | bytes 6291686 | solution.py:89
  16.4 1.3 dynamic-slice_bitcast_fusion
  17.7 24.5 %conditional.4 = ((bf16[1,1,256,1024]{3,2,1,0:T(8,128)(2,1)}, bf16[1,1,256,1024]{3,2,1,0:T(8,128)(2,1)})) conditional(s32[]{:T(128)} %clamp.93, (s32[]{:T(128)}, bf16[256,1024]{1,0:T(8,128)(2,1)S(1)}, bf16[256,1024]{1,0:T(8,128)(2,1)S(1)}) %tuple.754, (s32[]{:T(128)}, bf16[256,1024]{1,0:T(8,128)(2,1)S(1)}, ...), branch_computations={%region_3.6_spmd, %region_8.11_spmd, %region_13.16_spmd, %region_1... | conditional | flops 1 | bytes 4194440 | solution.py:89
  17.7 23.5 %conditional = (bf16[1,1,256,1024]{3,2,1,0:T(8,128)(2,1)}, bf16[1,1,256,1024]{3,2,1,0:T(8,128)(2,1)}) conditional(s32[]{:T(128)} %clamp.89, (bf16[256,1024]{1,0:T(8,128)(2,1)S(1)}, bf16[256,1024]{1,0:T(8,128)(2,1)S(1)}) %tuple.726, (bf16[256,1024]{1,0:T(8,128)(2,1)S(1)}, bf16[256,1024]{1,0:T(8,128)(2,1)S(1)}) %tuple.726, ...), branch_computations={%region_4.2_spmd, %region_5.0_spmd, %region_6.0_spmd, %region_7.0_... | conditional | bytes 4194400 | solution.py:89
  17.7 2.8 collective-permute-start
  20.5 12.1 %collective-permute-start.1 = (bf16[256,1024]{1,0:T(8,128)(2,1)S(1)}, bf16[256,1024]{1,0:T(8,128)(2,1)}, u32[]{:S(2)}, u32[]{:S(2)}) collective-permute-start(bf16[256,1024]{1,0:T(8,128)(2,1)S(1)} %get-tuple-element.1265), channel_id=1, source_target_pairs={{0,255},{1,0},{2,1},{3,2},{4,3},{5,4},{6,5},{7,6},{8,7},{9,8},{10,... | collective-permute-start | bytes 1572872 | tf_op jit(solution)/shard_map/while/body/eval_jaxpr/cond/branch_0_fun/cond/branch_0_fun/cond/branch_0_fun/ppermute | solution.py:77
  32.6 0.0 collective-permute-done
  32.6 8.6 %collective-permute-done.1 = bf16[256,1024]{1,0:T(8,128)(2,1)} collective-permute-done((bf16[256,1024]{1,0:T(8,128)(2,1)S(1)}, bf16[256,1024]{1,0:T(8,128)(2,1)}, u32[]{:S(2)}, u32[]{:S(2)}) %collective-permute-start.1) | collective-permute-done | bytes 524320 | tf_op jit(solution)/shard_map/while/body/eval_jaxpr/cond/branch_0_fun/cond/branch_0_fun/cond/branch_0_fun/ppermute | solution.py:77
  82.5 0.7 and_reduce_fusion.3
  83.2 2.8 select_dynamic-update-slice_fusion.4
  86.1 2.9 select_dynamic-update-slice_fusion.5
  91.9 0.6 fusion.3
  99.7 70.2 %conditional.42 = ((bf16[1,1,256,1024]{3,2,1,0:T(8,128)(2,1)}, bf16[1,1,256,1024]{3,2,1,0:T(8,128)(2,1)})) conditional(s32[]{:T(128)} %clamp.131, (s32[]{:T(128)}, pred[]{:T(512)}, s32[]{:T(128)}, pred[]{:T(512)}, bf16[4,2,256,1024]{3,2,1,0:T(8,128)(2,1)}, /*index=5*/s32[]{:T(128)}, s32[]{:T(128)}, ...), branch_computations={%region_2.22_spmd, %region_23.43_spmd, %region_44.64_spmd, %region... | conditional | flops 6 | bytes 6291686 | solution.py:89
  109.3 1.3 dynamic-slice_bitcast_fusion.2
  110.6 31.0 %conditional.9 = ((bf16[1,1,256,1024]{3,2,1,0:T(8,128)(2,1)}, bf16[1,1,256,1024]{3,2,1,0:T(8,128)(2,1)})) conditional(s32[]{:T(128)} %clamp.98, (s32[]{:T(128)}, bf16[256,1024]{1,0:T(8,128)(2,1)S(1)}, bf16[256,1024]{1,0:T(8,128)(2,1)S(1)}) %tuple.790, (s32[]{:T(128)}, bf16[256,1024]{1,0:T(8,128)(2,1)S(1)}, ...), branch_computations={%region_24.27_spmd, %region_29.32_spmd, %region_34.37_spmd, %regio... | conditional | flops 1 | bytes 4194440 | solution.py:89
  110.7 30.2 %conditional.5 = (bf16[1,1,256,1024]{3,2,1,0:T(8,128)(2,1)}, bf16[1,1,256,1024]{3,2,1,0:T(8,128)(2,1)}) conditional(s32[]{:T(128)} %clamp.94, (bf16[256,1024]{1,0:T(8,128)(2,1)S(1)}, bf16[256,1024]{1,0:T(8,128)(2,1)S(1)}) %tuple.762, (bf16[256,1024]{1,0:T(8,128)(2,1)S(1)}, ...), branch_computations={%region_25.23_spmd, %region_26.0_spmd, %region_27.0_spmd, %region_... | conditional | bytes 4194400 | solution.py:89
  110.7 2.2 collective-permute-start.32
  112.9 10.4 %collective-permute-start.33 = (bf16[256,1024]{1,0:T(8,128)(2,1)S(1)}, bf16[256,1024]{1,0:T(8,128)(2,1)}, u32[]{:S(2)}, u32[]{:S(2)}) collective-permute-start(bf16[256,1024]{1,0:T(8,128)(2,1)S(1)} %get-tuple-element.1317), channel_id=1, source_target_pairs={{0,239},{1,240},{2,241},{3,242},{4,243},{5,244},{6,245},{7,246},{8... | collective-permute-start | bytes 1572872 | tf_op jit(solution)/shard_map/while/body/eval_jaxpr/cond/branch_1_fun/cond/branch_0_fun/cond/branch_0_fun/ppermute | solution.py:77
  123.3 4.4 %collective-permute-done.32 = bf16[256,1024]{1,0:T(8,128)(2,1)} collective-permute-done((bf16[256,1024]{1,0:T(8,128)(2,1)S(1)}, bf16[256,1024]{1,0:T(8,128)(2,1)}, u32[]{:S(2)}, u32[]{:S(2)}) %collective-permute-start.32) | collective-permute-done | bytes 524320 | tf_op jit(solution)/shard_map/while/body/eval_jaxpr/cond/branch_1_fun/cond/branch_0_fun/cond/branch_0_fun/ppermute | solution.py:76
  127.8 13.1 %collective-permute-done.33 = bf16[256,1024]{1,0:T(8,128)(2,1)} collective-permute-done((bf16[256,1024]{1,0:T(8,128)(2,1)S(1)}, bf16[256,1024]{1,0:T(8,128)(2,1)}, u32[]{:S(2)}, u32[]{:S(2)}) %collective-permute-start.33) | collective-permute-done | bytes 524320 | tf_op jit(solution)/shard_map/while/body/eval_jaxpr/cond/branch_1_fun/cond/branch_0_fun/cond/branch_0_fun/ppermute | solution.py:77
  169.8 0.7 and_reduce_fusion.3
  170.6 2.9 select_dynamic-update-slice_fusion.4
  173.4 2.8 select_dynamic-update-slice_fusion.5
  179.2 0.6 fusion.3
  187.0 91.7 %conditional.42 = ((bf16[1,1,256,1024]{3,2,1,0:T(8,128)(2,1)}, bf16[1,1,256,1024]{3,2,1,0:T(8,128)(2,1)})) conditional(s32[]{:T(128)} %clamp.131, (s32[]{:T(128)}, pred[]{:T(512)}, s32[]{:T(128)}, pred[]{:T(512)}, bf16[4,2,256,1024]{3,2,1,0:T(8,128)(2,1)}, /*index=5*/s32[]{:T(128)}, s32[]{:T(128)}, ...), branch_computations={%region_2.22_spmd, %region_23.43_spmd, %region_44.64_spmd, %region... | conditional | flops 6 | bytes 6291686 | solution.py:89
  196.5 1.3 dynamic-slice_bitcast_fusion.8
  197.8 53.3 %conditional.24 = ((bf16[1,1,256,1024]{3,2,1,0:T(8,128)(2,1)}, bf16[1,1,256,1024]{3,2,1,0:T(8,128)(2,1)})) conditional(s32[]{:T(128)} %clamp.113, (s32[]{:T(128)}, bf16[256,1024]{1,0:T(8,128)(2,1)S(1)}, bf16[256,1024]{1,0:T(8,128)(2,1)S(1)}) %tuple.898, (s32[]{:T(128)}, bf16[256,1024]{1,0:T(8,128)(2,1)S(1)}, ...), branch_computations={%region_87.90_spmd, %region_92.95_spmd, %region_97.100_spmd, %regi... | conditional | flops 1 | bytes 4194440 | solution.py:89
  198.1 52.4 %conditional.23 = (bf16[1,1,256,1024]{3,2,1,0:T(8,128)(2,1)}, bf16[1,1,256,1024]{3,2,1,0:T(8,128)(2,1)}) conditional(s32[]{:T(128)} %clamp.112, (bf16[256,1024]{1,0:T(8,128)(2,1)S(1)}, bf16[256,1024]{1,0:T(8,128)(2,1)S(1)}) %tuple.894, (bf16[256,1024]{1,0:T(8,128)(2,1)S(1)}, ...), branch_computations={%region_103.101_spmd, %region_104.0_spmd, %region_105.0_spmd, %reg... | conditional | bytes 4194400 | solution.py:89
  198.1 8.3 %collective-permute-start.156 = (bf16[256,1024]{1,0:T(8,128)(2,1)S(1)}, bf16[256,1024]{1,0:T(8,128)(2,1)}, u32[]{:S(2)}, u32[]{:S(2)}) collective-permute-start(bf16[256,1024]{1,0:T(8,128)(2,1)S(1)} %get-tuple-element.1509), channel_id=1, source_target_pairs={{0,79},{1,80},{2,81},{3,82},{4,83},{5,84},{6,85},{7,86},{8,87},{9,... | collective-permute-start | bytes 1572872 | tf_op jit(solution)/shard_map/while/body/eval_jaxpr/cond/branch_4_fun/cond/branch_3_fun/cond/branch_2_fun/ppermute | solution.py:76
  206.4 11.8 %collective-permute-start.157 = (bf16[256,1024]{1,0:T(8,128)(2,1)S(1)}, bf16[256,1024]{1,0:T(8,128)(2,1)}, u32[]{:S(2)}, u32[]{:S(2)}) collective-permute-start(bf16[256,1024]{1,0:T(8,128)(2,1)S(1)} %get-tuple-element.1510), channel_id=1, source_target_pairs={{0,177},{1,178},{2,179},{3,180},{4,181},{5,182},{6,183},{7,184},{8... | collective-permute-start | bytes 1572872 | tf_op jit(solution)/shard_map/while/body/eval_jaxpr/cond/branch_4_fun/cond/branch_3_fun/cond/branch_2_fun/ppermute | solution.py:77
  218.2 32.3 %collective-permute-done.156 = bf16[256,1024]{1,0:T(8,128)(2,1)} collective-permute-done((bf16[256,1024]{1,0:T(8,128)(2,1)S(1)}, bf16[256,1024]{1,0:T(8,128)(2,1)}, u32[]{:S(2)}, u32[]{:S(2)}) %collective-permute-start.156) | collective-permute-done | bytes 524320 | tf_op jit(solution)/shard_map/while/body/eval_jaxpr/cond/branch_4_fun/cond/branch_3_fun/cond/branch_2_fun/ppermute | solution.py:76
  250.5 0.0 collective-permute-done.157
  278.7 0.7 and_reduce_fusion.3
  279.4 2.9 select_dynamic-update-slice_fusion.4
  282.3 2.9 select_dynamic-update-slice_fusion.5
  293.2 7.7 %shard_map.94 = (f32[1,256]{1,0:T(1,128)}, f32[256,1024]{1,0:T(8,128)}, f32[256,1024]{1,0:T(8,128)}, f32[8,128]{1,0:T(8,128)S(1)}) custom-call(f32[1]{0:T(128)S(6)} %copy.355.scale_ref, f32[1]{0:T(128)S(6)} %copy.356.bias_ref, bf16[4,2,256,1024]{3,2,1,0:T(8,128)(2,1)} %get-tuple-element.1695.held_ref), custom_call_target="tpu_custom_call" | custom-call | tf_op jit(solution)/shard_map/pallas_call | solution.py:164
  300.9 0.6 copy-done
  301.5 34.5 %shard_map.95 = f32[8,128]{1,0:T(8,128)} custom-call(f32[8,128]{1,0:T(8,128)} %copy-done), custom_call_target="tpu_custom_call" | custom-call | tf_op jit(solution)/shard_map/pallas_call | solution.py:231
  335.9 1.3 slice_reduce_fusion
  (3 shorter events, 0.0 us)
Async XLA Ops:
  0.6 7.7 %copy-start.2 = (s32[4]{0:T(128)S(1)}, s32[4]{0:T(128)}, u32[]{:S(2)}) copy-start(s32[4]{0:T(128)} %constant.438.clone.1) | copy-start | bytes 52
  0.6 4.2 %copy-start.1 = (bf16[256,1024]{1,0:T(8,128)(2,1)S(1)}, bf16[256,1024]{1,0:T(8,128)(2,1)}, u32[]{:S(2)}) copy-start(bf16[256,1024]{1,0:T(8,128)(2,1)} %param.185) | copy-start | bytes 1572868
  17.7 14.9 %collective-permute-start = (bf16[256,1024]{1,0:T(8,128)(2,1)S(1)}, bf16[256,1024]{1,0:T(8,128)(2,1)}, u32[]{:S(2)}, u32[]{:S(2)}) collective-permute-start(bf16[256,1024]{1,0:T(8,128)(2,1)S(1)} %get-tuple-element.1264), channel_id=1, source_target_pairs={{0,1},{1,2},{2,3},{3,4},{4,5},{5,6},{6,7},{7,8},{8,9},{9,10},{10,1... | collective-permute-start | bytes 1572872 | tf_op jit(solution)/shard_map/while/body/eval_jaxpr/cond/branch_0_fun/cond/branch_0_fun/cond/branch_0_fun/ppermute | solution.py:76
  20.5 20.7 %collective-permute-start.1 = (bf16[256,1024]{1,0:T(8,128)(2,1)S(1)}, bf16[256,1024]{1,0:T(8,128)(2,1)}, u32[]{:S(2)}, u32[]{:S(2)}) collective-permute-start(bf16[256,1024]{1,0:T(8,128)(2,1)S(1)} %get-tuple-element.1265), channel_id=1, source_target_pairs={{0,255},{1,0},{2,1},{3,2},{4,3},{5,4},{6,5},{7,6},{8,7},{9,8},{10,... | collective-permute-start | bytes 1572872 | tf_op jit(solution)/shard_map/while/body/eval_jaxpr/cond/branch_0_fun/cond/branch_0_fun/cond/branch_0_fun/ppermute | solution.py:77
  110.7 17.1 %collective-permute-start.32 = (bf16[256,1024]{1,0:T(8,128)(2,1)S(1)}, bf16[256,1024]{1,0:T(8,128)(2,1)}, u32[]{:S(2)}, u32[]{:S(2)}) collective-permute-start(bf16[256,1024]{1,0:T(8,128)(2,1)S(1)} %get-tuple-element.1316), channel_id=1, source_target_pairs={{0,17},{1,18},{2,19},{3,20},{4,21},{5,22},{6,23},{7,24},{8,25},{9,... | collective-permute-start | bytes 1572872 | tf_op jit(solution)/shard_map/while/body/eval_jaxpr/cond/branch_1_fun/cond/branch_0_fun/cond/branch_0_fun/ppermute | solution.py:76
  112.9 27.9 %collective-permute-start.33 = (bf16[256,1024]{1,0:T(8,128)(2,1)S(1)}, bf16[256,1024]{1,0:T(8,128)(2,1)}, u32[]{:S(2)}, u32[]{:S(2)}) collective-permute-start(bf16[256,1024]{1,0:T(8,128)(2,1)S(1)} %get-tuple-element.1317), channel_id=1, source_target_pairs={{0,239},{1,240},{2,241},{3,242},{4,243},{5,244},{6,245},{7,246},{8... | collective-permute-start | bytes 1572872 | tf_op jit(solution)/shard_map/while/body/eval_jaxpr/cond/branch_1_fun/cond/branch_0_fun/cond/branch_0_fun/ppermute | solution.py:77
  198.1 52.4 %collective-permute-start.156 = (bf16[256,1024]{1,0:T(8,128)(2,1)S(1)}, bf16[256,1024]{1,0:T(8,128)(2,1)}, u32[]{:S(2)}, u32[]{:S(2)}) collective-permute-start(bf16[256,1024]{1,0:T(8,128)(2,1)S(1)} %get-tuple-element.1509), channel_id=1, source_target_pairs={{0,79},{1,80},{2,81},{3,82},{4,83},{5,84},{6,85},{7,86},{8,87},{9,... | collective-permute-start | bytes 1572872 | tf_op jit(solution)/shard_map/while/body/eval_jaxpr/cond/branch_4_fun/cond/branch_3_fun/cond/branch_2_fun/ppermute | solution.py:76
  206.4 44.1 %collective-permute-start.157 = (bf16[256,1024]{1,0:T(8,128)(2,1)S(1)}, bf16[256,1024]{1,0:T(8,128)(2,1)}, u32[]{:S(2)}, u32[]{:S(2)}) collective-permute-start(bf16[256,1024]{1,0:T(8,128)(2,1)S(1)} %get-tuple-element.1510), channel_id=1, source_target_pairs={{0,177},{1,178},{2,179},{3,180},{4,181},{5,182},{6,183},{7,184},{8... | collective-permute-start | bytes 1572872 | tf_op jit(solution)/shard_map/while/body/eval_jaxpr/cond/branch_4_fun/cond/branch_3_fun/cond/branch_2_fun/ppermute | solution.py:77
  300.9 0.6 copy-start

commit v2 on v1

--- a/solution.py
+++ b/solution.py
@@ -11,30 +11,51 @@
 EPSILON = 1e-06
 ROUNDS = 3
 HALF = 128
-BRANCHES = (8, 4, 4)
 STAGES = ((1, 8), (8, 4), (32, 8))
 MESH = pl.DeviceIdType.MESH
 
-
-def shift_costs():
-    return np.array(COST, np.int32)
-
-
-COST = [112, 165, 217, 270, 217, 165, 151, 165, 178, 191, 217, 270, 230, 243, 256, 270, 256, 243, 230, 270, 217, 191, 178, 165, 151, 165, 217, 270, 217, 165, 161, 165, 168, 171, 217, 270, 217, 184, 187, 191, 194, 197, 217, 270, 230, 243, 256, 270, 256, 243, 230, 270, 233, 237, 240, 243, 247, 250, 253, 270, 260, 263, 266, 270, 273, 276, 279, 283, 286, 289, 292, 296, 299, 302, 306, 309, 312, 315, 319, 322, 325, 329, 332, 335, 338, 342, 345, 348, 352, 355, 358, 361, 365, 368, 371, 375, 378, 381, 384, 388, 391, 394, 397, 401, 404, 407, 411, 414, 417, 420, 424, 427, 430, 434, 437, 440, 443, 447, 450, 453, 457, 460, 463, 466, 470, 473, 476, 480]
-
-
-def schedule_kernel(plan_ref, cost_ref, out_ref):
+SHIFTS = (1, 2, 3, 4, 5, 6, 7, 8, 9, 10, 11, 12, 13, 14, 15, 16, 17, 18, 19, 20, 21, 22, 23, 24, 25, 26, 27, 28, 29, 30, 31, 32, 64, 96)
+WIDTH = 6
+COST = [156, 211, 216, 234, 232, 215, 210, 213, 220, 262, 270, 295, 292, 274, 280, 241, 258, 231, 242, 269, 253, 284, 240, 216, 223, 226, 239, 283, 249, 238, 234, 212, 369, 423, 428, 446, 444, 427, 422, 425, 433, 447, 454, 457, 468, 476, 456, 431, 439, 441, 449, 451, 464, 454, 450, 428, 435, 438, 451, 476, 461, 450, 447, 339, 495, 550, 555, 573, 571, 554, 549, 552, 559, 600, 609, 634, 631, 613, 619, 580, 597, 570, 581, 608, 592, 623, 579, 555, 562, 565, 578, 622, 588, 577, 573, 453, 609, 664, 669, 687, 685, 668, 663, 666, 673, 715, 723, 748, 745, 727, 734, 694, 711, 684, 695, 722, 706, 737, 693, 669, 676, 679, 692, 736, 702, 691, 687, 666]
+FIRST = [0, 2, 4, 6, 8, 10, 12, 14, 16, 18, 20, 22, 24, 26, 28, 30, 32, 34, 36, 38, 40, 42, 44, 46, 48, 50, 52, 54, 56, 58, 60, 62, 0, 2, 4, 6, 8, 10, 12, 14, 16, 34, 34, 34, 36, 40, 44, 46, 46, 46, 48, 50, 46, 46, 46, 46, 48, 50, 52, 58, 56, 58, 60, 64, 0, 2, 4, 6, 8, 10, 12, 14, 16, 18, 20, 22, 24, 26, 28, 30, 32, 34, 36, 38, 40, 42, 44, 46, 48, 50, 52, 54, 56, 58, 60, 66, 0, 2, 4, 6, 8, 10, 12, 14, 16, 18, 20, 22, 24, 26, 28, 30, 32, 34, 36, 38, 40, 42, 44, 46, 48, 50, 52, 54, 56, 58, 60, 62]
+SECOND = [-1, -1, -1, -1, -1, -1, -1, -1, -1, -1, -1, -1, -1, -1, -1, -1, -1, -1, -1, -1, -1, -1, -1, -1, -1, -1, -1, -1, -1, -1, -1, -1, 62, 62, 62, 62, 62, 62, 62, 62, 62, 46, 48, 50, 50, 48, 46, 46, 48, 50, 50, 50, 56, 58, 60, 62, 62, 62, 62, 58, 62, 62, 62, -1, 64, 64, 64, 64, 64, 64, 64, 64, 64, 64, 64, 64, 64, 64, 64, 64, 64, 64, 64, 64, 64, 64, 64, 64, 64, 64, 64, 64, 64, 64, 64, -1, 66, 66, 66, 66, 66, 66, 66, 66, 66, 66, 66, 66, 66, 66, 66, 66, 66, 66, 66, 66, 66, 66, 66, 66, 66, 66, 66, 66, 66, 66, 66, 66]
+
+
+def plan_kernel(plan_ref, table_ref, audio_ref, text_ref, held_ref, code_ref, count_ref, sems):
+    own = [
+        pltpu.make_async_copy(ref, held_ref.at[i], sems.at[i])
+        for i, ref in enumerate((audio_ref, text_ref))
+    ]
+    for copy in own:
+        copy.start()
     me = lax.axis_index("dp")
     offsets = [(plan_ref[0, r] - me) & 255 for r in range(ROUNDS)]
 
+    def entry(distance):
+        return jnp.maximum(jnp.minimum(distance, 256 - distance) - 1, 0)
+
     def cost(distance):
-        return cost_ref[jnp.maximum(jnp.minimum(distance, 256 - distance) - 1, 0)]
+        return table_ref[entry(distance)]
+
+    def write(at, transfer, source, target):
+        leaf = transfer >> 1
+        back = transfer & 1
+        high = lax.div(leaf, WIDTH)
+        code_ref[at] = (
+            high
+            | ((leaf - high * WIDTH) << 4)
+            | ((2 * source + back) << 8)
+            | ((2 * source + 1 - back) << 12)
+            | ((2 * target + back) << 16)
+            | ((2 * target + 1 - back) << 20)
+        )
 
     far = jnp.int32(1 << 28)
     best = [cost(s) for s in offsets]
     parent = [jnp.int32(0)] * ROUNDS
-    step_of = list(offsets)
+    away = list(offsets)
     done = [jnp.int32(0)] * ROUNDS
+    count = jnp.int32(0)
     for step in range(ROUNDS):
         keys = [jnp.where(done[j] == 1, far, best[j]) for j in range(ROUNDS)]
         first = (keys[0] <= keys[1]) & (keys[0] <= keys[2])
@@ -43,13 +64,14 @@
         def chosen(values):
             return jnp.where(pick == 0, values[0], jnp.where(pick == 1, values[1], values[2]))
 
-        distance = chosen(step_of)
+        distance = chosen(away)
         at = chosen(offsets)
-        wrapped = jnp.where(distance <= HALF, 0, 1)
-        out_ref[4 * step] = chosen(parent)
-        out_ref[4 * step + 1] = jnp.maximum(jnp.minimum(distance, 256 - distance) - 1, 0)
-        out_ref[4 * step + 2] = wrapped
-        out_ref[4 * step + 3] = 0
+        mirrored = jnp.where(distance <= HALF, 0, 1)
+        one = table_ref[HALF + entry(distance)]
+        two = table_ref[2 * HALF + entry(distance)]
+        write(count, one ^ mirrored, chosen(parent), step + 1)
+        write(count + 1, jnp.maximum(two, 0) ^ mirrored, jnp.int32(step + 1), step + 1)
+        count = count + jnp.where(two >= 0, 2, 1)
         for j in range(ROUNDS):
             done[j] = jnp.where(pick == j, 1, done[j])
             onward = (offsets[j] - at) & 255
@@ -57,36 +79,73 @@
             nearer = price < best[j]
             best[j] = jnp.where(nearer, price, best[j])
             parent[j] = jnp.where(nearer, step + 1, parent[j])
-            step_of[j] = jnp.where(nearer, onward, step_of[j])
-
-
-def make_schedule(plan):
+            away[j] = jnp.where(nearer, onward, away[j])
+    count_ref[0] = count
+    for copy in own:
+        copy.wait()
+
+
+def plan_transfers(audio, text, plan):
+    smem = pl.BlockSpec(memory_space=pltpu.SMEM)
+    anywhere = pl.BlockSpec(memory_space=pl.ANY)
     return pl.pallas_call(
-        schedule_kernel,
-        out_shape=jax.ShapeDtypeStruct((4 * ROUNDS,), jnp.int32),
-        in_specs=[pl.BlockSpec(memory_space=pltpu.SMEM)] * 2,
-        out_specs=pl.BlockSpec(memory_space=pltpu.SMEM),
-    )(plan, jnp.asarray(shift_costs()))
-
-
-def both_ways(distance, blocks):
-    ahead, back = blocks
-    peers = lax.axis_size("dp")
-    return (
-        lax.ppermute(ahead, "dp", [(i, (i + distance) % peers) for i in range(peers)]),
-        lax.ppermute(back, "dp", [(i, (i - distance) % peers) for i in range(peers)]),
-    )
-
-
-def exchange(distances, digits, widths, blocks):
-    if not widths:
-        return both_ways(distances[0], blocks)
-    count = len(distances) // widths[0]
-    branches = [
-        partial(exchange, distances[i * count : (i + 1) * count], digits[1:], widths[1:])
-        for i in range(widths[0])
+        plan_kernel,
+        out_shape=(
+            jax.ShapeDtypeStruct((2 * (ROUNDS + 1),) + audio.shape, audio.dtype),
+            jax.ShapeDtypeStruct((8,), jnp.int32),
+            jax.ShapeDtypeStruct((1,), jnp.int32),
+        ),
+        in_specs=[smem, smem, anywhere, anywhere],
+        out_specs=(anywhere, smem, smem),
+        scratch_shapes=[pltpu.SemaphoreType.DMA((2,))],
+    )(plan, jnp.asarray(np.array(COST + FIRST + SECOND, np.int32)), audio, text)
+
+
+def swap_kernel(distance, ahead_ref, back_ref, ahead_out, back_out, send_sem, recv_sem):
+    me = lax.axis_index("dp")
+    after = lax.rem(me + distance, 256)
+    before = lax.rem(me + 256 - distance, 256)
+    barrier = pltpu.get_barrier_semaphore()
+    for device in (after, before):
+        pl.semaphore_signal(barrier, inc=1, device_id=(device,), device_id_type=MESH)
+    pl.semaphore_wait(barrier, 2)
+    copies = [
+        pltpu.make_async_remote_copy(
+            src_ref=src,
+            dst_ref=dst,
+            send_sem=send_sem.at[i],
+            recv_sem=recv_sem.at[i],
+            device_id=(device,),
+            device_id_type=MESH,
+        )
+        for i, (src, dst, device) in enumerate(
+            ((ahead_ref, ahead_out, after), (back_ref, back_out, before))
+        )
     ]
-    return lax.switch(digits[0], branches, blocks)
+    for copy in copies:
+        copy.start()
+    for copy in copies:
+        copy.wait()
+
+
+def both_ways(leaf, blocks):
+    anywhere = pl.BlockSpec(memory_space=pl.ANY)
+    return pl.pallas_call(
+        partial(swap_kernel, SHIFTS[leaf]),
+        out_shape=[jax.ShapeDtypeStruct(b.shape, b.dtype) for b in blocks],
+        in_specs=[anywhere] * 2,
+        out_specs=[anywhere] * 2,
+        scratch_shapes=[pltpu.SemaphoreType.DMA((2,)), pltpu.SemaphoreType.DMA((2,))],
+        compiler_params=pltpu.CompilerParams(collective_id=1 + leaf, has_side_effects=True),
+    )(*blocks)
+
+
+def exchange(high, low, blocks):
+    def group(i, blocks):
+        leaves = range(i * WIDTH, min((i + 1) * WIDTH, len(SHIFTS)))
+        return lax.switch(low, [partial(both_ways, leaf) for leaf in leaves], blocks)
+
+    return lax.switch(high, [partial(group, i) for i in range(-(-len(SHIFTS) // WIDTH))], blocks)
 
 
 def unit_rows(raw):
@@ -108,21 +167,21 @@
 def loss_kernel(scale_ref, bias_ref, held_ref, row_ref, ga_ref, gt_ref, tot_ref):
     scale = jnp.exp(jnp.full((1, 1), scale_ref[0], jnp.float32))
     bias = bias_ref[0]
-    n = held_ref.shape[2]
+    n = held_ref.shape[1]
     rows = lax.broadcasted_iota(jnp.int32, (n, n), 0)
     cols = lax.broadcasted_iota(jnp.int32, (n, n), 1)
     eye = (rows == cols).astype(jnp.float32)
 
-    audio_wide, audio_recip, audio_unit = unit_rows(held_ref[0, 0])
-    text_wide, text_recip, text_unit = unit_rows(held_ref[0, 1])
+    audio_wide, audio_recip, audio_unit = unit_rows(held_ref[0])
+    text_wide, text_recip, text_unit = unit_rows(held_ref[1])
     losses_sum = jnp.zeros((n, n), jnp.float32)
     slopes_sum = jnp.zeros((n, n), jnp.float32)
     scaled_sum = jnp.zeros((n, n), jnp.float32)
     audio_grad = jnp.zeros(audio_wide.shape, jnp.float32)
     text_grad = jnp.zeros(text_wide.shape, jnp.float32)
     for slot in range(ROUNDS + 1):
-        far_text = text_unit if slot == 0 else unit_rows(held_ref[slot, 1])[2]
-        far_audio = audio_unit if slot == 0 else unit_rows(held_ref[slot, 0])[2]
+        far_text = text_unit if slot == 0 else unit_rows(held_ref[2 * slot + 1])[2]
+        far_audio = audio_unit if slot == 0 else unit_rows(held_ref[2 * slot])[2]
         scaled = scale * dot_t(audio_unit, far_text)
         logits = scaled + bias
         small = jnp.exp(-jnp.abs(logits))
@@ -158,7 +217,7 @@
 
 
 def loss_and_grads(log_scale, bias, held):
-    n, d = held.shape[2:]
+    n, d = held.shape[1:]
     vmem = pl.BlockSpec(memory_space=pltpu.VMEM)
     smem = pl.BlockSpec(memory_space=pltpu.SMEM)
     return pl.pallas_call(
@@ -239,24 +298,19 @@
 
 
 def local(audio, text, log_scale, bias, plan):
-    n, d = audio.shape
+    n = audio.shape[0]
     player_count = lax.axis_size("dp")
-    steps = make_schedule(plan)
-    held = jnp.zeros((ROUNDS + 1, 2, n, d), audio.dtype)
-    held = held.at[0, 0].set(audio).at[0, 1].set(text)
+    held, codes, count = plan_transfers(audio, text, plan)
 
     def fetch(step, held):
-        parent, branch, wrapped = [steps[4 * step + i] for i in range(3)]
-        blocks = (held[parent, wrapped], held[parent, 1 - wrapped])
-        digits = []
-        for width in reversed(BRANCHES):
-            digits.insert(0, lax.rem(branch, width))
-            branch = lax.div(branch, width)
-        ahead, back = exchange(list(range(1, HALF + 1)), digits, BRANCHES, blocks)
-        held = held.at[step + 1, wrapped].set(ahead)
-        return held.at[step + 1, 1 - wrapped].set(back)
-
-    held = lax.fori_loop(0, ROUNDS, fetch, held)
+        code = lax.dynamic_index_in_dim(codes, step, keepdims=False)
+        high, low, *at = [(code >> (4 * i)) & 15 for i in range(6)]
+        blocks = [lax.dynamic_index_in_dim(held, i, keepdims=False) for i in at[:2]]
+        for block, i in zip(exchange(high, low, blocks), at[2:]):
+            held = lax.dynamic_update_index_in_dim(held, block, i, 0)
+        return held
+
+    held = lax.fori_loop(0, count[0], fetch, held)
     row_loss, grad_audio, grad_text, parts = loss_and_grads(log_scale, bias, held)
     stats = all_stats(parts, float((ROUNDS + 1) * n * n * player_count))
     return (row_loss.reshape(n), grad_audio, grad_text, stats)

time: 340 us -> 248 us (0.73)
  Pallas kernels: 43.5 us -> 181 us
  loops' own time: 153 us -> 28.8 us
  waiting for transfers between devices: 58.4 us -> 0 us
  starting transfers between devices: 47.6 us -> 0 us
  local copies, waits for them, and re-layouts: 13.9 us -> 35.6 us
  other arithmetic: 19.3 us -> 0 us
    pallas_call x1 -> x7, Pallas kernels: 1.34 us -> 147 us  [the longest x6 113 us: both_ways(): pl.pallas_call(partial(swap_kernel, SHIFTS[leaf]), out_shape=[jax.ShapeDt...]
    another operation x10 -> x13, loops' own time: 153 us -> 28.8 us  [the longest x1 24.4 us: local(): held = lax.fori_loop(0, count[0], fetch, held)]
    ppermute x6 -> x0, waiting for transfers between devices: 58.4 us -> none  [the longest x3 36.7 us: both_ways(): lax.ppermute(ahead, 'dp', [(i, (i + distance) % peers) for i in range(pee...]
    ppermute x6 -> x0, starting transfers between devices: 47.6 us -> none  [the longest x3 34.4 us: both_ways(): lax.ppermute(back, 'dp', [(i, (i - distance) % peers) for i in range(peer...]
    dynamic_update_slice x0 -> x12, local copies, waits for them, and re-layouts: none -> 22.6 us  [fetch(): held = lax.dynamic_update_index_in_dim(held, block, i, 0)]
    scatter x6 -> x0, other arithmetic: 17.2 us -> none  [the longest x3 8.59 us: fetch(): held = held.at[step + 1, wrapped].set(ahead)]
    pallas_call x1, Pallas kernels: 34.5 us -> 26.1 us  [all_stats(): pl.pallas_call(partial(stats_kernel, denominator), out_shape=jax.ShapeDty...]
    scatter x2 -> x0, local copies, waits for them, and re-layouts: 5.74 us -> none  [local(): held = held.at[0, 0].set(audio).at[0, 1].set(text)]
  transfers between devices with their start and end apart: 6 -> 0, of which waited for: 4 -> 0; matrix products, arithmetic and copies ran while one was open for 0% -> 0% of each run, Pallas kernels for 0% -> 0%
where the time goes in v2:
time: 248 us; the launch traced here: 247 us
  Pallas kernels  181 us (73%)
  local copies, waits for them, and re-layouts  35.6 us (14%)
  loops' own time  28.8 us (12%)
    pallas_call x6, Pallas kernels, both_ways(): pl.pallas_call(partial(swap_kernel, SHIFTS[leaf]), out_shape=[jax.ShapeDt...  113 us
    pallas_call x1, Pallas kernels, plan_transfers(): pl.pallas_call(plan_kernel, out_shape=(jax.ShapeDtypeStruct((2 * (ROUNDS...  34.2 us
    pallas_call x1, Pallas kernels, all_stats(): pl.pallas_call(partial(stats_kernel, denominator), out_shape=jax.ShapeDty...  26.1 us
    another operation x1, loops' own time, local(): held = lax.fori_loop(0, count[0], fetch, held)  24.4 us
    dynamic_update_slice x12, local copies, waits for them, and re-layouts, fetch(): held = lax.dynamic_update_index_in_dim(held, block, i, 0)  22.6 us
    pallas_call x1, Pallas kernels, loss_and_grads(): pl.pallas_call(loss_kernel, out_shape=(jax.ShapeDtypeStruct((1, n), jnp.f...  7.67 us
    squeeze x6, local copies, waits for them, and re-layouts, fetch(): blocks = [lax.dynamic_index_in_dim(held, i, keepdims=False) for i in at[:2]]  7.66 us

profile of v2, /device:TPU:1, one launch (start us, length us, event | category | flops | bytes accessed | tf_op | source)
XLA Modules:
  0.0 247.0 jit_solution(15592590918338221287)
XLA Ops:
  0.6 34.2 %shard_map.93 = (bf16[8,256,1024]{2,1,0:T(8,128)(2,1)}, s32[8]{0:T(128)S(1)}, s32[1]{0:T(128)}) custom-call(s32[1,3]{1,0:T(1,128)} %plan_ref.1, s32[384]{0:T(512)} %constant.133.clone.table_ref, bf16[256,1024]{1,0:T(8,128)(2,1)} %audio_ref.1, bf16[256,1024]{1,0:T(8,128)(2,1)} %text_ref.1), custom_call_target="tpu_custom_call" | custom-call | tf_op jit(solution)/shard_map/pallas_call | solution.py:91
  34.8 175.3 %while.10 = (s32[]{:T(128)}, bf16[8,256,1024]{2,1,0:T(8,128)(2,1)}, s32[]{:T(128)}, s32[8]{0:T(128)S(1)}, s32[]{:T(128)}, /*index=5*/s32[]{:T(128)}, s32[]{:T(12...) while((s32[]{:T(128)}, bf16[8,256,1024]{2,1,0:T(8,128)(2,1)}, s32[]{:T(128)}, ...), condition=%wide.region_41.42_spmd, body=%wide.region_0.41_spmd.sunk | while | flops 31 | bytes 4194867 | solution.py:313
  35.5 0.6 dynamic_slice.92
  38.0 22.8 %conditional.8 = ((bf16[1,256,1024]{2,1,0:T(8,128)(2,1)}, bf16[1,256,1024]{2,1,0:T(8,128)(2,1)})) conditional(s32[]{:T(128)} %clamp.28, (s32[]{:T(128)}, s32[]{:T(128)}, bf16[8,256,1024]{2,1,0:T(8,128)(2,1)}, s32[]{:T(128)}) %tuple.312, (s32[]{:T(128)}, s32[]{:T(128)}, bf16[8,256,1024]{2,1,0:T(8,128)(2,1)}, ...), branch_computations={%region_1.7_spmd, %region_8.14_spmd, %region_15.21_spmd, %region_2... | conditional | flops 9 | bytes 2097308 | solution.py:148
  38.0 1.3 dynamic-slice_bitcast_fusion.2
  40.0 20.8 %conditional.1 = (bf16[1,256,1024]{2,1,0:T(8,128)(2,1)}, bf16[1,256,1024]{2,1,0:T(8,128)(2,1)}) conditional(s32[]{:T(128)} %clamp.21, (bf16[256,1024]{1,0:T(8,128)(2,1)S(1)}, bf16[256,1024]{1,0:T(8,128)(2,1)S(1)}) %tuple.235, (bf16[256,1024]{1,0:T(8,128)(2,1)S(1)}, bf16[256,1024]{1,0:T(8,128)(2,1)S(1)}) %tuple.235, ...), branch_computations={%region_9.8_spmd, %region_10.9_spmd, %region_11.10_spmd, %region_1... | conditional | bytes 16 | solution.py:146
  40.0 20.8 %branch_1_fun.7 = (bf16[256,1024]{1,0:T(8,128)(2,1)}, bf16[256,1024]{1,0:T(8,128)(2,1)}) custom-call(bf16[256,1024]{1,0:T(8,128)(2,1)S(1)} %get-tuple-element.656.ahead_ref, bf16[256,1024]{1,0:T(8,128)(2,1)S(1)} %get-tuple-element.657.back_ref), custom_call_target="tpu_custom_call" | custom-call | tf_op jit(solution)/shard_map/while/body/cond/branch_1_fun/cond/branch_1_fun/pallas_call | solution.py:133
  61.5 1.9 constant_dynamic-update-slice_fusion.4
  64.0 1.9 constant_dynamic-update-slice_fusion.5
  66.6 0.6 dynamic_slice.92
  69.1 15.4 %conditional.8 = ((bf16[1,256,1024]{2,1,0:T(8,128)(2,1)}, bf16[1,256,1024]{2,1,0:T(8,128)(2,1)})) conditional(s32[]{:T(128)} %clamp.28, (s32[]{:T(128)}, s32[]{:T(128)}, bf16[8,256,1024]{2,1,0:T(8,128)(2,1)}, s32[]{:T(128)}) %tuple.312, (s32[]{:T(128)}, s32[]{:T(128)}, bf16[8,256,1024]{2,1,0:T(8,128)(2,1)}, ...), branch_computations={%region_1.7_spmd, %region_8.14_spmd, %region_15.21_spmd, %region_2... | conditional | flops 9 | bytes 2097308 | solution.py:148
  69.1 1.3 dynamic-slice_bitcast_fusion.10
  71.1 13.4 %conditional.5 = (bf16[1,256,1024]{2,1,0:T(8,128)(2,1)}, bf16[1,256,1024]{2,1,0:T(8,128)(2,1)}) conditional(s32[]{:T(128)} %clamp.25, (bf16[256,1024]{1,0:T(8,128)(2,1)S(1)}, bf16[256,1024]{1,0:T(8,128)(2,1)S(1)}) %tuple.281, (bf16[256,1024]{1,0:T(8,128)(2,1)S(1)}, bf16[256,1024]{1,0:T(8,128)(2,1)S(1)}) %tuple.281, ...), branch_computations={%region_37.36_spmd, %region_38.37_spmd, %region_39.38_spmd, %regio... | conditional | bytes 16 | solution.py:146
  71.1 13.4 %branch_1_fun.11 = (bf16[256,1024]{1,0:T(8,128)(2,1)}, bf16[256,1024]{1,0:T(8,128)(2,1)}) custom-call(bf16[256,1024]{1,0:T(8,128)(2,1)S(1)} %get-tuple-element.768.ahead_ref, bf16[256,1024]{1,0:T(8,128)(2,1)S(1)} %get-tuple-element.769.back_ref), custom_call_target="tpu_custom_call" | custom-call | tf_op jit(solution)/shard_map/while/body/cond/branch_5_fun/cond/branch_1_fun/pallas_call | solution.py:133
  85.1 1.9 constant_dynamic-update-slice_fusion.4
  87.7 1.9 constant_dynamic-update-slice_fusion.5
  90.2 0.6 dynamic_slice.92
  92.8 28.4 %conditional.8 = ((bf16[1,256,1024]{2,1,0:T(8,128)(2,1)}, bf16[1,256,1024]{2,1,0:T(8,128)(2,1)})) conditional(s32[]{:T(128)} %clamp.28, (s32[]{:T(128)}, s32[]{:T(128)}, bf16[8,256,1024]{2,1,0:T(8,128)(2,1)}, s32[]{:T(128)}) %tuple.312, (s32[]{:T(128)}, s32[]{:T(128)}, bf16[8,256,1024]{2,1,0:T(8,128)(2,1)}, ...), branch_computations={%region_1.7_spmd, %region_8.14_spmd, %region_15.21_spmd, %region_2... | conditional | flops 9 | bytes 2097308 | solution.py:148
  92.8 1.3 dynamic-slice_bitcast_fusion.4
  94.7 26.4 %conditional.2 = (bf16[1,256,1024]{2,1,0:T(8,128)(2,1)}, bf16[1,256,1024]{2,1,0:T(8,128)(2,1)}) conditional(s32[]{:T(128)} %clamp.22, (bf16[256,1024]{1,0:T(8,128)(2,1)S(1)}, bf16[256,1024]{1,0:T(8,128)(2,1)S(1)}) %tuple.247, (bf16[256,1024]{1,0:T(8,128)(2,1)S(1)}, bf16[256,1024]{1,0:T(8,128)(2,1)S(1)}) %tuple.247, ...), branch_computations={%region_16.15_spmd, %region_17.16_spmd, %region_18.17_spmd, %regio... | conditional | bytes 16 | solution.py:146
  94.8 26.3 %branch_5_fun.7 = (bf16[256,1024]{1,0:T(8,128)(2,1)}, bf16[256,1024]{1,0:T(8,128)(2,1)}) custom-call(bf16[256,1024]{1,0:T(8,128)(2,1)S(1)} %get-tuple-element.700.ahead_ref, bf16[256,1024]{1,0:T(8,128)(2,1)S(1)} %get-tuple-element.701.back_ref), custom_call_target="tpu_custom_call" | custom-call | tf_op jit(solution)/shard_map/while/body/cond/branch_2_fun/cond/branch_5_fun/pallas_call | solution.py:133
  121.8 1.9 constant_dynamic-update-slice_fusion.4
  124.3 1.9 constant_dynamic-update-slice_fusion.5
  126.9 0.6 dynamic_slice.92
  129.4 20.2 %conditional.8 = ((bf16[1,256,1024]{2,1,0:T(8,128)(2,1)}, bf16[1,256,1024]{2,1,0:T(8,128)(2,1)})) conditional(s32[]{:T(128)} %clamp.28, (s32[]{:T(128)}, s32[]{:T(128)}, bf16[8,256,1024]{2,1,0:T(8,128)(2,1)}, s32[]{:T(128)}) %tuple.312, (s32[]{:T(128)}, s32[]{:T(128)}, bf16[8,256,1024]{2,1,0:T(8,128)(2,1)}, ...), branch_computations={%region_1.7_spmd, %region_8.14_spmd, %region_15.21_spmd, %region_2... | conditional | flops 9 | bytes 2097308 | solution.py:148
  129.4 1.3 dynamic-slice_bitcast_fusion.8
  131.4 18.2 %conditional.4 = (bf16[1,256,1024]{2,1,0:T(8,128)(2,1)}, bf16[1,256,1024]{2,1,0:T(8,128)(2,1)}) conditional(s32[]{:T(128)} %clamp.24, (bf16[256,1024]{1,0:T(8,128)(2,1)S(1)}, bf16[256,1024]{1,0:T(8,128)(2,1)S(1)}) %tuple.271, (bf16[256,1024]{1,0:T(8,128)(2,1)S(1)}, bf16[256,1024]{1,0:T(8,128)(2,1)S(1)}) %tuple.271, ...), branch_computations={%region_30.29_spmd, %region_31.30_spmd, %region_32.31_spmd, %regio... | conditional | bytes 16 | solution.py:146
  131.4 18.2 %branch_0_fun.10 = (bf16[256,1024]{1,0:T(8,128)(2,1)}, bf16[256,1024]{1,0:T(8,128)(2,1)}) custom-call(bf16[256,1024]{1,0:T(8,128)(2,1)S(1)} %get-tuple-element.736.ahead_ref, bf16[256,1024]{1,0:T(8,128)(2,1)S(1)} %get-tuple-element.737.back_ref), custom_call_target="tpu_custom_call" | custom-call | tf_op jit(solution)/shard_map/while/body/cond/branch_4_fun/cond/branch_0_fun/pallas_call | solution.py:133
  150.2 1.9 constant_dynamic-update-slice_fusion.4
  152.7 1.9 constant_dynamic-update-slice_fusion.5
  155.3 0.6 dynamic_slice.92
  157.8 18.4 %conditional.8 = ((bf16[1,256,1024]{2,1,0:T(8,128)(2,1)}, bf16[1,256,1024]{2,1,0:T(8,128)(2,1)})) conditional(s32[]{:T(128)} %clamp.28, (s32[]{:T(128)}, s32[]{:T(128)}, bf16[8,256,1024]{2,1,0:T(8,128)(2,1)}, s32[]{:T(128)}) %tuple.312, (s32[]{:T(128)}, s32[]{:T(128)}, bf16[8,256,1024]{2,1,0:T(8,128)(2,1)}, ...), branch_computations={%region_1.7_spmd, %region_8.14_spmd, %region_15.21_spmd, %region_2... | conditional | flops 9 | bytes 2097308 | solution.py:148
  157.9 1.3 dynamic-slice_bitcast_fusion.8
  159.8 16.4 %conditional.4 = (bf16[1,256,1024]{2,1,0:T(8,128)(2,1)}, bf16[1,256,1024]{2,1,0:T(8,128)(2,1)}) conditional(s32[]{:T(128)} %clamp.24, (bf16[256,1024]{1,0:T(8,128)(2,1)S(1)}, bf16[256,1024]{1,0:T(8,128)(2,1)S(1)}) %tuple.271, (bf16[256,1024]{1,0:T(8,128)(2,1)S(1)}, bf16[256,1024]{1,0:T(8,128)(2,1)S(1)}) %tuple.271, ...), branch_computations={%region_30.29_spmd, %region_31.30_spmd, %region_32.31_spmd, %regio... | conditional | bytes 16 | solution.py:146
  159.8 16.4 %branch_1_fun.10 = (bf16[256,1024]{1,0:T(8,128)(2,1)}, bf16[256,1024]{1,0:T(8,128)(2,1)}) custom-call(bf16[256,1024]{1,0:T(8,128)(2,1)S(1)} %get-tuple-element.740.ahead_ref, bf16[256,1024]{1,0:T(8,128)(2,1)S(1)} %get-tuple-element.741.back_ref), custom_call_target="tpu_custom_call" | custom-call | tf_op jit(solution)/shard_map/while/body/cond/branch_4_fun/cond/branch_1_fun/pallas_call | solution.py:133
  176.9 1.9 constant_dynamic-update-slice_fusion.4
  179.4 1.9 constant_dynamic-update-slice_fusion.5
  182.0 0.6 dynamic_slice.92
  184.5 19.7 %conditional.8 = ((bf16[1,256,1024]{2,1,0:T(8,128)(2,1)}, bf16[1,256,1024]{2,1,0:T(8,128)(2,1)})) conditional(s32[]{:T(128)} %clamp.28, (s32[]{:T(128)}, s32[]{:T(128)}, bf16[8,256,1024]{2,1,0:T(8,128)(2,1)}, s32[]{:T(128)}) %tuple.312, (s32[]{:T(128)}, s32[]{:T(128)}, bf16[8,256,1024]{2,1,0:T(8,128)(2,1)}, ...), branch_computations={%region_1.7_spmd, %region_8.14_spmd, %region_15.21_spmd, %region_2... | conditional | flops 9 | bytes 2097308 | solution.py:148
  184.5 1.3 dynamic-slice_bitcast_fusion.10
  186.5 17.7 %conditional.5 = (bf16[1,256,1024]{2,1,0:T(8,128)(2,1)}, bf16[1,256,1024]{2,1,0:T(8,128)(2,1)}) conditional(s32[]{:T(128)} %clamp.25, (bf16[256,1024]{1,0:T(8,128)(2,1)S(1)}, bf16[256,1024]{1,0:T(8,128)(2,1)S(1)}) %tuple.281, (bf16[256,1024]{1,0:T(8,128)(2,1)S(1)}, bf16[256,1024]{1,0:T(8,128)(2,1)S(1)}) %tuple.281, ...), branch_computations={%region_37.36_spmd, %region_38.37_spmd, %region_39.38_spmd, %regio... | conditional | bytes 16 | solution.py:146
  186.5 17.7 %branch_2_fun.11 = (bf16[256,1024]{1,0:T(8,128)(2,1)}, bf16[256,1024]{1,0:T(8,128)(2,1)}) custom-call(bf16[256,1024]{1,0:T(8,128)(2,1)S(1)} %get-tuple-element.772.ahead_ref, bf16[256,1024]{1,0:T(8,128)(2,1)S(1)} %get-tuple-element.773.back_ref), custom_call_target="tpu_custom_call" | custom-call | tf_op jit(solution)/shard_map/while/body/cond/branch_5_fun/cond/branch_2_fun/pallas_call | solution.py:133
  204.8 1.9 constant_dynamic-update-slice_fusion.4
  207.4 1.9 constant_dynamic-update-slice_fusion.5
  211.4 7.7 %shard_map.94 = (f32[1,256]{1,0:T(1,128)}, f32[256,1024]{1,0:T(8,128)}, f32[256,1024]{1,0:T(8,128)}, f32[8,128]{1,0:T(8,128)S(1)}) custom-call(f32[1]{0:T(128)S(6)} %copy.98.scale_ref, f32[1]{0:T(128)S(6)} %copy.99.bias_ref, bf16[8,256,1024]{2,1,0:T(8,128)(2,1)} %get-tuple-element.807.held_ref), custom_call_target="tpu_custom_call" | custom-call | tf_op jit(solution)/shard_map/pallas_call | solution.py:223
  219.0 0.6 copy-done
  219.6 26.1 %shard_map.95 = f32[8,128]{1,0:T(8,128)} custom-call(f32[8,128]{1,0:T(8,128)} %copy-done), custom_call_target="tpu_custom_call" | custom-call | tf_op jit(solution)/shard_map/pallas_call | solution.py:290
  245.7 1.3 slice_reduce_fusion
  (1 shorter events, 0.0 us)
Async XLA Ops:
  219.0 0.6 copy-start

commit v3 on v2

--- a/solution.py
+++ b/solution.py
@@ -13,15 +13,15 @@
 HALF = 128
 STAGES = ((1, 8), (8, 4), (32, 8))
 MESH = pl.DeviceIdType.MESH
-
-SHIFTS = (1, 2, 3, 4, 5, 6, 7, 8, 9, 10, 11, 12, 13, 14, 15, 16, 17, 18, 19, 20, 21, 22, 23, 24, 25, 26, 27, 28, 29, 30, 31, 32, 64, 96)
-WIDTH = 6
-COST = [156, 211, 216, 234, 232, 215, 210, 213, 220, 262, 270, 295, 292, 274, 280, 241, 258, 231, 242, 269, 253, 284, 240, 216, 223, 226, 239, 283, 249, 238, 234, 212, 369, 423, 428, 446, 444, 427, 422, 425, 433, 447, 454, 457, 468, 476, 456, 431, 439, 441, 449, 451, 464, 454, 450, 428, 435, 438, 451, 476, 461, 450, 447, 339, 495, 550, 555, 573, 571, 554, 549, 552, 559, 600, 609, 634, 631, 613, 619, 580, 597, 570, 581, 608, 592, 623, 579, 555, 562, 565, 578, 622, 588, 577, 573, 453, 609, 664, 669, 687, 685, 668, 663, 666, 673, 715, 723, 748, 745, 727, 734, 694, 711, 684, 695, 722, 706, 737, 693, 669, 676, 679, 692, 736, 702, 691, 687, 666]
-FIRST = [0, 2, 4, 6, 8, 10, 12, 14, 16, 18, 20, 22, 24, 26, 28, 30, 32, 34, 36, 38, 40, 42, 44, 46, 48, 50, 52, 54, 56, 58, 60, 62, 0, 2, 4, 6, 8, 10, 12, 14, 16, 34, 34, 34, 36, 40, 44, 46, 46, 46, 48, 50, 46, 46, 46, 46, 48, 50, 52, 58, 56, 58, 60, 64, 0, 2, 4, 6, 8, 10, 12, 14, 16, 18, 20, 22, 24, 26, 28, 30, 32, 34, 36, 38, 40, 42, 44, 46, 48, 50, 52, 54, 56, 58, 60, 66, 0, 2, 4, 6, 8, 10, 12, 14, 16, 18, 20, 22, 24, 26, 28, 30, 32, 34, 36, 38, 40, 42, 44, 46, 48, 50, 52, 54, 56, 58, 60, 62]
-SECOND = [-1, -1, -1, -1, -1, -1, -1, -1, -1, -1, -1, -1, -1, -1, -1, -1, -1, -1, -1, -1, -1, -1, -1, -1, -1, -1, -1, -1, -1, -1, -1, -1, 62, 62, 62, 62, 62, 62, 62, 62, 62, 46, 48, 50, 50, 48, 46, 46, 48, 50, 50, 50, 56, 58, 60, 62, 62, 62, 62, 58, 62, 62, 62, -1, 64, 64, 64, 64, 64, 64, 64, 64, 64, 64, 64, 64, 64, 64, 64, 64, 64, 64, 64, 64, 64, 64, 64, 64, 64, 64, 64, 64, 64, 64, 64, -1, 66, 66, 66, 66, 66, 66, 66, 66, 66, 66, 66, 66, 66, 66, 66, 66, 66, 66, 66, 66, 66, 66, 66, 66, 66, 66, 66, 66, 66, 66, 66, 66]
-
-
-def plan_kernel(plan_ref, table_ref, audio_ref, text_ref, held_ref, code_ref, count_ref, sems):
+MIB = 1024 * 1024
+
+SHIFTS = (1, 2, 3, 4, 6, 7, 9, 10, 11, 14, 15, 16, 17, 18, 19, 20, 21, 23, 24, 26, 27, 29, 30, 32, 33, 40, 46, 57, 59, 63, 64, 65, 73, 91, 128)
+COST = [156, 211, 216, 234, 371, 215, 210, 366, 220, 262, 270, 426, 424, 274, 280, 241, 258, 231, 242, 269, 253, 397, 240, 216, 372, 226, 239, 395, 249, 238, 369, 212, 271, 423, 428, 446, 448, 427, 422, 335, 433, 447, 458, 457, 468, 359, 456, 431, 466, 441, 454, 451, 464, 454, 453, 428, 347, 438, 363, 476, 461, 450, 358, 339, 388, 541, 555, 573, 572, 554, 549, 547, 462, 600, 579, 590, 594, 571, 599, 580, 563, 570, 573, 586, 589, 596, 573, 555, 560, 565, 477, 606, 588, 577, 570, 551, 601, 659, 688, 697, 708, 695, 693, 674, 674, 733, 718, 735, 708, 698, 728, 711, 750, 695, 693, 711, 703, 716, 690, 705, 679, 684, 689, 703, 685, 680, 626, 469]
+FIRST = [0, 2, 4, 6, 1, 8, 10, 0, 12, 14, 16, 0, 8, 18, 20, 22, 24, 26, 28, 30, 32, 1, 34, 36, 0, 38, 40, 0, 42, 44, 1, 46, 48, 2, 4, 6, 10, 8, 10, 50, 12, 26, 28, 26, 28, 52, 34, 36, 34, 36, 36, 38, 36, 36, 34, 36, 54, 38, 56, 44, 42, 44, 58, 60, 62, 48, 4, 6, 8, 8, 10, 46, 64, 14, 26, 28, 26, 46, 22, 22, 36, 26, 38, 40, 38, 42, 36, 36, 46, 38, 66, 42, 42, 44, 46, 46, 46, 48, 38, 12, 41, 39, 50, 50, 46, 48, 22, 24, 26, 52, 25, 23, 21, 54, 36, 54, 38, 40, 13, 54, 11, 9, 46, 7, 5, 3, 1, 68]
+SECOND = [-1, -1, -1, -1, 8, -1, -1, 10, -1, -1, -1, 16, 10, -1, -1, -1, -1, -1, -1, -1, -1, 34, -1, -1, 36, -1, -1, 40, -1, -1, 46, -1, -1, 46, 46, 46, 44, 46, 46, -1, 46, 36, 36, 38, 38, -1, 36, 36, 38, 38, 40, 38, 42, 44, 46, 46, -1, 46, -1, 44, 46, 46, -1, -1, -1, 48, 60, 60, 58, 60, 60, 50, -1, 60, 54, 54, 56, 52, 58, 60, 54, 60, 54, 54, 56, 54, 58, 60, 54, 60, -1, 58, 60, 60, 58, 60, 62, 62, 64, 66, 68, 68, 58, 60, 64, 64, 66, 66, 66, 60, 68, 68, 68, 54, 66, 56, 66, 66, 68, 58, 68, 68, 66, 68, 68, 68, 68, -1]
+
+
+def plan_kernel(plan_ref, table_ref, audio_ref, text_ref, held_ref, pair_ref, code_ref, leaf_ref, sems):
     own = [
         pltpu.make_async_copy(ref, held_ref.at[i], sems.at[i])
         for i, ref in enumerate((audio_ref, text_ref))
@@ -38,12 +38,9 @@
         return table_ref[entry(distance)]
 
     def write(at, transfer, source, target):
-        leaf = transfer >> 1
         back = transfer & 1
-        high = lax.div(leaf, WIDTH)
         code_ref[at] = (
-            high
-            | ((leaf - high * WIDTH) << 4)
+            (transfer >> 1)
             | ((2 * source + back) << 8)
             | ((2 * source + 1 - back) << 12)
             | ((2 * target + back) << 16)
@@ -80,47 +77,110 @@
             best[j] = jnp.where(nearer, price, best[j])
             parent[j] = jnp.where(nearer, step + 1, parent[j])
             away[j] = jnp.where(nearer, onward, away[j])
-    count_ref[0] = count
+    code_ref[count] = -1
+    code_ref[7] = -1
+    code = code_ref[0]
+    leaf_ref[0] = code & 255
+    backwards = ((code >> 8) & 1) == 1
+    audio, text = audio_ref[...], text_ref[...]
+    pair_ref[0] = jnp.where(backwards, text, audio)
+    pair_ref[1] = jnp.where(backwards, audio, text)
     for copy in own:
         copy.wait()
 
 
 def plan_transfers(audio, text, plan):
     smem = pl.BlockSpec(memory_space=pltpu.SMEM)
-    anywhere = pl.BlockSpec(memory_space=pl.ANY)
+    vmem = pl.BlockSpec(memory_space=pltpu.VMEM)
     return pl.pallas_call(
         plan_kernel,
         out_shape=(
             jax.ShapeDtypeStruct((2 * (ROUNDS + 1),) + audio.shape, audio.dtype),
+            jax.ShapeDtypeStruct((2,) + audio.shape, audio.dtype),
             jax.ShapeDtypeStruct((8,), jnp.int32),
             jax.ShapeDtypeStruct((1,), jnp.int32),
         ),
-        in_specs=[smem, smem, anywhere, anywhere],
-        out_specs=(anywhere, smem, smem),
+        in_specs=[smem, smem, vmem, vmem],
+        out_specs=(pl.BlockSpec(memory_space=pl.ANY), vmem, smem, smem),
         scratch_shapes=[pltpu.SemaphoreType.DMA((2,))],
+        compiler_params=pltpu.CompilerParams(vmem_limit_bytes=16 * MIB),
     )(plan, jnp.asarray(np.array(COST + FIRST + SECOND, np.int32)), audio, text)
 
 
-def swap_kernel(distance, ahead_ref, back_ref, ahead_out, back_out, send_sem, recv_sem):
+def store_kernel(held_in, landed_ref, code_in, held_ref, pair_ref, code_ref, leaf_ref, sems):
+    codes = [code_in[i] for i in range(8)]
+    targets = [(codes[0] >> 16) & 7, (codes[0] >> 20) & 7]
+    stores = [
+        pltpu.make_async_copy(landed_ref.at[i], held_ref.at[targets[i]], sems.at[i])
+        for i in range(2)
+    ]
+    for copy in stores:
+        copy.start()
+    for i in range(7):
+        code_ref[i] = codes[i + 1]
+    code_ref[7] = -1
+    leaf_ref[0] = jnp.where(codes[1] < 0, -1, codes[1] & 255)
+    sources = [(codes[1] >> 8) & 7, (codes[1] >> 12) & 7]
+    fresh = (sources[0] >> 1) == (targets[0] >> 1)
+
+    @pl.when(fresh)
+    def _():
+        same = sources[0] == targets[0]
+        first, second = landed_ref[0], landed_ref[1]
+        pair_ref[0] = jnp.where(same, first, second)
+        pair_ref[1] = jnp.where(same, second, first)
+
+    @pl.when(jnp.logical_not(fresh) & (codes[1] >= 0))
+    def _():
+        loads = [
+            pltpu.make_async_copy(held_ref.at[sources[i]], pair_ref.at[i], sems.at[2 + i])
+            for i in range(2)
+        ]
+        for copy in loads:
+            copy.start()
+        for copy in loads:
+            copy.wait()
+
+    for copy in stores:
+        copy.wait()
+
+
+def store_landed(held, landed, codes):
+    smem = pl.BlockSpec(memory_space=pltpu.SMEM)
+    vmem = pl.BlockSpec(memory_space=pltpu.VMEM)
+    return pl.pallas_call(
+        store_kernel,
+        out_shape=(
+            jax.ShapeDtypeStruct(held.shape, held.dtype),
+            jax.ShapeDtypeStruct(landed.shape, landed.dtype),
+            jax.ShapeDtypeStruct((8,), jnp.int32),
+            jax.ShapeDtypeStruct((1,), jnp.int32),
+        ),
+        in_specs=[pl.BlockSpec(memory_space=pl.ANY), vmem, smem],
+        out_specs=(pl.BlockSpec(memory_space=pl.ANY), vmem, smem, smem),
+        scratch_shapes=[pltpu.SemaphoreType.DMA((4,))],
+        input_output_aliases={0: 0, 2: 2},
+        compiler_params=pltpu.CompilerParams(vmem_limit_bytes=16 * MIB),
+    )(held, landed, codes)
+
+
+def swap_kernel(distance, pair_ref, landed_ref, send_sem, recv_sem):
     me = lax.axis_index("dp")
-    after = lax.rem(me + distance, 256)
-    before = lax.rem(me + 256 - distance, 256)
+    partners = (lax.rem(me + distance, 256), lax.rem(me + 256 - distance, 256))
     barrier = pltpu.get_barrier_semaphore()
-    for device in (after, before):
+    for device in partners:
         pl.semaphore_signal(barrier, inc=1, device_id=(device,), device_id_type=MESH)
     pl.semaphore_wait(barrier, 2)
     copies = [
         pltpu.make_async_remote_copy(
-            src_ref=src,
-            dst_ref=dst,
+            src_ref=pair_ref.at[i],
+            dst_ref=landed_ref.at[i],
             send_sem=send_sem.at[i],
             recv_sem=recv_sem.at[i],
             device_id=(device,),
             device_id_type=MESH,
         )
-        for i, (src, dst, device) in enumerate(
-            ((ahead_ref, ahead_out, after), (back_ref, back_out, before))
-        )
+        for i, device in enumerate(partners)
     ]
     for copy in copies:
         copy.start()
@@ -128,24 +188,18 @@
         copy.wait()
 
 
-def both_ways(leaf, blocks):
+def swap(leaf, pair):
     anywhere = pl.BlockSpec(memory_space=pl.ANY)
     return pl.pallas_call(
         partial(swap_kernel, SHIFTS[leaf]),
-        out_shape=[jax.ShapeDtypeStruct(b.shape, b.dtype) for b in blocks],
-        in_specs=[anywhere] * 2,
-        out_specs=[anywhere] * 2,
+        out_shape=jax.ShapeDtypeStruct(pair.shape, pair.dtype),
+        in_specs=[anywhere],
+        out_specs=anywhere,
         scratch_shapes=[pltpu.SemaphoreType.DMA((2,)), pltpu.SemaphoreType.DMA((2,))],
-        compiler_params=pltpu.CompilerParams(collective_id=1 + leaf, has_side_effects=True),
-    )(*blocks)
-
-
-def exchange(high, low, blocks):
-    def group(i, blocks):
-        leaves = range(i * WIDTH, min((i + 1) * WIDTH, len(SHIFTS)))
-        return lax.switch(low, [partial(both_ways, leaf) for leaf in leaves], blocks)
-
-    return lax.switch(high, [partial(group, i) for i in range(-(-len(SHIFTS) // WIDTH))], blocks)
+        compiler_params=pltpu.CompilerParams(
+            collective_id=1 + leaf, has_side_effects=True, vmem_limit_bytes=MIB
+        ),
+    )(pair)
 
 
 def unit_rows(raw):
@@ -230,7 +284,7 @@
         ),
         in_specs=[smem, smem, vmem],
         out_specs=(vmem, vmem, vmem, vmem),
-        compiler_params=pltpu.CompilerParams(vmem_limit_bytes=48 * 1024 * 1024),
+        compiler_params=pltpu.CompilerParams(vmem_limit_bytes=36 * MIB),
     )(log_scale, bias, held)
 
 
@@ -293,24 +347,23 @@
         in_specs=[vmem],
         out_specs=vmem,
         scratch_shapes=scratch,
-        compiler_params=pltpu.CompilerParams(collective_id=0, has_side_effects=True),
+        compiler_params=pltpu.CompilerParams(
+            collective_id=0, has_side_effects=True, vmem_limit_bytes=4 * MIB
+        ),
     )(parts)[:3, 0]
 
 
 def local(audio, text, log_scale, bias, plan):
     n = audio.shape[0]
     player_count = lax.axis_size("dp")
-    held, codes, count = plan_transfers(audio, text, plan)
-
-    def fetch(step, held):
-        code = lax.dynamic_index_in_dim(codes, step, keepdims=False)
-        high, low, *at = [(code >> (4 * i)) & 15 for i in range(6)]
-        blocks = [lax.dynamic_index_in_dim(held, i, keepdims=False) for i in at[:2]]
-        for block, i in zip(exchange(high, low, blocks), at[2:]):
-            held = lax.dynamic_update_index_in_dim(held, block, i, 0)
-        return held
-
-    held = lax.fori_loop(0, count[0], fetch, held)
+    leaves = [partial(swap, leaf) for leaf in range(len(SHIFTS))]
+
+    def transfer(state):
+        held, pair, codes, leaf = state
+        return store_landed(held, lax.switch(leaf[0], leaves, pair), codes)
+
+    state = plan_transfers(audio, text, plan)
+    held = lax.while_loop(lambda state: state[3][0] >= 0, transfer, state)[0]
     row_loss, grad_audio, grad_text, parts = loss_and_grads(log_scale, bias, held)
     stats = all_stats(parts, float((ROUNDS + 1) * n * n * player_count))
     return (row_loss.reshape(n), grad_audio, grad_text, stats)

time: 248 us -> 135 us (0.54)
  Pallas kernels: 181 us -> 120 us
  local copies, waits for them, and re-layouts: 35.6 us -> 4.04 us
  loops' own time: 28.8 us -> 7.78 us
    pallas_call x1, Pallas kernels: 34.2 us -> 2.14 us  [plan_transfers(): pl.pallas_call(plan_kernel, out_shape=(jax.ShapeDtypeStruct((2 * (ROUNDS...]
    dynamic_update_slice x12 -> x0, local copies, waits for them, and re-layouts: 22.6 us -> none  [fetch(): held = lax.dynamic_update_index_in_dim(held, block, i, 0)]
    another operation x13 -> x6, loops' own time: 28.8 us -> 7.78 us  [the longest x1 7.42 us: local(): held = lax.while_loop(lambda state: state[3][0] >= 0, transfer, state)[0]]
    pallas_call x6 -> x10, Pallas kernels: 113 us -> 96.1 us  [the longest x5 85.2 us: swap(): pl.pallas_call(partial(swap_kernel, SHIFTS[leaf]), out_shape=jax.ShapeDty...]
    pallas_call x1, Pallas kernels: 26.1 us -> 14.4 us  [all_stats(): pl.pallas_call(partial(stats_kernel, denominator), out_shape=jax.ShapeDty...]
    squeeze x6 -> x0, local copies, waits for them, and re-layouts: 7.66 us -> none  [fetch(): blocks = [lax.dynamic_index_in_dim(held, i, keepdims=False) for i in at[:2]]]
    dynamic_slice x6 -> x0, local copies, waits for them, and re-layouts: 3.52 us -> none  [fetch(): code = lax.dynamic_index_in_dim(codes, step, keepdims=False)]
    unnamed x2 -> x8, local copies, waits for them, and re-layouts: 0.58 us -> 3.41 us
where the time goes in v3:
time: 135 us; the launch traced here: 134 us
  Pallas kernels  120 us (89%)
  loops' own time  7.78 us (6%)
  local copies, waits for them, and re-layouts  4.04 us (3%)
  between operations  1.96 us (1%)
    pallas_call x5, Pallas kernels, swap(): pl.pallas_call(partial(swap_kernel, SHIFTS[leaf]), out_shape=jax.ShapeDty...  85.2 us
    pallas_call x1, Pallas kernels, all_stats(): pl.pallas_call(partial(stats_kernel, denominator), out_shape=jax.ShapeDty...  14.4 us
    pallas_call x5, Pallas kernels, store_landed(): pl.pallas_call(store_kernel, out_shape=(jax.ShapeDtypeStruct(held.shape,...  10.9 us
    pallas_call x1, Pallas kernels, loss_and_grads(): pl.pallas_call(loss_kernel, out_shape=(jax.ShapeDtypeStruct((1, n), jnp.f...  7.67 us
    another operation x1, loops' own time, local(): held = lax.while_loop(lambda state: state[3][0] >= 0, transfer, state)[0]  7.42 us
    unnamed x8, local copies, waits for them, and re-layouts  3.41 us

profile of v3, /device:TPU:1, one launch (start us, length us, event | category | flops | bytes accessed | tf_op | source)
XLA Modules:
  0.0 134.1 jit_solution(1759730306531138509)
XLA Ops:
  0.6 0.0 copy-start
  0.6 1.0 copy-done
  1.7 0.0 copy-start.1
  1.7 1.0 copy-done.1
  2.7 0.0 copy-start.2
  2.7 0.7 copy-done.2
  3.4 0.0 copy-start.3
  3.4 0.7 copy-done.3
  4.1 2.1 %shard_map.93 = (bf16[8,256,1024]{2,1,0:T(8,128)(2,1)}, bf16[2,256,1024]{2,1,0:T(8,128)(2,1)S(1)}, s32[8]{0:T(128)S(1)}, s32[1]{0:T(128)}) custom-call(s32[1,3]{1,0:T(1,128)S(1)} %copy-done.3, s32[384]{0:T(512)S(1)} %copy-done.2, bf16[256,1024]{1,0:T(8,128)(2,1)S(1)} %copy-done, bf16[256,1024]{1,0:T(8,128)(2,1)S(1)} %copy-done.1), custom_call_target="tpu_custom_call" | custom-call | tf_op jit(solution)/shard_map/pallas_call | solution.py:95
  6.2 103.9 %while.119 = (bf16[8,256,1024]{2,1,0:T(8,128)(2,1)}, bf16[2,256,1024]{2,1,0:T(8,128)(2,1)S(1)}, s32[8]{0:T(128)S(1)}, s32[1]{0:T(128)}, s32[1]{0:T(128)}, /*index=5*/s32[1]{0:T(128)}) while((bf16[8,256,1024]{2,1,0:T(8,128)(2,1)}, bf16[2,256,1024]{2,1,0:T(8,128)(2,1)S(1)}, s32[8]{0:T(128)S(1)}, s32[1]{0:T(128)}, s32[1]{0:T(128)}, ...), condition=%wide.region_36.0_spmd, body=%wide.region_0.0_spmd | while | flops 2 | bytes 81 | solution.py:366
  7.5 20.6 %conditional.1 = (bf16[2,256,1024]{2,1,0:T(8,128)(2,1)S(1)}) conditional(s32[]{:T(128)} %bitcast.4, bf16[2,256,1024]{2,1,0:T(8,128)(2,1)S(1)} %get-tuple-element.142, bf16[2,256,1024]{2,1,0:T(8,128)(2,1)S(1)} %get-tuple-element.142, bf16[2,256,1024]{2,1,0:T(8,128)(2,1)S(1)} %get-tuple-element.142, ...), branch_computations={%region_1.0_spmd, %region_2.0_spmd, %region_3.0_spmd, %region_4.0_... | conditional | bytes 8 | solution.py:363
  7.6 20.5 %branch_18_fun.1 = bf16[2,256,1024]{2,1,0:T(8,128)(2,1)S(1)} custom-call(bf16[2,256,1024]{2,1,0:T(8,128)(2,1)S(1)} %pair_ref.18), custom_call_target="tpu_custom_call" | custom-call | tf_op jit(solution)/shard_map/while/body/cond/branch_18_fun/pallas_call | solution.py:193
  28.1 2.2 %body.1 = (bf16[8,256,1024]{2,1,0:T(8,128)(2,1)}, bf16[2,256,1024]{2,1,0:T(8,128)(2,1)S(1)}, s32[8]{0:T(128)S(1)}, s32[1]{0:T(128)}) custom-call(bf16[8,256,1024]{2,1,0:T(8,128)(2,1)} %get-tuple-element.141.held_in, bf16[2,256,1024]{2,1,0:T(8,128)(2,1)S(1)} %get-tuple-element.153.landed_ref, ...), custom_call_target="tpu_custom_call", output_to_operand_aliasing={{0}: (0, {}), {2}: (2, {})} | custom-call | tf_op jit(solution)/shard_map/while/body/pallas_call | solution.py:151
  31.6 14.2 %conditional.1 = (bf16[2,256,1024]{2,1,0:T(8,128)(2,1)S(1)}) conditional(s32[]{:T(128)} %bitcast.4, bf16[2,256,1024]{2,1,0:T(8,128)(2,1)S(1)} %get-tuple-element.142, bf16[2,256,1024]{2,1,0:T(8,128)(2,1)S(1)} %get-tuple-element.142, bf16[2,256,1024]{2,1,0:T(8,128)(2,1)S(1)} %get-tuple-element.142, ...), branch_computations={%region_1.0_spmd, %region_2.0_spmd, %region_3.0_spmd, %region_4.0_... | conditional | bytes 8 | solution.py:363
  31.7 14.2 %branch_18_fun.1 = bf16[2,256,1024]{2,1,0:T(8,128)(2,1)S(1)} custom-call(bf16[2,256,1024]{2,1,0:T(8,128)(2,1)S(1)} %pair_ref.18), custom_call_target="tpu_custom_call" | custom-call | tf_op jit(solution)/shard_map/while/body/cond/branch_18_fun/pallas_call | solution.py:193
  45.9 2.2 %body.1 = (bf16[8,256,1024]{2,1,0:T(8,128)(2,1)}, bf16[2,256,1024]{2,1,0:T(8,128)(2,1)S(1)}, s32[8]{0:T(128)S(1)}, s32[1]{0:T(128)}) custom-call(bf16[8,256,1024]{2,1,0:T(8,128)(2,1)} %get-tuple-element.141.held_in, bf16[2,256,1024]{2,1,0:T(8,128)(2,1)S(1)} %get-tuple-element.153.landed_ref, ...), custom_call_target="tpu_custom_call", output_to_operand_aliasing={{0}: (0, {}), {2}: (2, {})} | custom-call | tf_op jit(solution)/shard_map/while/body/pallas_call | solution.py:151
  49.4 17.9 %conditional.1 = (bf16[2,256,1024]{2,1,0:T(8,128)(2,1)S(1)}) conditional(s32[]{:T(128)} %bitcast.4, bf16[2,256,1024]{2,1,0:T(8,128)(2,1)S(1)} %get-tuple-element.142, bf16[2,256,1024]{2,1,0:T(8,128)(2,1)S(1)} %get-tuple-element.142, bf16[2,256,1024]{2,1,0:T(8,128)(2,1)S(1)} %get-tuple-element.142, ...), branch_computations={%region_1.0_spmd, %region_2.0_spmd, %region_3.0_spmd, %region_4.0_... | conditional | bytes 8 | solution.py:363
  49.4 17.9 %branch_5_fun.1 = bf16[2,256,1024]{2,1,0:T(8,128)(2,1)S(1)} custom-call(bf16[2,256,1024]{2,1,0:T(8,128)(2,1)S(1)} %pair_ref.5), custom_call_target="tpu_custom_call" | custom-call | tf_op jit(solution)/shard_map/while/body/cond/branch_5_fun/pallas_call | solution.py:193
  67.4 2.2 %body.1 = (bf16[8,256,1024]{2,1,0:T(8,128)(2,1)}, bf16[2,256,1024]{2,1,0:T(8,128)(2,1)S(1)}, s32[8]{0:T(128)S(1)}, s32[1]{0:T(128)}) custom-call(bf16[8,256,1024]{2,1,0:T(8,128)(2,1)} %get-tuple-element.141.held_in, bf16[2,256,1024]{2,1,0:T(8,128)(2,1)S(1)} %get-tuple-element.153.landed_ref, ...), custom_call_target="tpu_custom_call", output_to_operand_aliasing={{0}: (0, {}), {2}: (2, {})} | custom-call | tf_op jit(solution)/shard_map/while/body/pallas_call | solution.py:151
  70.8 16.2 %conditional.1 = (bf16[2,256,1024]{2,1,0:T(8,128)(2,1)S(1)}) conditional(s32[]{:T(128)} %bitcast.4, bf16[2,256,1024]{2,1,0:T(8,128)(2,1)S(1)} %get-tuple-element.142, bf16[2,256,1024]{2,1,0:T(8,128)(2,1)S(1)} %get-tuple-element.142, bf16[2,256,1024]{2,1,0:T(8,128)(2,1)S(1)} %get-tuple-element.142, ...), branch_computations={%region_1.0_spmd, %region_2.0_spmd, %region_3.0_spmd, %region_4.0_... | conditional | bytes 8 | solution.py:363
  70.9 16.1 %branch_19_fun.1 = bf16[2,256,1024]{2,1,0:T(8,128)(2,1)S(1)} custom-call(bf16[2,256,1024]{2,1,0:T(8,128)(2,1)S(1)} %pair_ref.19), custom_call_target="tpu_custom_call" | custom-call | tf_op jit(solution)/shard_map/while/body/cond/branch_19_fun/pallas_call | solution.py:193
  87.0 2.2 %body.1 = (bf16[8,256,1024]{2,1,0:T(8,128)(2,1)}, bf16[2,256,1024]{2,1,0:T(8,128)(2,1)S(1)}, s32[8]{0:T(128)S(1)}, s32[1]{0:T(128)}) custom-call(bf16[8,256,1024]{2,1,0:T(8,128)(2,1)} %get-tuple-element.141.held_in, bf16[2,256,1024]{2,1,0:T(8,128)(2,1)S(1)} %get-tuple-element.153.landed_ref, ...), custom_call_target="tpu_custom_call", output_to_operand_aliasing={{0}: (0, {}), {2}: (2, {})} | custom-call | tf_op jit(solution)/shard_map/while/body/pallas_call | solution.py:151
  90.5 16.6 %conditional.1 = (bf16[2,256,1024]{2,1,0:T(8,128)(2,1)S(1)}) conditional(s32[]{:T(128)} %bitcast.4, bf16[2,256,1024]{2,1,0:T(8,128)(2,1)S(1)} %get-tuple-element.142, bf16[2,256,1024]{2,1,0:T(8,128)(2,1)S(1)} %get-tuple-element.142, bf16[2,256,1024]{2,1,0:T(8,128)(2,1)S(1)} %get-tuple-element.142, ...), branch_computations={%region_1.0_spmd, %region_2.0_spmd, %region_3.0_spmd, %region_4.0_... | conditional | bytes 8 | solution.py:363
  90.6 16.5 %branch_19_fun.1 = bf16[2,256,1024]{2,1,0:T(8,128)(2,1)S(1)} custom-call(bf16[2,256,1024]{2,1,0:T(8,128)(2,1)S(1)} %pair_ref.19), custom_call_target="tpu_custom_call" | custom-call | tf_op jit(solution)/shard_map/while/body/cond/branch_19_fun/pallas_call | solution.py:193
  107.1 2.2 %body.1 = (bf16[8,256,1024]{2,1,0:T(8,128)(2,1)}, bf16[2,256,1024]{2,1,0:T(8,128)(2,1)S(1)}, s32[8]{0:T(128)S(1)}, s32[1]{0:T(128)}) custom-call(bf16[8,256,1024]{2,1,0:T(8,128)(2,1)} %get-tuple-element.141.held_in, bf16[2,256,1024]{2,1,0:T(8,128)(2,1)S(1)} %get-tuple-element.153.landed_ref, ...), custom_call_target="tpu_custom_call", output_to_operand_aliasing={{0}: (0, {}), {2}: (2, {})} | custom-call | tf_op jit(solution)/shard_map/while/body/pallas_call | solution.py:151
  111.4 7.7 %shard_map.94 = (f32[1,256]{1,0:T(1,128)}, f32[256,1024]{1,0:T(8,128)}, f32[256,1024]{1,0:T(8,128)}, f32[8,128]{1,0:T(8,128)S(1)}) custom-call(f32[1]{0:T(128)S(6)} %copy.61.scale_ref, f32[1]{0:T(128)S(6)} %copy.62.bias_ref, bf16[8,256,1024]{2,1,0:T(8,128)(2,1)} %get-tuple-element.101.held_ref), custom_call_target="tpu_custom_call" | custom-call | tf_op jit(solution)/shard_map/pallas_call | solution.py:277
  119.1 14.4 %shard_map.95 = f32[8,128]{1,0:T(8,128)S(1)} custom-call(f32[8,128]{1,0:T(8,128)S(1)} %get-tuple-element.105.part_ref), custom_call_target="tpu_custom_call" | custom-call | tf_op jit(solution)/shard_map/pallas_call | solution.py:344
  133.5 0.6 slice_reduce_fusion
Async XLA Ops:
  0.6 1.0 copy-start
  1.7 1.0 copy-start.1
  2.7 0.7 copy-start.2
  3.4 0.7 copy-start.3

commit v4 on v3

v4 whole, which is shorter than its diff:
```python
from functools import partial

import jax
import jax.numpy as jnp
import numpy as np
from jax import lax
from jax.experimental import pallas as pl
from jax.experimental.pallas import tpu as pltpu
from jax.sharding import PartitionSpec as P

EPSILON = 1e-06
ROUNDS = 3
HALF = 128
STAGES = ((1, 8), (8, 4), (32, 8))
MESH = pl.DeviceIdType.MESH
MIB = 1024 * 1024
ANY = pl.BlockSpec(memory_space=pl.ANY)
VMEM = pl.BlockSpec(memory_space=pltpu.VMEM)
SMEM = pl.BlockSpec(memory_space=pltpu.SMEM)

SHIFTS = (1, 2, 5, 6, 7, 8, 9, 16, 19, 21, 23, 24, 25, 26, 28, 30, 31, 32, 33, 34, 36, 37, 41, 42, 43, 45, 46, 50, 54, 55, 57, 61, 64, 67, 128)
COST = [159, 206, 365, 412, 260, 213, 212, 209, 248, 407, 454, 426, 424, 422, 421, 322, 408, 409, 338, 427, 324, 402, 261, 196, 229, 214, 373, 299, 372, 213, 216, 170, 228, 269, 427, 317, 302, 383, 381, 379, 313, 327, 345, 504, 348, 348, 458, 393, 425, 323, 443, 429, 474, 330, 325, 366, 329, 384, 443, 426, 338, 383, 386, 282, 398, 439, 388, 487, 472, 494, 493, 491, 483, 497, 515, 537, 518, 518, 521, 536, 525, 492, 543, 543, 535, 500, 495, 478, 498, 496, 551, 555, 508, 495, 498, 451, 510, 550, 558, 598, 584, 597, 611, 579, 595, 609, 627, 660, 630, 630, 659, 653, 736, 604, 668, 663, 710, 612, 607, 592, 594, 595, 643, 716, 620, 588, 541, 382]
FIRST = [0, 2, 0, 2, 4, 6, 8, 10, 12, 0, 2, 6, 6, 6, 8, 14, 9, 7, 16, 7, 18, 3, 20, 22, 24, 26, 0, 28, 1, 30, 32, 34, 36, 38, 0, 40, 42, 6, 8, 10, 44, 46, 48, 0, 50, 52, 20, 22, 22, 54, 24, 26, 20, 56, 58, 22, 60, 26, 26, 30, 62, 30, 32, 64, 34, 34, 66, 34, 34, 6, 8, 10, 34, 34, 34, 26, 34, 34, 22, 30, 22, 34, 26, 30, 22, 34, 34, 22, 34, 26, 30, 32, 34, 30, 32, 34, 36, 38, 34, 40, 42, 27, 25, 23, 44, 46, 48, 56, 50, 52, 56, 58, 52, 54, 56, 58, 54, 56, 58, 11, 9, 7, 5, 60, 62, 3, 1, 68]
SECOND = [-1, -1, 2, 2, -1, -1, -1, -1, -1, 12, 12, 6, 8, 10, 10, -1, 22, 22, -1, 26, -1, 22, -1, -1, -1, -1, 26, -1, 30, -1, -1, -1, -1, -1, 38, -1, -1, 34, 34, 34, -1, -1, -1, 48, -1, -1, 22, 22, 24, -1, 26, 26, 30, -1, -1, 34, -1, 34, 36, 30, -1, 34, 34, -1, 36, 38, -1, 40, 42, 64, 64, 64, 44, 46, 48, 54, 50, 52, 58, 54, 60, 54, 60, 56, 62, 56, 58, 64, 60, 64, 62, 62, 62, 64, 64, 64, 64, 64, 66, 64, 64, 68, 68, 68, 64, 64, 64, 56, 64, 64, 60, 60, 66, 64, 62, 62, 66, 64, 64, 68, 68, 68, 68, 66, 64, 68, 68, -1]

LANDED = 3
SOURCE, BACK, TARGET, LAST = 8, 10, 11, 13


def plan_kernel(
    plan_ref, table_ref, scale_ref, bias_ref, audio_ref, text_ref,
    pair_ref, code_ref, leaf_ref, scalar_ref, own_ref, held_ref, sems,
):
    loads = [
        pltpu.make_async_copy(ref, pair_ref.at[i], sems.at[i])
        for i, ref in enumerate((audio_ref, text_ref))
    ]
    keeps = [
        pltpu.make_async_copy(pair_ref.at[i], own_ref.at[i], sems.at[2 + i]) for i in range(2)
    ]
    for copy in loads:
        copy.start()
    scalar_ref[0:1, :] = jnp.full((1, 128), scale_ref[0], jnp.float32)
    scalar_ref[1:8, :] = jnp.full((7, 128), bias_ref[0], jnp.float32)
    me = lax.axis_index("dp")
    offsets = [(plan_ref[0, r] - me) & 255 for r in range(ROUNDS)]

    def entry(distance):
        return jnp.maximum(jnp.minimum(distance, 256 - distance) - 1, 0)

    def cost(distance):
        return table_ref[entry(distance)]

    def code(transfer, source, target):
        return (
            (transfer >> 1) | (source << SOURCE) | ((transfer & 1) << BACK) | (target << TARGET)
        )

    for load, keep in zip(loads, keeps):
        load.wait()
        keep.start()
    far = jnp.int32(1 << 28)
    best = [cost(s) for s in offsets]
    parent = [jnp.int32(0)] * ROUNDS
    away = list(offsets)
    done = [jnp.int32(0)] * ROUNDS
    count = jnp.int32(0)
    for step in range(ROUNDS):
        keys = [jnp.where(done[j] == 1, far, best[j]) for j in range(ROUNDS)]
        first = (keys[0] <= keys[1]) & (keys[0] <= keys[2])
        pick = jnp.where(first, 0, jnp.where(keys[1] <= keys[2], 1, 2))

        def chosen(values):
            return jnp.where(pick == 0, values[0], jnp.where(pick == 1, values[1], values[2]))

        distance = chosen(away)
        at = chosen(offsets)
        mirrored = jnp.where(distance <= HALF, 0, 1)
        one = table_ref[HALF + entry(distance)] ^ mirrored
        two = table_ref[2 * HALF + entry(distance)]
        twice = two >= 0
        two = jnp.maximum(two, 0) ^ mirrored
        source = chosen(parent)
        if step > 0:
            source = jnp.where(source == step, LANDED, source)
        code_ref[count] = code(one, source, jnp.where(twice, 0, step + 1))
        code_ref[count + 1] = code(two, LANDED, step + 1)
        count = count + jnp.where(twice, 2, 1)
        for j in range(ROUNDS):
            done[j] = jnp.where(pick == j, 1, done[j])
            onward = (offsets[j] - at) & 255
            price = cost(onward)
            nearer = price < best[j]
            best[j] = jnp.where(nearer, price, best[j])
            parent[j] = jnp.where(nearer, step + 1, parent[j])
            away[j] = jnp.where(nearer, onward, away[j])
    code_ref[count - 1] = code_ref[count - 1] | (1 << LAST)
    leaf_ref[0] = code_ref[0] & 255
    for copy in keeps:
        copy.wait()

    @pl.when(((code_ref[0] >> BACK) & 1) == 1)
    def _():
        audio, text = pair_ref[0], pair_ref[1]
        pair_ref[0] = text
        pair_ref[1] = audio


def plan_transfers(audio, text, log_scale, bias, plan):
    return pl.pallas_call(
        plan_kernel,
        out_shape=(
            jax.ShapeDtypeStruct((2,) + audio.shape, audio.dtype),
            jax.ShapeDtypeStruct((8,), jnp.int32),
            jax.ShapeDtypeStruct((1,), jnp.int32),
            jax.ShapeDtypeStruct((8, 128), jnp.float32),
            jax.ShapeDtypeStruct((2,) + audio.shape, audio.dtype),
            jax.ShapeDtypeStruct((2 * (ROUNDS - 1),) + audio.shape, audio.dtype),
        ),
        in_specs=[SMEM, SMEM, SMEM, SMEM, ANY, ANY],
        out_specs=(VMEM, SMEM, SMEM, VMEM, ANY, ANY),
        scratch_shapes=[pltpu.SemaphoreType.DMA((4,))],
    )(plan, jnp.asarray(np.array(COST + FIRST + SECOND, np.int32)), log_scale, bias, audio, text)


def store_kernel(
    held_in, own_in, landed_ref, code_in,
    held_ref, own_ref, pair_ref, code_ref, leaf_ref, sems,
):
    codes = [code_in[i] for i in range(8)]
    back = (codes[0] >> BACK) & 1
    target = (codes[0] >> TARGET) & 3
    slot = jnp.where(target == 2, 1, 0)
    stores = [
        pltpu.make_async_copy(
            landed_ref.at[i], held_ref.at[2 * slot + (back if i == 0 else 1 - back)], sems.at[i]
        )
        for i in range(2)
    ]

    @pl.when(target > 0)
    def _():
        for copy in stores:
            copy.start()

    for i in range(7):
        code_ref[i] = codes[i + 1]
    code_ref[7] = 0
    leaf_ref[0] = (codes[1] & 255) | (((codes[1] >> LAST) & 1) << 8)
    source = (codes[1] >> SOURCE) & 3
    turn = (codes[1] >> BACK) & 1

    def load(first, second):
        loads = [
            pltpu.make_async_copy(ref, pair_ref.at[i], sems.at[2 + i])
            for i, ref in enumerate((first, second))
        ]
        for copy in loads:
            copy.start()
        for copy in loads:
            copy.wait()

    @pl.when(source == LANDED)
    def _():
        same = back == turn
        first, second = landed_ref[0], landed_ref[1]
        pair_ref[0] = jnp.where(same, first, second)
        pair_ref[1] = jnp.where(same, second, first)

    @pl.when(source == 0)
    def _():
        load(own_ref.at[turn], own_ref.at[1 - turn])

    @pl.when((source == 1) | (source == 2))
    def _():
        at = 2 * jnp.where(source == 2, 1, 0)
        load(held_ref.at[at + turn], held_ref.at[at + 1 - turn])

    @pl.when(target > 0)
    def _():
        for copy in stores:
            copy.wait()


def store_landed(held, own, landed, codes):
    return pl.pallas_call(
        store_kernel,
        out_shape=(
            jax.ShapeDtypeStruct(held.shape, held.dtype),
            jax.ShapeDtypeStruct(own.shape, own.dtype),
            jax.ShapeDtypeStruct(landed.shape, landed.dtype),
            jax.ShapeDtypeStruct((8,), jnp.int32),
            jax.ShapeDtypeStruct((1,), jnp.int32),
        ),
        in_specs=[ANY, ANY, VMEM, SMEM],
        out_specs=(ANY, ANY, VMEM, SMEM, SMEM),
        scratch_shapes=[pltpu.SemaphoreType.DMA((4,))],
        input_output_aliases={0: 0, 1: 1, 3: 3},
    )(held, own, landed, codes)


def swap_kernel(distance, pair_ref, landed_ref, send_sem, recv_sem):
    me = lax.axis_index("dp")
    partners = (lax.rem(me + distance, 256), lax.rem(me + 256 - distance, 256))
    barrier = pltpu.get_barrier_semaphore()
    for device in partners:
        pl.semaphore_signal(barrier, inc=1, device_id=(device,), device_id_type=MESH)
    pl.semaphore_wait(barrier, 2)
    copies = [
        pltpu.make_async_remote_copy(
            src_ref=pair_ref.at[i],
            dst_ref=landed_ref.at[i],
            send_sem=send_sem.at[i],
            recv_sem=recv_sem.at[i],
            device_id=(device,),
            device_id_type=MESH,
        )
        for i, device in enumerate(partners)
    ]
    for copy in copies:
        copy.start()
    for copy in copies:
        copy.wait()


def swap(leaf, pair):
    return pl.pallas_call(
        partial(swap_kernel, SHIFTS[leaf]),
        out_shape=jax.ShapeDtypeStruct(pair.shape, pair.dtype),
        in_specs=[ANY],
        out_specs=ANY,
        scratch_shapes=[pltpu.SemaphoreType.DMA((2,)), pltpu.SemaphoreType.DMA((2,))],
        compiler_params=pltpu.CompilerParams(
            collective_id=1 + leaf, has_side_effects=True, vmem_limit_bytes=MIB
        ),
    )(pair)


def unit_rows(raw):
    wide = raw.astype(jnp.float32)
    recip = lax.rsqrt(jnp.sum(wide * wide, axis=-1, keepdims=True) + EPSILON)
    wide = wide * recip
    return wide, recip, wide.astype(jnp.bfloat16)


def dot_t(a, b):
    return lax.dot_general(a, b, (((1,), (1,)), ((), ())), preferred_element_type=jnp.float32)


def project(wide, recip, grad):
    along = jnp.sum(wide * grad, axis=-1, keepdims=True)
    return recip * (grad - wide * along)


def loss_kernel(
    scalar_ref, code_ref, audio_ref, text_ref, held_ref, landed_ref,
    row_ref, ga_ref, gt_ref, tot_ref, audio_out, text_out, sems,
):
    n = audio_ref.shape[0]
    scale = jnp.exp(scalar_ref[0:1, 0:1])
    bias = scalar_ref[1:2, 0:1]
    rows = lax.broadcasted_iota(jnp.int32, (n, n), 0)
    cols = lax.broadcasted_iota(jnp.int32, (n, n), 1)
    eye = (rows == cols).astype(jnp.float32)
    backwards = ((code_ref[0] >> BACK) & 1) == 1

    audio_wide, audio_recip, audio_unit = unit_rows(audio_ref[...])
    text_wide, text_recip, text_unit = unit_rows(text_ref[...])
    losses_sum = jnp.zeros((n, n), jnp.float32)
    slopes_sum = jnp.zeros((n, n), jnp.float32)
    scaled_sum = jnp.zeros((n, n), jnp.float32)
    audio_grad = jnp.zeros(audio_wide.shape, jnp.float32)
    text_grad = jnp.zeros(text_wide.shape, jnp.float32)
    for slot in range(ROUNDS + 1):
        if slot == 0:
            far_text = text_unit
        elif slot < ROUNDS:
            far_text = unit_rows(held_ref[2 * slot - 1])[2]
        else:
            far_text = unit_rows(jnp.where(backwards, landed_ref[0], landed_ref[1]))[2]
        scaled = scale * dot_t(audio_unit, far_text)
        logits = scaled + bias
        small = jnp.exp(-jnp.abs(logits))
        slopes = jnp.where(logits >= 0.0, 1.0, small) / (1.0 + small)
        if slot == 0:
            flipped = jnp.where(rows == cols, -logits, logits)
            slopes = slopes - eye
        else:
            flipped = logits
        losses_sum = losses_sum + (jnp.maximum(flipped, 0.0) + jnp.log1p(small))
        slopes_sum = slopes_sum + slopes
        scaled_sum = scaled_sum + slopes * scaled
        weights = (scale * slopes).astype(jnp.bfloat16)
        audio_grad = audio_grad + jnp.dot(weights, far_text, preferred_element_type=jnp.float32)
    audio_out[...] = project(audio_wide, audio_recip, audio_grad)
    audio_store = pltpu.make_async_copy(audio_out, ga_ref, sems.at[0])
    audio_store.start()

    for slot in range(ROUNDS + 1):
        if slot == 0:
            far_audio = audio_unit
        elif slot < ROUNDS:
            far_audio = unit_rows(held_ref[2 * slot - 2])[2]
        else:
            far_audio = unit_rows(jnp.where(backwards, landed_ref[1], landed_ref[0]))[2]
        logits = scale * dot_t(text_unit, far_audio) + bias
        small = jnp.exp(-jnp.abs(logits))
        slopes = jnp.where(logits >= 0.0, 1.0, small) / (1.0 + small)
        if slot == 0:
            slopes = slopes - eye
        weights = (scale * slopes).astype(jnp.bfloat16)
        text_grad = text_grad + jnp.dot(weights, far_audio, preferred_element_type=jnp.float32)
    text_out[...] = project(text_wide, text_recip, text_grad)
    text_store = pltpu.make_async_copy(text_out, gt_ref, sems.at[1])
    text_store.start()

    folded = losses_sum[:, : n // 2] + losses_sum[:, n // 2 :]
    row_ref[...] = jnp.sum(folded.T, axis=0, keepdims=True)
    parts = []
    for total in (losses_sum, slopes_sum, scaled_sum):
        down = jnp.sum(total, axis=0, keepdims=True)
        parts.append(down[:, : n // 2] + down[:, n // 2 :])
    tot_ref[...] = jnp.concatenate(parts + [jnp.zeros((5, n // 2), jnp.float32)], axis=0)
    audio_store.wait()
    text_store.wait()


def loss_and_grads(scalars, codes, audio, text, held, landed):
    n, d = audio.shape
    return pl.pallas_call(
        loss_kernel,
        out_shape=(
            jax.ShapeDtypeStruct((1, n), jnp.float32),
            jax.ShapeDtypeStruct((n, d), jnp.float32),
            jax.ShapeDtypeStruct((n, d), jnp.float32),
            jax.ShapeDtypeStruct((8, n // 2), jnp.float32),
        ),
        in_specs=[VMEM, SMEM, VMEM, VMEM, VMEM, VMEM],
        out_specs=(VMEM, ANY, ANY, VMEM),
        scratch_shapes=[
            pltpu.VMEM((n, d), jnp.float32),
            pltpu.VMEM((n, d), jnp.float32),
            pltpu.SemaphoreType.DMA((2,)),
        ],
        compiler_params=pltpu.CompilerParams(vmem_limit_bytes=40 * MIB),
    )(scalars, codes, audio, text, held, landed)


def stats_kernel(denominator, part_ref, out_ref, *scratch):
    me = lax.axis_index("dp")
    buffers, sends, recvs = scratch[0:3], scratch[3:6], scratch[6:9]
    groups = []
    for stride, peers in STAGES:
        digit = lax.rem(lax.div(me, stride), peers)
        others = []
        for k in range(1, peers):
            other = lax.rem(digit + k, peers)
            others.append((other, me + (other - digit) * stride))
        groups.append((digit, others))
    barrier = pltpu.get_barrier_semaphore()
    count = 0
    for _, others in groups:
        for _, device in others:
            pl.semaphore_signal(barrier, inc=1, device_id=(device,), device_id_type=MESH)
            count += 1
    pl.semaphore_wait(barrier, count)
    value = part_ref[...]
    sent = []
    for stage, (digit, others) in enumerate(groups):
        buffer, send, recv = buffers[stage], sends[stage], recvs[stage]
        buffer[digit] = value
        for other, device in others:
            pltpu.make_async_remote_copy(
                src_ref=buffer.at[digit],
                dst_ref=buffer.at[digit],
                send_sem=send.at[other],
                recv_sem=recv.at[digit],
                device_id=(device,),
                device_id_type=MESH,
            ).start()
        for other, device in others:
            arrived = pltpu.make_async_remote_copy(
                src_ref=buffer.at[digit],
                dst_ref=buffer.at[other],
                send_sem=send.at[other],
                recv_sem=recv.at[other],
                device_id=(device,),
                device_id_type=MESH,
            )
            arrived.wait_recv()
            sent.append(arrived)
        value = buffer[0]
        for j in range(1, STAGES[stage][1]):
            value = value + buffer[j]
    for copy in sent:
        copy.wait_send()
    total = jnp.sum(value, axis=1, keepdims=True) / denominator
    out_ref[...] = jnp.broadcast_to(total, out_ref.shape)


def all_stats(parts, denominator):
    scratch = [pltpu.VMEM((peers,) + parts.shape, jnp.float32) for _, peers in STAGES]
    scratch += [pltpu.SemaphoreType.DMA((peers,)) for _, peers in STAGES] * 2
    return pl.pallas_call(
        partial(stats_kernel, denominator),
        out_shape=jax.ShapeDtypeStruct(parts.shape, jnp.float32),
        in_specs=[VMEM],
        out_specs=VMEM,
        scratch_shapes=scratch,
        compiler_params=pltpu.CompilerParams(
            collective_id=0, has_side_effects=True, vmem_limit_bytes=4 * MIB
        ),
    )(parts)[:3, 0]


def local(audio, text, log_scale, bias, plan):
    n, d = audio.shape
    player_count = lax.axis_size("dp")
    leaves = [partial(swap, leaf) for leaf in range(len(SHIFTS))]
    pair, codes, leaf, scalars, own, held = plan_transfers(audio, text, log_scale, bias, plan)

    def transfer(state):
        held, own, pair, codes, leaf = state
        landed = lax.switch(leaf[0], leaves, pair)
        return store_landed(held, own, landed, codes)

    state = (held, own, pair, codes, leaf)
    held, _, pair, codes, leaf = lax.while_loop(lambda s: s[4][0] < 256, transfer, state)
    landed = lax.switch(leaf[0] - 256, leaves, pair)
    row_loss, grad_audio, grad_text, parts = loss_and_grads(
        scalars, codes, audio, text, held, landed
    )
    stats = all_stats(parts, float((ROUNDS + 1) * n * n * player_count))
    return (row_loss.reshape(n), grad_audio, grad_text, stats)


def solution(mesh):
    return jax.shard_map(
        local,
        mesh=mesh,
        in_specs=(P("dp", None), P("dp", None), P(), P(), P("dp", None)),
        out_specs=(P("dp"), P("dp", None), P("dp", None), P()),
        check_vma=False,
    )
```

time: 135 us -> 145 us (1.074)
  Pallas kernels: 120 us -> 136 us
  local copies, waits for them, and re-layouts: 4.04 us -> 0.65 us
  loops' own time: 7.78 us -> 5.07 us
    pallas_call x5 -> x4, Pallas kernels: 85.2 us -> 102 us  [swap(): pl.pallas_call(partial(swap_kernel, SHIFTS[leaf]), out_shape=jax.ShapeDty...]
    pallas_call x5 -> x3, Pallas kernels: 10.9 us -> 6.21 us  [store_landed(): pl.pallas_call(store_kernel, out_shape=(jax.ShapeDtypeStruct(held.shape,...]
    unnamed x8 -> x6, local copies, waits for them, and re-layouts: 3.41 us -> 0.02 us
    pallas_call x1, Pallas kernels: 14.4 us -> 17.2 us  [all_stats(): pl.pallas_call(partial(stats_kernel, denominator), out_shape=jax.ShapeDty...]
    another operation x6 -> x5, loops' own time: 7.78 us -> 5.07 us  [the longest x1 4.6 us: local(): lax.while_loop(lambda s: s[4][0] < 256, transfer, state)]
where the time goes in v4:
time: 145 us
  Pallas kernels  136 us (94%)
  loops' own time  5.07 us (3%)
  between operations  2.66 us (2%)
    pallas_call x4, Pallas kernels, swap(): pl.pallas_call(partial(swap_kernel, SHIFTS[leaf]), out_shape=jax.ShapeDty...  102 us
    pallas_call x1, Pallas kernels, all_stats(): pl.pallas_call(partial(stats_kernel, denominator), out_shape=jax.ShapeDty...  17.2 us
    pallas_call x1, Pallas kernels, loss_and_grads(): pl.pallas_call(loss_kernel, out_shape=(jax.ShapeDtypeStruct((1, n), jnp.f...  8.18 us
    pallas_call x3, Pallas kernels, store_landed(): pl.pallas_call(store_kernel, out_shape=(jax.ShapeDtypeStruct(held.shape,...  6.21 us
    another operation x1, loops' own time, local(): lax.while_loop(lambda s: s[4][0] < 256, transfer, state)  4.6 us

profile of v4, /device:TPU:1, one launch (start us, length us, event | category | flops | bytes accessed | tf_op | source)
XLA Modules:
  0.0 144.7 jit_solution(16455758219421969040)
XLA Ops:
  1.9 2.8 %shard_map.93 = (bf16[2,256,1024]{2,1,0:T(8,128)(2,1)S(1)}, s32[8]{0:T(128)S(1)}, s32[1]{0:T(128)}, f32[8,128]{1,0:T(8,128)}, bf16[2,256,1024]{2,1,0:T(8,128)(2,1)S(1)}, /*index=5*/bf16[4,256,1024]{2,1,0:T(8,128)(2,1)}) custom-call(s32[1,3]{1,0:T(1,128)} %plan_ref.1, s32[384]{0:T(512)} %constant.21.clone.table_ref, f32[1]{0:T(128)S(6)} %copy.101.scale_ref, ...), custom_call_target="tpu_custom_call" | custom-call | tf_op jit(solution)/shard_map/pallas_call | solution.py:110
  4.7 84.9 %while.226 = (bf16[4,256,1024]{2,1,0:T(8,128)(2,1)}, bf16[2,256,1024]{2,1,0:T(8,128)(2,1)S(1)}, bf16[2,256,1024]{2,1,0:T(8,128)(2,1)S(1)}, s32[8]{0:T(128)S(1)}, s32[1]{0:T(128)}, /*index=5*/s32[1]{0:T(128)}, s32[1]{0:T(128)}) while((bf16[4,256,1024]{2,1,0:T(8,128)(2,1)}, bf16[2,256,1024]{2,1,0:T(8,128)(2,1)S(1)}, ...), condition=%wide.region_36.0_spmd, body=%wide.region_0.0_spmd | while | flops 2 | bytes 89 | solution.py:428
  6.0 24.8 %conditional.3 = (bf16[2,256,1024]{2,1,0:T(8,128)(2,1)S(1)}) conditional(s32[]{:T(128)} %bitcast.5, bf16[2,256,1024]{2,1,0:T(8,128)(2,1)S(1)} %get-tuple-element.245, bf16[2,256,1024]{2,1,0:T(8,128)(2,1)S(1)} %get-tuple-element.245, bf16[2,256,1024]{2,1,0:T(8,128)(2,1)S(1)} %get-tuple-element.245, ...), branch_computations={%region_1.0_spmd, %region_2.0_spmd, %region_3.0_spmd, %region_4.0_... | conditional | bytes 8 | solution.py:424
  6.0 24.7 %branch_6_fun.2 = bf16[2,256,1024]{2,1,0:T(8,128)(2,1)S(1)} custom-call(bf16[2,256,1024]{2,1,0:T(8,128)(2,1)S(1)} %pair_ref.6), custom_call_target="tpu_custom_call" | custom-call | tf_op jit(solution)/shard_map/while/body/cond/branch_6_fun/pallas_call | solution.py:227
  30.8 2.2 %body.1 = (bf16[4,256,1024]{2,1,0:T(8,128)(2,1)}, bf16[2,256,1024]{2,1,0:T(8,128)(2,1)S(1)}, bf16[2,256,1024]{2,1,0:T(8,128)(2,1)S(1)}, s32[8]{0:T(128)S(1)}, s32[1]{0:T(128)}) custom-call(bf16[4,256,1024]{2,1,0:T(8,128)(2,1)} %get-tuple-element.243.held_in, ...), custom_call_target="tpu_custom_call", output_to_operand_aliasing={{0}: (0, {}), {1}: (1, {}), {3}: (3, {})} | custom-call | tf_op jit(solution)/shard_map/while/body/pallas_call | solution.py:186
  34.2 21.7 %conditional.3 = (bf16[2,256,1024]{2,1,0:T(8,128)(2,1)S(1)}) conditional(s32[]{:T(128)} %bitcast.5, bf16[2,256,1024]{2,1,0:T(8,128)(2,1)S(1)} %get-tuple-element.245, bf16[2,256,1024]{2,1,0:T(8,128)(2,1)S(1)} %get-tuple-element.245, bf16[2,256,1024]{2,1,0:T(8,128)(2,1)S(1)} %get-tuple-element.245, ...), branch_computations={%region_1.0_spmd, %region_2.0_spmd, %region_3.0_spmd, %region_4.0_... | conditional | bytes 8 | solution.py:424
  34.3 21.7 %branch_1_fun.2 = bf16[2,256,1024]{2,1,0:T(8,128)(2,1)S(1)} custom-call(bf16[2,256,1024]{2,1,0:T(8,128)(2,1)S(1)} %pair_ref.1), custom_call_target="tpu_custom_call" | custom-call | tf_op jit(solution)/shard_map/while/body/cond/branch_1_fun/pallas_call | solution.py:227
  56.0 2.8 %body.1 = (bf16[4,256,1024]{2,1,0:T(8,128)(2,1)}, bf16[2,256,1024]{2,1,0:T(8,128)(2,1)S(1)}, bf16[2,256,1024]{2,1,0:T(8,128)(2,1)S(1)}, s32[8]{0:T(128)S(1)}, s32[1]{0:T(128)}) custom-call(bf16[4,256,1024]{2,1,0:T(8,128)(2,1)} %get-tuple-element.243.held_in, ...), custom_call_target="tpu_custom_call", output_to_operand_aliasing={{0}: (0, {}), {1}: (1, {}), {3}: (3, {})} | custom-call | tf_op jit(solution)/shard_map/while/body/pallas_call | solution.py:186
  60.1 27.6 %conditional.3 = (bf16[2,256,1024]{2,1,0:T(8,128)(2,1)S(1)}) conditional(s32[]{:T(128)} %bitcast.5, bf16[2,256,1024]{2,1,0:T(8,128)(2,1)S(1)} %get-tuple-element.245, bf16[2,256,1024]{2,1,0:T(8,128)(2,1)S(1)} %get-tuple-element.245, bf16[2,256,1024]{2,1,0:T(8,128)(2,1)S(1)} %get-tuple-element.245, ...), branch_computations={%region_1.0_spmd, %region_2.0_spmd, %region_3.0_spmd, %region_4.0_... | conditional | bytes 8 | solution.py:424
  60.1 27.5 %branch_28_fun.2 = bf16[2,256,1024]{2,1,0:T(8,128)(2,1)S(1)} custom-call(bf16[2,256,1024]{2,1,0:T(8,128)(2,1)S(1)} %pair_ref.28), custom_call_target="tpu_custom_call" | custom-call | tf_op jit(solution)/shard_map/while/body/cond/branch_28_fun/pallas_call | solution.py:227
  87.7 1.3 body.1
  90.3 0.0 copy-start
  90.3 0.0 copy-start.1
  90.3 0.0 copy-start.2
  90.3 28.4 %conditional.2 = (bf16[2,256,1024]{2,1,0:T(8,128)(2,1)S(1)}) conditional(s32[]{:T(128)} %bitcast.2, bf16[2,256,1024]{2,1,0:T(8,128)(2,1)S(1)} %get-tuple-element.195, bf16[2,256,1024]{2,1,0:T(8,128)(2,1)S(1)} %get-tuple-element.195, bf16[2,256,1024]{2,1,0:T(8,128)(2,1)S(1)} %get-tuple-element.195, ...), branch_computations={%region_37.0_spmd, %region_38.0_spmd, %region_39.0_spmd, %region_4... | conditional | bytes 8 | solution.py:429
  90.4 28.1 %branch_31_fun.3 = bf16[2,256,1024]{2,1,0:T(8,128)(2,1)S(1)} custom-call(bf16[2,256,1024]{2,1,0:T(8,128)(2,1)S(1)} %pair_ref.66), custom_call_target="tpu_custom_call" | custom-call | tf_op jit(solution)/shard_map/cond/branch_31_fun/pallas_call | solution.py:227
  118.7 0.0 copy-done
  118.7 0.0 copy-done.1
  118.7 0.0 copy-done.2
  118.7 8.2 %shard_map.94 = (f32[1,256]{1,0:T(1,128)}, f32[256,1024]{1,0:T(8,128)}, f32[256,1024]{1,0:T(8,128)}, f32[8,128]{1,0:T(8,128)S(1)}) custom-call(f32[8,128]{1,0:T(8,128)S(1)} %copy-done.2, s32[8]{0:T(128)S(1)} %get-tuple-element.192.code_ref, bf16[256,1024]{1,0:T(8,128)(2,1)S(1)} %copy-done, bf16[256,1024]{1,0:T(8,128)(2,1)S(1)} %copy-done.1, ...), custom_call_target="tpu_custom_call" | custom-call | tf_op jit(solution)/shard_map/pallas_call | solution.py:330
  126.9 17.2 %shard_map.95 = f32[8,128]{1,0:T(8,128)S(1)} custom-call(f32[8,128]{1,0:T(8,128)S(1)} %get-tuple-element.199.part_ref), custom_call_target="tpu_custom_call" | custom-call | tf_op jit(solution)/shard_map/pallas_call | solution.py:404
  144.1 0.6 slice_reduce_fusion
Async XLA Ops:
  90.3 28.4 %copy-start = (bf16[256,1024]{1,0:T(8,128)(2,1)S(1)}, bf16[256,1024]{1,0:T(8,128)(2,1)}, u32[]{:S(2)}) copy-start(bf16[256,1024]{1,0:T(8,128)(2,1)} %audio_ref.3) | copy-start | bytes 1572868
  90.3 28.4 %copy-start.1 = (bf16[256,1024]{1,0:T(8,128)(2,1)S(1)}, bf16[256,1024]{1,0:T(8,128)(2,1)}, u32[]{:S(2)}) copy-start(bf16[256,1024]{1,0:T(8,128)(2,1)} %text_ref.3) | copy-start | bytes 1572868
  90.3 28.4 %copy-start.2 = (f32[8,128]{1,0:T(8,128)S(1)}, f32[8,128]{1,0:T(8,128)}, u32[]{:S(2)}) copy-start(f32[8,128]{1,0:T(8,128)} %get-tuple-element.186.scalar_ref) | copy-start | bytes 12292

commit v5 on v4

--- a/solution.py
+++ b/solution.py
@@ -253,9 +253,60 @@
 
 
 def loss_kernel(
-    scalar_ref, code_ref, audio_ref, text_ref, held_ref, landed_ref,
-    row_ref, ga_ref, gt_ref, tot_ref, audio_out, text_out, sems,
+    denominator, scalar_ref, code_ref, audio_ref, text_ref, held_ref, landed_ref,
+    row_ref, ga_ref, gt_ref, stats_ref, audio_out, text_out, sems, *scratch,
 ):
+    me = lax.axis_index("dp")
+    count = len(STAGES)
+    buffers, sends, recvs = [scratch[i * count : (i + 1) * count] for i in range(3)]
+    groups = []
+    for stride, peers in STAGES:
+        digit = lax.rem(lax.div(me, stride), peers)
+        others = []
+        for k in range(1, peers):
+            other = lax.rem(digit + k, peers)
+            others.append((other, me + (other - digit) * stride))
+        groups.append((digit, others))
+    barrier = pltpu.get_barrier_semaphore()
+    for _, others in groups:
+        for _, device in others:
+            pl.semaphore_signal(barrier, inc=1, device_id=(device,), device_id_type=MESH)
+
+    def copies(stage):
+        digit, others = groups[stage]
+        return [
+            pltpu.make_async_remote_copy(
+                src_ref=buffers[stage].at[digit],
+                dst_ref=buffers[stage].at[digit],
+                send_sem=sends[stage].at[other],
+                recv_sem=recvs[stage].at[digit],
+                device_id=(device,),
+                device_id_type=MESH,
+            )
+            for other, device in others
+        ]
+
+    def send(stage, value):
+        buffers[stage][groups[stage][0]] = value
+        for copy in copies(stage):
+            copy.start()
+
+    def receive(stage):
+        digit, others = groups[stage]
+        for other, device in others:
+            pltpu.make_async_remote_copy(
+                src_ref=buffers[stage].at[digit],
+                dst_ref=buffers[stage].at[other],
+                send_sem=sends[stage].at[other],
+                recv_sem=recvs[stage].at[other],
+                device_id=(device,),
+                device_id_type=MESH,
+            ).wait_recv()
+        value = buffers[stage][0]
+        for j in range(1, STAGES[stage][1]):
+            value = value + buffers[stage][j]
+        return value
+
     n = audio_ref.shape[0]
     scale = jnp.exp(scalar_ref[0:1, 0:1])
     bias = scalar_ref[1:2, 0:1]
@@ -263,14 +314,12 @@
     cols = lax.broadcasted_iota(jnp.int32, (n, n), 1)
     eye = (rows == cols).astype(jnp.float32)
     backwards = ((code_ref[0] >> BACK) & 1) == 1
-
     audio_wide, audio_recip, audio_unit = unit_rows(audio_ref[...])
     text_wide, text_recip, text_unit = unit_rows(text_ref[...])
     losses_sum = jnp.zeros((n, n), jnp.float32)
     slopes_sum = jnp.zeros((n, n), jnp.float32)
     scaled_sum = jnp.zeros((n, n), jnp.float32)
-    audio_grad = jnp.zeros(audio_wide.shape, jnp.float32)
-    text_grad = jnp.zeros(text_wide.shape, jnp.float32)
+    far_texts, far_weights = [], []
     for slot in range(ROUNDS + 1):
         if slot == 0:
             far_text = text_unit
@@ -290,12 +339,26 @@
         losses_sum = losses_sum + (jnp.maximum(flipped, 0.0) + jnp.log1p(small))
         slopes_sum = slopes_sum + slopes
         scaled_sum = scaled_sum + slopes * scaled
-        weights = (scale * slopes).astype(jnp.bfloat16)
+        far_texts.append(far_text)
+        far_weights.append((scale * slopes).astype(jnp.bfloat16))
+
+    parts = []
+    for total in (losses_sum, slopes_sum, scaled_sum):
+        down = jnp.sum(total, axis=0, keepdims=True)
+        parts.append(down[:, : n // 2] + down[:, n // 2 :])
+    parts = jnp.concatenate(parts + [jnp.zeros((5, n // 2), jnp.float32)], axis=0)
+    pl.semaphore_wait(barrier, sum(peers - 1 for _, peers in STAGES))
+    send(0, parts)
+
+    audio_grad = jnp.zeros(audio_wide.shape, jnp.float32)
+    for far_text, weights in zip(far_texts, far_weights):
         audio_grad = audio_grad + jnp.dot(weights, far_text, preferred_element_type=jnp.float32)
     audio_out[...] = project(audio_wide, audio_recip, audio_grad)
     audio_store = pltpu.make_async_copy(audio_out, ga_ref, sems.at[0])
     audio_store.start()
-
+    send(1, receive(0))
+
+    text_grad = jnp.zeros(text_wide.shape, jnp.float32)
     for slot in range(ROUNDS + 1):
         if slot == 0:
             far_audio = audio_unit
@@ -310,30 +373,32 @@
             slopes = slopes - eye
         weights = (scale * slopes).astype(jnp.bfloat16)
         text_grad = text_grad + jnp.dot(weights, far_audio, preferred_element_type=jnp.float32)
+        if slot == 1:
+            send(2, receive(1))
     text_out[...] = project(text_wide, text_recip, text_grad)
     text_store = pltpu.make_async_copy(text_out, gt_ref, sems.at[1])
     text_store.start()
-
     folded = losses_sum[:, : n // 2] + losses_sum[:, n // 2 :]
     row_ref[...] = jnp.sum(folded.T, axis=0, keepdims=True)
-    parts = []
-    for total in (losses_sum, slopes_sum, scaled_sum):
-        down = jnp.sum(total, axis=0, keepdims=True)
-        parts.append(down[:, : n // 2] + down[:, n // 2 :])
-    tot_ref[...] = jnp.concatenate(parts + [jnp.zeros((5, n // 2), jnp.float32)], axis=0)
+    total = jnp.sum(receive(2), axis=1, keepdims=True) / denominator
+    stats_ref[...] = jnp.broadcast_to(total, stats_ref.shape)
+    for stage in range(len(STAGES)):
+        for copy in copies(stage):
+            copy.wait_send()
     audio_store.wait()
     text_store.wait()
 
 
-def loss_and_grads(scalars, codes, audio, text, held, landed):
+def loss_and_grads(denominator, scalars, codes, audio, text, held, landed):
     n, d = audio.shape
+    part = (8, n // 2)
     return pl.pallas_call(
-        loss_kernel,
+        partial(loss_kernel, denominator),
         out_shape=(
             jax.ShapeDtypeStruct((1, n), jnp.float32),
             jax.ShapeDtypeStruct((n, d), jnp.float32),
             jax.ShapeDtypeStruct((n, d), jnp.float32),
-            jax.ShapeDtypeStruct((8, n // 2), jnp.float32),
+            jax.ShapeDtypeStruct(part, jnp.float32),
         ),
         in_specs=[VMEM, SMEM, VMEM, VMEM, VMEM, VMEM],
         out_specs=(VMEM, ANY, ANY, VMEM),
@@ -341,76 +406,13 @@
             pltpu.VMEM((n, d), jnp.float32),
             pltpu.VMEM((n, d), jnp.float32),
             pltpu.SemaphoreType.DMA((2,)),
-        ],
-        compiler_params=pltpu.CompilerParams(vmem_limit_bytes=40 * MIB),
+        ]
+        + [pltpu.VMEM((peers,) + part, jnp.float32) for _, peers in STAGES]
+        + [pltpu.SemaphoreType.DMA((peers,)) for _, peers in STAGES] * 2,
+        compiler_params=pltpu.CompilerParams(
+            collective_id=0, has_side_effects=True, vmem_limit_bytes=40 * MIB
+        ),
     )(scalars, codes, audio, text, held, landed)
-
-
-def stats_kernel(denominator, part_ref, out_ref, *scratch):
-    me = lax.axis_index("dp")
-    buffers, sends, recvs = scratch[0:3], scratch[3:6], scratch[6:9]
-    groups = []
-    for stride, peers in STAGES:
-        digit = lax.rem(lax.div(me, stride), peers)
-        others = []
-        for k in range(1, peers):
-            other = lax.rem(digit + k, peers)
-            others.append((other, me + (other - digit) * stride))
-        groups.append((digit, others))
-    barrier = pltpu.get_barrier_semaphore()
-    count = 0
-    for _, others in groups:
-        for _, device in others:
-            pl.semaphore_signal(barrier, inc=1, device_id=(device,), device_id_type=MESH)
-            count += 1
-    pl.semaphore_wait(barrier, count)
-    value = part_ref[...]
-    sent = []
-    for stage, (digit, others) in enumerate(groups):
-        buffer, send, recv = buffers[stage], sends[stage], recvs[stage]
-        buffer[digit] = value
-        for other, device in others:
-            pltpu.make_async_remote_copy(
-                src_ref=buffer.at[digit],
-                dst_ref=buffer.at[digit],
-                send_sem=send.at[other],
-                recv_sem=recv.at[digit],
-                device_id=(device,),
-                device_id_type=MESH,
-            ).start()
-        for other, device in others:
-            arrived = pltpu.make_async_remote_copy(
-                src_ref=buffer.at[digit],
-                dst_ref=buffer.at[other],
-                send_sem=send.at[other],
-                recv_sem=recv.at[other],
-                device_id=(device,),
-                device_id_type=MESH,
-            )
-            arrived.wait_recv()
-            sent.append(arrived)
-        value = buffer[0]
-        for j in range(1, STAGES[stage][1]):
-            value = value + buffer[j]
-    for copy in sent:
-        copy.wait_send()
-    total = jnp.sum(value, axis=1, keepdims=True) / denominator
-    out_ref[...] = jnp.broadcast_to(total, out_ref.shape)
-
-
-def all_stats(parts, denominator):
-    scratch = [pltpu.VMEM((peers,) + parts.shape, jnp.float32) for _, peers in STAGES]
-    scratch += [pltpu.SemaphoreType.DMA((peers,)) for _, peers in STAGES] * 2
-    return pl.pallas_call(
-        partial(stats_kernel, denominator),
-        out_shape=jax.ShapeDtypeStruct(parts.shape, jnp.float32),
-        in_specs=[VMEM],
-        out_specs=VMEM,
-        scratch_shapes=scratch,
-        compiler_params=pltpu.CompilerParams(
-            collective_id=0, has_side_effects=True, vmem_limit_bytes=4 * MIB
-        ),
-    )(parts)[:3, 0]
 
 
 def local(audio, text, log_scale, bias, plan):
@@ -427,11 +429,10 @@
     state = (held, own, pair, codes, leaf)
     held, _, pair, codes, leaf = lax.while_loop(lambda s: s[4][0] < 256, transfer, state)
     landed = lax.switch(leaf[0] - 256, leaves, pair)
-    row_loss, grad_audio, grad_text, parts = loss_and_grads(
-        scalars, codes, audio, text, held, landed
+    row_loss, grad_audio, grad_text, stats = loss_and_grads(
+        float((ROUNDS + 1) * n * n * player_count), scalars, codes, audio, text, held, landed
     )
-    stats = all_stats(parts, float((ROUNDS + 1) * n * n * player_count))
-    return (row_loss.reshape(n), grad_audio, grad_text, stats)
+    return (row_loss.reshape(n), grad_audio, grad_text, stats[:3, 0])
 
 
 def solution(mesh):

time: 145 us -> 156 us (1.076)
  Pallas kernels: 136 us -> 142 us
  loops' own time: 5.07 us -> 7.86 us
  local copies, waits for them, and re-layouts: 0.65 us -> 3.15 us
    pallas_call x4 -> x6, Pallas kernels: 102 us -> 110 us  [swap(): pl.pallas_call(partial(swap_kernel, SHIFTS[leaf]), out_shape=jax.ShapeDty...]
    pallas_call x2 -> x1, Pallas kernels: 25.3 us -> 20.8 us  [loss_and_grads(): pl.pallas_call(partial(loss_kernel, denominator), out_shape=(jax.ShapeDty...]
    another operation x1, loops' own time: 4.6 us -> 7.24 us  [local(): lax.while_loop(lambda s: s[4][0] < 256, transfer, state)]
    pallas_call x3 -> x5, Pallas kernels: 6.21 us -> 8.77 us  [store_landed(): pl.pallas_call(store_kernel, out_shape=(jax.ShapeDtypeStruct(held.shape,...]
    unnamed x6 -> x9, local copies, waits for them, and re-layouts: 0.02 us -> 2.52 us
where the time goes in v5:
time: 156 us
  Pallas kernels  142 us (91%)
  loops' own time  7.86 us (5%)
  local copies, waits for them, and re-layouts  3.15 us (2%)
  between operations  2.65 us (2%)
    pallas_call x6, Pallas kernels, swap(): pl.pallas_call(partial(swap_kernel, SHIFTS[leaf]), out_shape=jax.ShapeDty...  110 us
    pallas_call x1, Pallas kernels, loss_and_grads(): pl.pallas_call(partial(loss_kernel, denominator), out_shape=(jax.ShapeDty...  20.8 us
    pallas_call x5, Pallas kernels, store_landed(): pl.pallas_call(store_kernel, out_shape=(jax.ShapeDtypeStruct(held.shape,...  8.77 us
    another operation x1, loops' own time, local(): lax.while_loop(lambda s: s[4][0] < 256, transfer, state)  7.24 us

profile of v5, /device:TPU:1, one launch (start us, length us, event | category | flops | bytes accessed | tf_op | source)
XLA Modules:
  0.0 155.7 jit_solution(17593398824559601708)
XLA Ops:
  1.9 2.8 %shard_map.93 = (bf16[2,256,1024]{2,1,0:T(8,128)(2,1)S(1)}, s32[8]{0:T(128)S(1)}, s32[1]{0:T(128)}, f32[8,128]{1,0:T(8,128)}, bf16[2,256,1024]{2,1,0:T(8,128)(2,1)S(1)}, /*index=5*/bf16[4,256,1024]{2,1,0:T(8,128)(2,1)}) custom-call(s32[1,3]{1,0:T(1,128)} %plan_ref.1, s32[384]{0:T(512)} %constant.21.clone.table_ref, f32[1]{0:T(128)S(6)} %copy.104.scale_ref, ...), custom_call_target="tpu_custom_call" | custom-call | tf_op jit(solution)/shard_map/pallas_call | solution.py:110
  4.7 111.8 %while.226 = (bf16[4,256,1024]{2,1,0:T(8,128)(2,1)}, bf16[2,256,1024]{2,1,0:T(8,128)(2,1)S(1)}, bf16[2,256,1024]{2,1,0:T(8,128)(2,1)S(1)}, s32[8]{0:T(128)S(1)}, s32[1]{0:T(128)}, /*index=5*/s32[1]{0:T(128)}, s32[1]{0:T(128)}) while((bf16[4,256,1024]{2,1,0:T(8,128)(2,1)}, bf16[2,256,1024]{2,1,0:T(8,128)(2,1)S(1)}, ...), condition=%wide.region_36.0_spmd, body=%wide.region_0.0_spmd | while | flops 2 | bytes 89 | solution.py:430
  6.0 20.6 %conditional.3 = (bf16[2,256,1024]{2,1,0:T(8,128)(2,1)S(1)}) conditional(s32[]{:T(128)} %bitcast.5, bf16[2,256,1024]{2,1,0:T(8,128)(2,1)S(1)} %get-tuple-element.245, bf16[2,256,1024]{2,1,0:T(8,128)(2,1)S(1)} %get-tuple-element.245, bf16[2,256,1024]{2,1,0:T(8,128)(2,1)S(1)} %get-tuple-element.245, ...), branch_computations={%region_1.0_spmd, %region_2.0_spmd, %region_3.0_spmd, %region_4.0_... | conditional | bytes 8 | solution.py:426
  6.1 20.5 %branch_11_fun.2 = bf16[2,256,1024]{2,1,0:T(8,128)(2,1)S(1)} custom-call(bf16[2,256,1024]{2,1,0:T(8,128)(2,1)S(1)} %pair_ref.11), custom_call_target="tpu_custom_call" | custom-call | tf_op jit(solution)/shard_map/while/body/cond/branch_11_fun/pallas_call | solution.py:227
  26.6 1.3 body.1
  29.2 21.7 %conditional.3 = (bf16[2,256,1024]{2,1,0:T(8,128)(2,1)S(1)}) conditional(s32[]{:T(128)} %bitcast.5, bf16[2,256,1024]{2,1,0:T(8,128)(2,1)S(1)} %get-tuple-element.245, bf16[2,256,1024]{2,1,0:T(8,128)(2,1)S(1)} %get-tuple-element.245, bf16[2,256,1024]{2,1,0:T(8,128)(2,1)S(1)} %get-tuple-element.245, ...), branch_computations={%region_1.0_spmd, %region_2.0_spmd, %region_3.0_spmd, %region_4.0_... | conditional | bytes 8 | solution.py:426
  29.2 21.6 %branch_29_fun.2 = bf16[2,256,1024]{2,1,0:T(8,128)(2,1)S(1)} custom-call(bf16[2,256,1024]{2,1,0:T(8,128)(2,1)S(1)} %pair_ref.29), custom_call_target="tpu_custom_call" | custom-call | tf_op jit(solution)/shard_map/while/body/cond/branch_29_fun/pallas_call | solution.py:227
  50.9 2.2 %body.1 = (bf16[4,256,1024]{2,1,0:T(8,128)(2,1)}, bf16[2,256,1024]{2,1,0:T(8,128)(2,1)S(1)}, bf16[2,256,1024]{2,1,0:T(8,128)(2,1)S(1)}, s32[8]{0:T(128)S(1)}, s32[1]{0:T(128)}) custom-call(bf16[4,256,1024]{2,1,0:T(8,128)(2,1)} %get-tuple-element.243.held_in, ...), custom_call_target="tpu_custom_call", output_to_operand_aliasing={{0}: (0, {}), {1}: (1, {}), {3}: (3, {})} | custom-call | tf_op jit(solution)/shard_map/while/body/pallas_call | solution.py:186
  54.4 20.8 %conditional.3 = (bf16[2,256,1024]{2,1,0:T(8,128)(2,1)S(1)}) conditional(s32[]{:T(128)} %bitcast.5, bf16[2,256,1024]{2,1,0:T(8,128)(2,1)S(1)} %get-tuple-element.245, bf16[2,256,1024]{2,1,0:T(8,128)(2,1)S(1)} %get-tuple-element.245, bf16[2,256,1024]{2,1,0:T(8,128)(2,1)S(1)} %get-tuple-element.245, ...), branch_computations={%region_1.0_spmd, %region_2.0_spmd, %region_3.0_spmd, %region_4.0_... | conditional | bytes 8 | solution.py:426
  54.4 20.7 %branch_16_fun.2 = bf16[2,256,1024]{2,1,0:T(8,128)(2,1)S(1)} custom-call(bf16[2,256,1024]{2,1,0:T(8,128)(2,1)S(1)} %pair_ref.16), custom_call_target="tpu_custom_call" | custom-call | tf_op jit(solution)/shard_map/while/body/cond/branch_16_fun/pallas_call | solution.py:227
  75.2 1.3 body.1
  77.8 15.0 %conditional.3 = (bf16[2,256,1024]{2,1,0:T(8,128)(2,1)S(1)}) conditional(s32[]{:T(128)} %bitcast.5, bf16[2,256,1024]{2,1,0:T(8,128)(2,1)S(1)} %get-tuple-element.245, bf16[2,256,1024]{2,1,0:T(8,128)(2,1)S(1)} %get-tuple-element.245, bf16[2,256,1024]{2,1,0:T(8,128)(2,1)S(1)} %get-tuple-element.245, ...), branch_computations={%region_1.0_spmd, %region_2.0_spmd, %region_3.0_spmd, %region_4.0_... | conditional | bytes 8 | solution.py:426
  77.8 14.9 %branch_17_fun.2 = bf16[2,256,1024]{2,1,0:T(8,128)(2,1)S(1)} custom-call(bf16[2,256,1024]{2,1,0:T(8,128)(2,1)S(1)} %pair_ref.17), custom_call_target="tpu_custom_call" | custom-call | tf_op jit(solution)/shard_map/while/body/cond/branch_17_fun/pallas_call | solution.py:227
  92.7 2.8 %body.1 = (bf16[4,256,1024]{2,1,0:T(8,128)(2,1)}, bf16[2,256,1024]{2,1,0:T(8,128)(2,1)S(1)}, bf16[2,256,1024]{2,1,0:T(8,128)(2,1)S(1)}, s32[8]{0:T(128)S(1)}, s32[1]{0:T(128)}) custom-call(bf16[4,256,1024]{2,1,0:T(8,128)(2,1)} %get-tuple-element.243.held_in, ...), custom_call_target="tpu_custom_call", output_to_operand_aliasing={{0}: (0, {}), {1}: (1, {}), {3}: (3, {})} | custom-call | tf_op jit(solution)/shard_map/while/body/pallas_call | solution.py:186
  96.8 17.7 %conditional.3 = (bf16[2,256,1024]{2,1,0:T(8,128)(2,1)S(1)}) conditional(s32[]{:T(128)} %bitcast.5, bf16[2,256,1024]{2,1,0:T(8,128)(2,1)S(1)} %get-tuple-element.245, bf16[2,256,1024]{2,1,0:T(8,128)(2,1)S(1)} %get-tuple-element.245, bf16[2,256,1024]{2,1,0:T(8,128)(2,1)S(1)} %get-tuple-element.245, ...), branch_computations={%region_1.0_spmd, %region_2.0_spmd, %region_3.0_spmd, %region_4.0_... | conditional | bytes 8 | solution.py:426
  96.9 17.6 %branch_11_fun.2 = bf16[2,256,1024]{2,1,0:T(8,128)(2,1)S(1)} custom-call(bf16[2,256,1024]{2,1,0:T(8,128)(2,1)S(1)} %pair_ref.11), custom_call_target="tpu_custom_call" | custom-call | tf_op jit(solution)/shard_map/while/body/cond/branch_11_fun/pallas_call | solution.py:227
  114.6 1.3 body.1
  117.1 0.0 copy-start
  117.2 0.0 copy-start.1
  117.2 0.0 copy-start.2
  117.2 14.6 %conditional.2 = (bf16[2,256,1024]{2,1,0:T(8,128)(2,1)S(1)}) conditional(s32[]{:T(128)} %bitcast.2, bf16[2,256,1024]{2,1,0:T(8,128)(2,1)S(1)} %get-tuple-element.195, bf16[2,256,1024]{2,1,0:T(8,128)(2,1)S(1)} %get-tuple-element.195, bf16[2,256,1024]{2,1,0:T(8,128)(2,1)S(1)} %get-tuple-element.195, ...), branch_computations={%region_37.0_spmd, %region_38.0_spmd, %region_39.0_spmd, %region_4... | conditional | bytes 8 | solution.py:431
  117.2 14.3 %branch_11_fun.3 = bf16[2,256,1024]{2,1,0:T(8,128)(2,1)S(1)} custom-call(bf16[2,256,1024]{2,1,0:T(8,128)(2,1)S(1)} %pair_ref.46), custom_call_target="tpu_custom_call" | custom-call | tf_op jit(solution)/shard_map/cond/branch_11_fun/pallas_call | solution.py:227
  131.7 0.0 copy-done
  131.8 0.0 copy-done.1
  131.8 0.0 copy-done.2
  131.8 20.8 %shard_map.94 = (f32[1,256]{1,0:T(1,128)S(1)}, f32[256,1024]{1,0:T(8,128)S(1)}, f32[256,1024]{1,0:T(8,128)S(1)}, f32[8,128]{1,0:T(8,128)S(1)}) custom-call(f32[8,128]{1,0:T(8,128)S(1)} %copy-done.2, s32[8]{0:T(128)S(1)} %get-tuple-element.192.code_ref, bf16[256,1024]{1,0:T(8,128)(2,1)S(1)} %copy-done, bf16[256,1024]{1,0:T(8,128)(2,1)S(1)} %copy-done.1, ...), custom_call_target="tpu_custom_call" | custom-call | tf_op jit(solution)/shard_map/pallas_call | solution.py:395
  152.6 0.6 slice_reduce_fusion
  153.2 0.6 copy.106
  153.7 1.0 copy.107
  154.7 1.0 copy.108
Async XLA Ops:
  117.1 14.6 %copy-start = (bf16[256,1024]{1,0:T(8,128)(2,1)S(1)}, bf16[256,1024]{1,0:T(8,128)(2,1)}, u32[]{:S(2)}) copy-start(bf16[256,1024]{1,0:T(8,128)(2,1)} %audio_ref.3) | copy-start | bytes 1572868
  117.2 14.6 %copy-start.1 = (bf16[256,1024]{1,0:T(8,128)(2,1)S(1)}, bf16[256,1024]{1,0:T(8,128)(2,1)}, u32[]{:S(2)}) copy-start(bf16[256,1024]{1,0:T(8,128)(2,1)} %text_ref.3) | copy-start | bytes 1572868
  117.2 14.6 %copy-start.2 = (f32[8,128]{1,0:T(8,128)S(1)}, f32[8,128]{1,0:T(8,128)}, u32[]{:S(2)}) copy-start(f32[8,128]{1,0:T(8,128)} %get-tuple-element.186.scalar_ref) | copy-start | bytes 12292

commit v6 on v5

--- a/solution.py
+++ b/solution.py
@@ -253,10 +253,15 @@
 
 
 def loss_kernel(
-    denominator, scalar_ref, code_ref, audio_ref, text_ref, held_ref, landed_ref,
-    row_ref, ga_ref, gt_ref, stats_ref, audio_out, text_out, sems, *scratch,
+    denominator, scalar_ref, code_ref, audio_ref, text_ref, held_in, landed_ref,
+    row_ref, ga_ref, gt_ref, stats_ref, held_hbm, held_ref, sems, *scratch,
 ):
     me = lax.axis_index("dp")
+    loads = {
+        i: pltpu.make_async_copy(held_hbm.at[i], held_ref.at[i], sems.at[i]) for i in (1, 3, 0, 2)
+    }
+    for copy in loads.values():
+        copy.start()
     count = len(STAGES)
     buffers, sends, recvs = [scratch[i * count : (i + 1) * count] for i in range(3)]
     groups = []
@@ -320,10 +325,11 @@
     slopes_sum = jnp.zeros((n, n), jnp.float32)
     scaled_sum = jnp.zeros((n, n), jnp.float32)
     far_texts, far_weights = [], []
-    for slot in range(ROUNDS + 1):
+    for slot in (0, 3, 1, 2):
         if slot == 0:
             far_text = text_unit
         elif slot < ROUNDS:
+            loads[2 * slot - 1].wait()
             far_text = unit_rows(held_ref[2 * slot - 1])[2]
         else:
             far_text = unit_rows(jnp.where(backwards, landed_ref[0], landed_ref[1]))[2]
@@ -353,9 +359,7 @@
     audio_grad = jnp.zeros(audio_wide.shape, jnp.float32)
     for far_text, weights in zip(far_texts, far_weights):
         audio_grad = audio_grad + jnp.dot(weights, far_text, preferred_element_type=jnp.float32)
-    audio_out[...] = project(audio_wide, audio_recip, audio_grad)
-    audio_store = pltpu.make_async_copy(audio_out, ga_ref, sems.at[0])
-    audio_store.start()
+    ga_ref[...] = project(audio_wide, audio_recip, audio_grad)
     send(1, receive(0))
 
     text_grad = jnp.zeros(text_wide.shape, jnp.float32)
@@ -363,6 +367,7 @@
         if slot == 0:
             far_audio = audio_unit
         elif slot < ROUNDS:
+            loads[2 * slot - 2].wait()
             far_audio = unit_rows(held_ref[2 * slot - 2])[2]
         else:
             far_audio = unit_rows(jnp.where(backwards, landed_ref[1], landed_ref[0]))[2]
@@ -375,9 +380,7 @@
         text_grad = text_grad + jnp.dot(weights, far_audio, preferred_element_type=jnp.float32)
         if slot == 1:
             send(2, receive(1))
-    text_out[...] = project(text_wide, text_recip, text_grad)
-    text_store = pltpu.make_async_copy(text_out, gt_ref, sems.at[1])
-    text_store.start()
+    gt_ref[...] = project(text_wide, text_recip, text_grad)
     folded = losses_sum[:, : n // 2] + losses_sum[:, n // 2 :]
     row_ref[...] = jnp.sum(folded.T, axis=0, keepdims=True)
     total = jnp.sum(receive(2), axis=1, keepdims=True) / denominator
@@ -385,8 +388,6 @@
     for stage in range(len(STAGES)):
         for copy in copies(stage):
             copy.wait_send()
-    audio_store.wait()
-    text_store.wait()
 
 
 def loss_and_grads(denominator, scalars, codes, audio, text, held, landed):
@@ -399,20 +400,51 @@
             jax.ShapeDtypeStruct((n, d), jnp.float32),
             jax.ShapeDtypeStruct((n, d), jnp.float32),
             jax.ShapeDtypeStruct(part, jnp.float32),
-        ),
-        in_specs=[VMEM, SMEM, VMEM, VMEM, VMEM, VMEM],
-        out_specs=(VMEM, ANY, ANY, VMEM),
+            jax.ShapeDtypeStruct(held.shape, held.dtype),
+        ),
+        in_specs=[VMEM, SMEM, VMEM, VMEM, ANY, VMEM],
+        out_specs=(VMEM, VMEM, VMEM, VMEM, ANY),
+        input_output_aliases={4: 4},
         scratch_shapes=[
-            pltpu.VMEM((n, d), jnp.float32),
-            pltpu.VMEM((n, d), jnp.float32),
-            pltpu.SemaphoreType.DMA((2,)),
+            pltpu.VMEM(held.shape, held.dtype),
+            pltpu.SemaphoreType.DMA((4,)),
         ]
         + [pltpu.VMEM((peers,) + part, jnp.float32) for _, peers in STAGES]
         + [pltpu.SemaphoreType.DMA((peers,)) for _, peers in STAGES] * 2,
         compiler_params=pltpu.CompilerParams(
             collective_id=0, has_side_effects=True, vmem_limit_bytes=40 * MIB
         ),
-    )(scalars, codes, audio, text, held, landed)
+    )(scalars, codes, audio, text, held, landed)[:4]
+
+
+def result_kernel(row_in, ga_in, gt_in, stats_in, row_ref, ga_ref, gt_ref, stats_ref, sems):
+    moves = [
+        pltpu.make_async_copy(src, dst, sems.at[i])
+        for i, (src, dst) in enumerate(((ga_in, ga_ref), (gt_in, gt_ref)))
+    ]
+    for copy in moves:
+        copy.start()
+    row_ref[...] = row_in[...]
+    for i in range(3):
+        stats_ref[i] = stats_in[i, 0]
+    for copy in moves:
+        copy.wait()
+
+
+def results(row_loss, grad_audio, grad_text, stats):
+    return pl.pallas_call(
+        result_kernel,
+        out_shape=(
+            jax.ShapeDtypeStruct(row_loss.shape, jnp.float32),
+            jax.ShapeDtypeStruct(grad_audio.shape, jnp.float32),
+            jax.ShapeDtypeStruct(grad_text.shape, jnp.float32),
+            jax.ShapeDtypeStruct((3,), jnp.float32),
+        ),
+        in_specs=[VMEM] * 4,
+        out_specs=(VMEM, ANY, ANY, SMEM),
+        scratch_shapes=[pltpu.SemaphoreType.DMA((2,))],
+        compiler_params=pltpu.CompilerParams(vmem_limit_bytes=8 * MIB),
+    )(row_loss, grad_audio, grad_text, stats)
 
 
 def local(audio, text, log_scale, bias, plan):
@@ -429,10 +461,12 @@
     state = (held, own, pair, codes, leaf)
     held, _, pair, codes, leaf = lax.while_loop(lambda s: s[4][0] < 256, transfer, state)
     landed = lax.switch(leaf[0] - 256, leaves, pair)
-    row_loss, grad_audio, grad_text, stats = loss_and_grads(
-        float((ROUNDS + 1) * n * n * player_count), scalars, codes, audio, text, held, landed
+    row_loss, grad_audio, grad_text, stats = results(
+        *loss_and_grads(
+            float((ROUNDS + 1) * n * n * player_count), scalars, codes, audio, text, held, landed
+        )
     )
-    return (row_loss.reshape(n), grad_audio, grad_text, stats[:3, 0])
+    return (row_loss.reshape(n), grad_audio, grad_text, stats)
 
 
 def solution(mesh):

time: 156 us -> 141 us (0.904)
  Pallas kernels: 142 us -> 133 us
  local copies, waits for them, and re-layouts: 3.15 us -> 0.02 us
  loops' own time: 7.86 us -> 5.07 us
    pallas_call x6 -> x4, Pallas kernels: 110 us -> 92.2 us  [swap(): pl.pallas_call(partial(swap_kernel, SHIFTS[leaf]), out_shape=jax.ShapeDty...]
    pallas_call x1, Pallas kernels: 20.8 us -> 30.4 us  [loss_and_grads(): pl.pallas_call(partial(loss_kernel, denominator), out_shape=(jax.ShapeDty...]
    pallas_call x5 -> x3, Pallas kernels: 8.77 us -> 5.61 us  [store_landed(): pl.pallas_call(store_kernel, out_shape=(jax.ShapeDtypeStruct(held.shape,...]
    another operation x1, loops' own time: 7.24 us -> 4.6 us  [local(): lax.while_loop(lambda s: s[4][0] < 256, transfer, state)]
    unnamed x9 -> x6, local copies, waits for them, and re-layouts: 2.52 us -> 0.02 us
    pallas_call x0 -> x1, Pallas kernels: none -> 1.91 us  [results(): pl.pallas_call(result_kernel, out_shape=(jax.ShapeDtypeStruct(row_loss.sh...]
where the time goes in v6:
time: 141 us
  Pallas kernels  133 us (94%)
  loops' own time  5.07 us (4%)
  between operations  2.81 us (2%)
    pallas_call x4, Pallas kernels, swap(): pl.pallas_call(partial(swap_kernel, SHIFTS[leaf]), out_shape=jax.ShapeDty...  92.2 us
    pallas_call x1, Pallas kernels, loss_and_grads(): pl.pallas_call(partial(loss_kernel, denominator), out_shape=(jax.ShapeDty...  30.4 us
    pallas_call x3, Pallas kernels, store_landed(): pl.pallas_call(store_kernel, out_shape=(jax.ShapeDtypeStruct(held.shape,...  5.61 us
    another operation x1, loops' own time, local(): lax.while_loop(lambda s: s[4][0] < 256, transfer, state)  4.6 us

profile of v6, /device:TPU:1, one launch (start us, length us, event | category | flops | bytes accessed | tf_op | source)
XLA Modules:
  0.0 140.7 jit_solution(8947094207323059502)
XLA Ops:
  1.9 2.7 %shard_map.93 = (bf16[2,256,1024]{2,1,0:T(8,128)(2,1)S(1)}, s32[8]{0:T(128)S(1)}, s32[1]{0:T(128)}, f32[8,128]{1,0:T(8,128)}, bf16[2,256,1024]{2,1,0:T(8,128)(2,1)S(1)}, /*index=5*/bf16[4,256,1024]{2,1,0:T(8,128)(2,1)}) custom-call(s32[1,3]{1,0:T(1,128)} %plan_ref.1, s32[384]{0:T(512)} %constant.21.clone.table_ref, f32[1]{0:T(128)S(6)} %copy.103.scale_ref, ...), custom_call_target="tpu_custom_call" | custom-call | tf_op jit(solution)/shard_map/pallas_call | solution.py:110
  4.6 85.4 %while.226 = (bf16[4,256,1024]{2,1,0:T(8,128)(2,1)}, bf16[2,256,1024]{2,1,0:T(8,128)(2,1)S(1)}, bf16[2,256,1024]{2,1,0:T(8,128)(2,1)S(1)}, s32[8]{0:T(128)S(1)}, s32[1]{0:T(128)}, /*index=5*/s32[1]{0:T(128)}, s32[1]{0:T(128)}) while((bf16[4,256,1024]{2,1,0:T(8,128)(2,1)}, bf16[2,256,1024]{2,1,0:T(8,128)(2,1)S(1)}, ...), condition=%wide.region_36.0_spmd, body=%wide.region_0.0_spmd | while | flops 2 | bytes 89 | solution.py:462
  5.9 31.9 %conditional.3 = (bf16[2,256,1024]{2,1,0:T(8,128)(2,1)S(1)}) conditional(s32[]{:T(128)} %bitcast.5, bf16[2,256,1024]{2,1,0:T(8,128)(2,1)S(1)} %get-tuple-element.253, bf16[2,256,1024]{2,1,0:T(8,128)(2,1)S(1)} %get-tuple-element.253, bf16[2,256,1024]{2,1,0:T(8,128)(2,1)S(1)} %get-tuple-element.253, ...), branch_computations={%region_1.0_spmd, %region_2.0_spmd, %region_3.0_spmd, %region_4.0_... | conditional | bytes 8 | solution.py:458
  6.0 31.8 %branch_9_fun.2 = bf16[2,256,1024]{2,1,0:T(8,128)(2,1)S(1)} custom-call(bf16[2,256,1024]{2,1,0:T(8,128)(2,1)S(1)} %pair_ref.9), custom_call_target="tpu_custom_call" | custom-call | tf_op jit(solution)/shard_map/while/body/cond/branch_9_fun/pallas_call | solution.py:227
  37.8 2.1 %body.1 = (bf16[4,256,1024]{2,1,0:T(8,128)(2,1)}, bf16[2,256,1024]{2,1,0:T(8,128)(2,1)S(1)}, bf16[2,256,1024]{2,1,0:T(8,128)(2,1)S(1)}, s32[8]{0:T(128)S(1)}, s32[1]{0:T(128)}) custom-call(bf16[4,256,1024]{2,1,0:T(8,128)(2,1)} %get-tuple-element.251.held_in, ...), custom_call_target="tpu_custom_call", output_to_operand_aliasing={{0}: (0, {}), {1}: (1, {}), {3}: (3, {})} | custom-call | tf_op jit(solution)/shard_map/while/body/pallas_call | solution.py:186
  41.3 27.8 %conditional.3 = (bf16[2,256,1024]{2,1,0:T(8,128)(2,1)S(1)}) conditional(s32[]{:T(128)} %bitcast.5, bf16[2,256,1024]{2,1,0:T(8,128)(2,1)S(1)} %get-tuple-element.253, bf16[2,256,1024]{2,1,0:T(8,128)(2,1)S(1)} %get-tuple-element.253, bf16[2,256,1024]{2,1,0:T(8,128)(2,1)S(1)} %get-tuple-element.253, ...), branch_computations={%region_1.0_spmd, %region_2.0_spmd, %region_3.0_spmd, %region_4.0_... | conditional | bytes 8 | solution.py:458
  41.3 27.7 %branch_30_fun.2 = bf16[2,256,1024]{2,1,0:T(8,128)(2,1)S(1)} custom-call(bf16[2,256,1024]{2,1,0:T(8,128)(2,1)S(1)} %pair_ref.30), custom_call_target="tpu_custom_call" | custom-call | tf_op jit(solution)/shard_map/while/body/cond/branch_30_fun/pallas_call | solution.py:227
  69.1 2.2 %body.1 = (bf16[4,256,1024]{2,1,0:T(8,128)(2,1)}, bf16[2,256,1024]{2,1,0:T(8,128)(2,1)S(1)}, bf16[2,256,1024]{2,1,0:T(8,128)(2,1)S(1)}, s32[8]{0:T(128)S(1)}, s32[1]{0:T(128)}) custom-call(bf16[4,256,1024]{2,1,0:T(8,128)(2,1)} %get-tuple-element.251.held_in, ...), custom_call_target="tpu_custom_call", output_to_operand_aliasing={{0}: (0, {}), {1}: (1, {}), {3}: (3, {})} | custom-call | tf_op jit(solution)/shard_map/while/body/pallas_call | solution.py:186
  72.6 15.5 %conditional.3 = (bf16[2,256,1024]{2,1,0:T(8,128)(2,1)S(1)}) conditional(s32[]{:T(128)} %bitcast.5, bf16[2,256,1024]{2,1,0:T(8,128)(2,1)S(1)} %get-tuple-element.253, bf16[2,256,1024]{2,1,0:T(8,128)(2,1)S(1)} %get-tuple-element.253, bf16[2,256,1024]{2,1,0:T(8,128)(2,1)S(1)} %get-tuple-element.253, ...), branch_computations={%region_1.0_spmd, %region_2.0_spmd, %region_3.0_spmd, %region_4.0_... | conditional | bytes 8 | solution.py:458
  72.7 15.4 %branch_18_fun.2 = bf16[2,256,1024]{2,1,0:T(8,128)(2,1)S(1)} custom-call(bf16[2,256,1024]{2,1,0:T(8,128)(2,1)S(1)} %pair_ref.18), custom_call_target="tpu_custom_call" | custom-call | tf_op jit(solution)/shard_map/while/body/cond/branch_18_fun/pallas_call | solution.py:227
  88.1 1.3 body.1
  90.7 0.0 copy-start
  90.7 0.0 copy-start.1
  90.7 0.0 copy-start.2
  90.7 17.4 %conditional.2 = (bf16[2,256,1024]{2,1,0:T(8,128)(2,1)S(1)}) conditional(s32[]{:T(128)} %bitcast.2, bf16[2,256,1024]{2,1,0:T(8,128)(2,1)S(1)} %get-tuple-element.199, bf16[2,256,1024]{2,1,0:T(8,128)(2,1)S(1)} %get-tuple-element.199, bf16[2,256,1024]{2,1,0:T(8,128)(2,1)S(1)} %get-tuple-element.199, ...), branch_computations={%region_37.0_spmd, %region_38.0_spmd, %region_39.0_spmd, %region_4... | conditional | bytes 8 | solution.py:463
  90.8 17.2 %branch_32_fun.3 = bf16[2,256,1024]{2,1,0:T(8,128)(2,1)S(1)} custom-call(bf16[2,256,1024]{2,1,0:T(8,128)(2,1)S(1)} %pair_ref.67), custom_call_target="tpu_custom_call" | custom-call | tf_op jit(solution)/shard_map/cond/branch_32_fun/pallas_call | solution.py:227
  108.2 0.0 copy-done
  108.2 0.0 copy-done.1
  108.2 0.0 copy-done.2
  108.2 30.4 %shard_map.94 = (f32[1,256]{1,0:T(1,128)S(1)}, f32[256,1024]{1,0:T(8,128)S(1)}, f32[256,1024]{1,0:T(8,128)S(1)}, f32[8,128]{1,0:T(8,128)S(1)}, bf16[4,256,1024]{2,1,0:T(8,128)(2,1)}) custom-call(f32[8,128]{1,0:T(8,128)S(1)} %copy-done.2, s32[8]{0:T(128)S(1)} %get-tuple-element.196.code_ref, ...), custom_call_target="tpu_custom_call", output_to_operand_aliasing={{4}: (4, {})} | custom-call | tf_op jit(solution)/shard_map/pallas_call | solution.py:396
  138.6 1.9 %shard_map.95 = (f32[1,256]{1,0:T(1,128)}, f32[256,1024]{1,0:T(8,128)}, f32[256,1024]{1,0:T(8,128)}, f32[3]{0:T(128)}) custom-call(f32[1,256]{1,0:T(1,128)S(1)} %get-tuple-element.200.row_in, f32[256,1024]{1,0:T(8,128)S(1)} %get-tuple-element.201.ga_in, f32[256,1024]{1,0:T(8,128)S(1)} %get-tuple-element.202.gt_in, f32[8,128]{1,0:T(8,128)S(1)} %get-tuple-element.203.stats_in), custom_call_target="tpu_custom_call" | custom-call | tf_op jit(solution)/shard_map/pallas_call | solution.py:435
Async XLA Ops:
  90.7 17.5 %copy-start = (bf16[256,1024]{1,0:T(8,128)(2,1)S(1)}, bf16[256,1024]{1,0:T(8,128)(2,1)}, u32[]{:S(2)}) copy-start(bf16[256,1024]{1,0:T(8,128)(2,1)} %audio_ref.3) | copy-start | bytes 1572868
  90.7 17.5 %copy-start.1 = (bf16[256,1024]{1,0:T(8,128)(2,1)S(1)}, bf16[256,1024]{1,0:T(8,128)(2,1)}, u32[]{:S(2)}) copy-start(bf16[256,1024]{1,0:T(8,128)(2,1)} %text_ref.3) | copy-start | bytes 1572868
  90.7 17.5 %copy-start.2 = (f32[8,128]{1,0:T(8,128)S(1)}, f32[8,128]{1,0:T(8,128)}, u32[]{:S(2)}) copy-start(f32[8,128]{1,0:T(8,128)} %get-tuple-element.190.scalar_ref) | copy-start | bytes 12292
